TPU v7x, 256 devices: a whole 4x4x8 slice. The times are simulated.
256 devices in a mesh: loop: 128 (over z, y, x_lo, core), half: 2 (over x_hi).
Axes of the slice: x: 4 (x_hi: 2, x_lo: 2; x = x_hi * 2 + x_lo), y: 4, z: 8, core: 2. Of those that a mesh axis runs over, the one named last changes fastest.
Arguments:
- tokens: bfloat16 [131072, 4096], P(('loop', 'half')), may hold values from -36 to 36
- gain: float32 [4096], replicated, may hold values from 0.1 to 1.9
- w_key: bfloat16 [4096, 512], P('loop', 'half'), may hold values from -0.09375 to 0.09375
- w_value: bfloat16 [4096, 512], P('loop', 'half'), may hold values from -0.09375 to 0.09375
- d_keys: bfloat16 [131072, 512], P(('loop', 'half')), may hold values from -13.5 to 13.5
- d_values: bfloat16 [131072, 512], P(('loop', 'half')), may hold values from -13.5 to 13.5
Outputs:
- keys: bfloat16 [131072, 512], P(('loop', 'half'))
- values: bfloat16 [131072, 512], P(('loop', 'half'))
- d_tokens: bfloat16 [131072, 4096], P(('loop', 'half'))
- grad_key: float32 [4096, 512], P('loop', 'half')
- grad_value: float32 [4096, 512], P('loop', 'half')
- grad_gain: float32 [4096], replicated
All inputs are finite; a program needn't handle non-finite values.
Results may differ from a plain program's by a relative error of at most 0.0049.
Values may be sent and summed in bfloat16 or wider, within the bound.
No kernel may reach another device: no remote copies, remote signals or barrier semaphores. Data moves between devices by JAX's collectives and lax.ppermute only.
A program may use at most 128 MiB of HBM per device.

v0:
```python
import math

import jax
import jax.numpy as jnp
from jax import lax
from jax.sharding import PartitionSpec as P


def shards(tokens, gain, w_key, w_value, d_keys, d_values):
    rows = tokens.shape[0]
    width = w_key.shape[1]
    row_block = w_key.shape[0]
    pair = lax.axis_size("half")
    cycle = lax.axis_size("loop")
    total = rows * cycle * pair
    scale = 1.0 / math.sqrt(total)
    x_rows = tokens.astype(jnp.float32)
    inverse = lax.rsqrt(jnp.mean(x_rows * x_rows, axis=1, keepdims=True) + 1e-05)
    normal_rows = x_rows * inverse
    hidden = (normal_rows * gain).astype(jnp.bfloat16)
    joined = (
        lax.all_gather(w_key, "half", axis=1, tiled=True),
        lax.all_gather(w_value, "half", axis=1, tiled=True),
    )
    full_key, full_value = (
        lax.all_gather(joined[0], "loop", axis=0, tiled=True),
        lax.all_gather(joined[1], "loop", axis=0, tiled=True),
    )
    keys = jnp.dot(hidden, full_key, preferred_element_type=jnp.float32).astype(jnp.bfloat16)
    values = jnp.dot(hidden, full_value, preferred_element_type=jnp.float32).astype(jnp.bfloat16)
    d_hidden = jnp.einsum("tc,dc->td", d_keys, full_key, preferred_element_type=jnp.float32)
    d_hidden = d_hidden + jnp.einsum(
        "tc,dc->td", d_values, full_value, preferred_element_type=jnp.float32
    )
    grad_gain = lax.psum(jnp.sum(d_hidden * normal_rows, axis=0), ("loop", "half")) * scale
    scaled = d_hidden * gain
    along = jnp.mean(scaled * normal_rows, axis=1, keepdims=True)
    d_tokens = (inverse * (scaled - normal_rows * along)).astype(jnp.bfloat16)
    key_term = jnp.einsum("tr,tc->rc", hidden, d_keys, preferred_element_type=jnp.float32)
    value_term = jnp.einsum("tr,tc->rc", hidden, d_values, preferred_element_type=jnp.float32)
    partial_sum = lax.psum_scatter(
        jnp.concatenate([key_term, value_term], axis=1), "loop", scatter_dimension=0, tiled=True
    )
    mine = lax.psum_scatter(
        partial_sum.reshape(row_block, 2, pair, width), "half", scatter_dimension=2, tiled=True
    )
    grad_key = mine[:, 0, 0, :] * scale
    grad_value = mine[:, 1, 0, :] * scale
    return (keys, values, d_tokens, grad_key, grad_value, grad_gain)


def solution(mesh):
    return jax.shard_map(
        shards,
        mesh=mesh,
        in_specs=(
            P(("loop", "half"), None),
            P(),
            P("loop", "half"),
            P("loop", "half"),
            P(("loop", "half"), None),
            P(("loop", "half"), None),
        ),
        out_specs=(
            P(("loop", "half"), None),
            P(("loop", "half"), None),
            P(("loop", "half"), None),
            P("loop", "half"),
            P("loop", "half"),
            P(),
        ),
        check_vma=False,
    )
```

profile of v0, /device:TPU:1, one launch (start us, length us, event | category | flops | bytes accessed | tf_op | source)
XLA Modules:
  0.0 1083.4 jit_solution(14665511583187494820)
XLA Ops:
  7.2 0.0 copy-start
  7.2 0.0 all-gather.3.cloned.1.call-start
  7.2 7.1 all_gather.12
  14.3 0.0 all-gather.3.cloned.1.call-update
  14.4 0.0 all-gather.5.cloned.1.call-start
  14.4 5.1 all_gather.14
  19.5 0.0 all-gather.5.cloned.1.call-update
  19.5 0.0 reduce-scatter.7.cloned.1.call-start
  19.6 3.1 fusion.10
  22.7 0.0 copy-start.1
  22.7 0.0 copy-start.4
  22.7 0.0 copy-start.5
  22.7 0.0 copy-done
  22.7 5.1 fusion.13
  27.8 0.0 copy-done.1
  27.8 0.0 copy-done.4
  27.8 0.0 copy-done.5
  27.8 2.8 fusion.15
  30.6 6.3 pad_maximum_fusion
  36.9 17.5 %copy.14 = f32[4096,1024]{1,0:T(8,128)} copy(f32[4096,1024]{0,1:T(8,128)} %pad_maximum_fusion) | data formatting | bytes 33554432
  54.4 0.0 copy-start.6
  54.4 0.0 reduce-scatter.7.cloned.1.call-update
  54.4 0.0 all-reduce.3.cloned.1.call-start
  54.4 0.6 copy-done.6
  55.0 0.6 dynamic-slice
  55.6 177.3 %all-gather.3.cloned.1.call-done = bf16[4096,512]{1,0:T(8,128)(2,1)} async-done(((bf16[32,512]{1,0:T(8,128)(2,1)}), bf16[4096,512]{1,0:T(8,128)(2,1)}) %all-gather.3.cloned.1.call-update) | async-done | bytes 4194320 | tf_op jit(solution)/shard_map/all_gather | solution.py:26
  232.9 7.8 fusion.19
  240.7 208.4 %all-gather.5.cloned.1.call-done = bf16[4096,512]{1,0:T(8,128)(2,1)} async-done(((bf16[32,512]{1,0:T(8,128)(2,1)}), bf16[4096,512]{1,0:T(8,128)(2,1)}) %all-gather.5.cloned.1.call-update) | async-done | bytes 4194320 | tf_op jit(solution)/shard_map/all_gather | solution.py:27
  449.1 9.3 fusion.9
  458.3 76.6 %psum.7 = f32[4096]{0:T(1024)S(1)} all-reduce(f32[4096]{0:T(1024)S(1)} %get-tuple-element.6), channel_id=1, replica_groups=mesh['loop'=128,'half'=2] {'loop','half'}, use_global_device_ids=true, to_apply=%region_5.0 | all-reduce | flops 4096 | bytes 32768 | tf_op jit(solution)/shard_map/psum | solution.py:35
  535.0 0.0 copy-start.2
  535.0 0.0 copy-start.3
  535.0 0.0 slice-start
  535.0 6.9 convolution_convert_fusion.1
  541.8 0.0 copy-done.2
  541.8 0.0 copy-done.3
  541.8 0.0 slice-start.1
  541.8 3.2 convolution_convert_fusion
  545.0 0.0 slice-done
  545.0 0.0 slice-done.1
  545.1 4.1 fusion.8
  549.1 490.0 %reduce-scatter.7.cloned.1.call-done = f32[32,1024]{1,0:T(8,128)} async-done(((f32[4096,1024]{1,0:T(8,128)}), f32[32,1024]{1,0:T(8,128)}) %reduce-scatter.7.cloned.1.call-update) | async-done | bytes 131088
  1039.2 1.1 copy.15
  1040.3 0.8 copy.13
  1041.1 0.0 all-reduce.3.cloned.1.call-update
  1041.1 0.6 broadcast_multiply_fusion
  1041.7 33.1 %all-reduce.3.cloned.1.call-done = f32[32,2,2,256]{3,0,2,1:T(8,128)} async-done(((f32[32,2,2,256]{3,0,2,1:T(8,128)}), f32[32,2,2,256]{3,0,2,1:T(8,128)}) %all-reduce.3.cloned.1.call-update) | async-done | bytes 131088
  1074.8 2.0 fusion.11
  (3 shorter events, 0.0 us)
Async XLA Ops:
  7.2 15.5 %copy-start = (bf16[512,512]{1,0:T(8,128)(2,1)S(1)}, bf16[512,512]{1,0:T(8,128)(2,1)}, u32[]{:S(2)}) copy-start(bf16[512,512]{1,0:T(8,128)(2,1)} %param.11) | copy-start | bytes 1572868
  7.2 225.7 %all-gather.3.cloned.1.call-start = ((), (), s32[]{:S(2)}) async-start(), calls=%async_computation.1 | async-start | bytes 4227072 | tf_op jit(solution)/shard_map/all_gather | solution.py:26
  14.4 434.7 %all-gather.5.cloned.1.call-start = ((), (), s32[]{:S(2)}) async-start(), calls=%async_computation.2 | async-start | bytes 4227072 | tf_op jit(solution)/shard_map/all_gather | solution.py:27
  19.5 1019.6 %reduce-scatter.7.cloned.1.call-start = ((), (), s32[]{:S(2)}) async-start(), calls=%async_computation.3 | async-start | bytes 16908288
  22.7 5.1 copy-start.1
  22.7 5.1 copy-start.4
  22.7 5.1 copy-start.5
  54.4 0.7 copy-start.6
  54.4 1020.5 %all-reduce.3.cloned.1.call-start = ((), (), s32[]{:S(2)}) async-start(), calls=%async_computation.4 | async-start | bytes 262144
  535.0 6.9 copy-start.2
  535.0 6.9 copy-start.3
  535.0 10.1 slice-start
  541.8 3.2 slice-start.1
Sparse Core Ops, SparseCore 0:
  14.5 218.3 all-gather.2
  234.7 214.2 all-gather.4
  451.6 587.5 reduce-scatter.6
  1041.6 33.2 all-reduce.2
where the time goes:
time: 1080 us
  waiting for transfers between devices  909 us (84%)
  blocking collectives  88.8 us (8%)
  matrix products  34.9 us (3%)
  local copies, waits for them, and re-layouts  20.6 us (2%)
  other arithmetic  16 us (1%)
  between operations  13.9 us (1%)
    unnamed x6, waiting for transfers between devices  523 us
    all_gather x1, waiting for transfers between devices, shards(): lax.all_gather(joined[1], 'loop', axis=0, tiled=True)  208 us
    all_gather x1, waiting for transfers between devices, shards(): lax.all_gather(joined[0], 'loop', axis=0, tiled=True)  177 us
    psum x1, blocking collectives, shards(): lax.psum(jnp.sum(d_hidden * normal_rows, axis=0), ('loop', 'half')) * scale  76.6 us
  transfers between devices with their start and end apart: 4, of which 4 were waited for; matrix products, arithmetic and copies ran while one was open for 6% of the time, Pallas kernels for 0%

commit v1 on v0

v1 whole, which is shorter than its diff:
```python
import math

import jax
import jax.numpy as jnp
from jax import lax
from jax.experimental import pallas as pl
from jax.experimental.pallas import tpu as pltpu
from jax.sharding import Mesh
from jax.sharding import PartitionSpec as P

Z, Y, XL, CORE, XH = 8, 4, 2, 2, 2
AXES = ("z", "y", "xl", "core", "xh")
PLANE = ("y", "xl", "xh")
ROWS = 512
D = 4096
C = 512
W = D // Z
HALF = C // XH
BLOCK = 32
EPS = 1e-05
BF = jnp.bfloat16
F32 = jnp.float32
VMEM = 44 * 1024 * 1024


def inverse_of(x):
    x = x.astype(F32)
    return lax.rsqrt(jnp.sum(x * x, axis=1, keepdims=True) * (1.0 / D) + EPS)


def grads_kernel(own_ref, other_ref, gain_ref, d_own_ref, d_other_ref, out_ref, inv_ref):
    step = pl.program_id(0)

    @pl.when(step == 0)
    def _():
        inv_ref[0] = jnp.broadcast_to(inverse_of(own_ref[...]), (ROWS, 128))
        inv_ref[1] = jnp.broadcast_to(inverse_of(other_ref[...]), (ROWS, 128))

    columns = pl.ds(pl.multiple_of(step * W, W), W)
    gain = gain_ref[:, columns]

    def term(x_ref, which, d_ref):
        normal = x_ref[:, columns].astype(F32) * inv_ref[which, :, :1]
        hidden = (normal * gain).astype(BF)
        return lax.dot_general(
            hidden, d_ref[...], (((0,), (0,)), ((), ())), preferred_element_type=F32
        )

    total = term(own_ref, 0, d_own_ref) + term(other_ref, 1, d_other_ref)
    total = total.astype(BF)
    for place in range(Y * XL):
        for core in range(CORE):
            for half in range(XH):
                first = (place * CORE + core) * BLOCK
                out_ref[place * XH + half, 0, core] = total[
                    first : first + BLOCK, half * HALF : (half + 1) * HALF
                ]


def gradient_terms(own, other, gain, d_own, d_other):
    whole = lambda shape: pl.BlockSpec(shape, lambda i: (0,) * len(shape))
    return pl.pallas_call(
        grads_kernel,
        grid=(Z,),
        in_specs=[
            whole((ROWS, D)),
            whole((ROWS, D)),
            whole((1, D)),
            whole((ROWS, C)),
            whole((ROWS, C)),
        ],
        out_specs=pl.BlockSpec((Y * XL * XH, 1, CORE, BLOCK, HALF), lambda i: (0, i, 0, 0, 0)),
        out_shape=jax.ShapeDtypeStruct((Y * XL * XH, Z, CORE, BLOCK, HALF), BF),
        scratch_shapes=[pltpu.VMEM((2, ROWS, 128), F32)],
        compiler_params=pltpu.CompilerParams(vmem_limit_bytes=VMEM),
        cost_estimate=pl.CostEstimate(
            flops=2 * 2 * ROWS * D * C, bytes_accessed=13 << 20, transcendentals=2 * ROWS
        ),
        name="gradient_terms",
    )(own, other, gain, d_own, d_other)


def rows_kernel(x_ref, gain_ref, d0_ref, d1_ref, w0_ref, w1_ref, out0_ref, out1_ref, dx_ref,
                inv_ref, total_ref, along_ref):
    step = pl.program_id(0)

    @pl.when(step == 0)
    def _():
        inv_ref[...] = jnp.broadcast_to(inverse_of(x_ref[...]), (ROWS, 128))
        total_ref[...] = jnp.zeros_like(total_ref)

    columns = pl.ds(pl.multiple_of(lax.rem(step, Z) * W, W), W)
    gain = gain_ref[:, columns]
    normal = x_ref[:, columns].astype(F32) * inv_ref[:, :1]
    weights = jnp.concatenate(
        [ref[:, half].reshape(W, HALF) for ref in (w0_ref, w1_ref) for half in range(XH)], axis=1
    )

    @pl.when(step < Z)
    def _():
        hidden = (normal * gain).astype(BF)
        total_ref[...] += jnp.dot(hidden, weights, preferred_element_type=F32)

    @pl.when(step == Z)
    def _():
        first, second = total_ref[:, :C], total_ref[:, C:]
        along = jnp.sum(
            first * d0_ref[...].astype(F32) + second * d1_ref[...].astype(F32),
            axis=1,
            keepdims=True,
        )
        along_ref[...] = jnp.broadcast_to(along * (1.0 / D), (ROWS, 128))
        out0_ref[...] = first.astype(BF)
        out1_ref[...] = second.astype(BF)

    @pl.when(step >= Z)
    def _():
        cotangents = jnp.concatenate([d0_ref[...], d1_ref[...]], axis=1)
        d_hidden = lax.dot_general(
            cotangents, weights, (((1,), (1,)), ((), ())), preferred_element_type=F32
        )
        inverse = inv_ref[:, :1]
        dx_ref[...] = (inverse * (d_hidden * gain - normal * along_ref[:, :1])).astype(BF)


def rows_pass(x, gain, d0, d1, w0, w1):
    whole = lambda shape: pl.BlockSpec(shape, lambda i: (0,) * len(shape))
    weights = pl.BlockSpec((D // BLOCK // Z, XH, BLOCK, HALF), lambda i: (lax.rem(i, Z), 0, 0, 0))
    return pl.pallas_call(
        rows_kernel,
        grid=(2 * Z,),
        in_specs=[
            whole((ROWS, D)),
            whole((1, D)),
            whole((ROWS, C)),
            whole((ROWS, C)),
            weights,
            weights,
        ],
        out_specs=[
            whole((ROWS, C)),
            whole((ROWS, C)),
            pl.BlockSpec((ROWS, W), lambda i: (0, jnp.maximum(i - Z, 0))),
        ],
        out_shape=[
            jax.ShapeDtypeStruct((ROWS, C), BF),
            jax.ShapeDtypeStruct((ROWS, C), BF),
            jax.ShapeDtypeStruct((ROWS, D), BF),
        ],
        scratch_shapes=[
            pltpu.VMEM((ROWS, 128), F32),
            pltpu.VMEM((ROWS, 2 * C), F32),
            pltpu.VMEM((ROWS, 128), F32),
        ],
        compiler_params=pltpu.CompilerParams(vmem_limit_bytes=VMEM),
        cost_estimate=pl.CostEstimate(
            flops=2 * 2 * ROWS * D * 2 * C, bytes_accessed=26 << 20, transcendentals=ROWS
        ),
        name="rows_pass",
    )(x, gain, d0, d1, w0, w1)


def shards(tokens, gain, w_key, w_value, d_keys, d_values):
    scale = 1.0 / math.sqrt(ROWS * Z * Y * XL * CORE * XH)
    core = lax.axis_index("core")
    swap = lambda a: lax.ppermute(a, "core", [(0, 1), (1, 0)])
    row_gain = gain.reshape(1, D)

    pair = jnp.stack([w_key, w_value])
    sent = jnp.broadcast_to(pair[None, :, None], (Y * XL, CORE, XH, BLOCK, HALF))
    plane = lax.all_to_all(
        sent.reshape(Y * XL * CORE * XH, BLOCK, HALF), ("y", "xl", "core", "xh"), 0, 0, tiled=True
    )
    mine = lax.all_gather(plane, "z", axis=0, tiled=True)
    mine = mine.reshape(D // BLOCK, XH, BLOCK, HALF)
    theirs = swap(mine)

    first = core == 0
    d_mine = jnp.where(first, d_keys, d_values)
    d_theirs = jnp.where(first, d_values, d_keys)
    terms = gradient_terms(tokens, swap(tokens), row_gain, d_mine, swap(d_theirs))
    summed = lax.all_to_all(terms, PLANE, 0, 0, tiled=True)
    summed = jnp.sum(summed.astype(F32), axis=0)

    place = lax.axis_index("y") * XL + lax.axis_index("xl")
    blocks = mine.reshape(Z, Y * XL, CORE, XH, BLOCK, HALF)
    blocks = lax.dynamic_slice(
        blocks,
        (0, place, 0, lax.axis_index("xh"), 0, 0),
        (Z, 1, CORE, 1, BLOCK, HALF),
    ).reshape(Z, CORE, BLOCK, HALF)
    gains = jnp.sum(summed * blocks.astype(F32), axis=3).reshape(2, HALF)
    high = gains.astype(BF)
    low = (gains - high.astype(F32)).astype(BF)
    extra = jnp.concatenate([high, low, jnp.zeros((12, HALF), BF)])
    sent = jnp.concatenate(
        [
            summed.astype(BF).reshape(Z * CORE, BLOCK, HALF),
            jnp.broadcast_to(extra[None], (Z * CORE, 16, HALF)),
        ],
        axis=1,
    )
    received = lax.all_to_all(sent, ("z", "core"), 0, 0, tiled=True).astype(F32)
    grads = jnp.sum(received[:, :BLOCK].reshape(Z, 2, BLOCK, HALF), axis=0) * scale
    gains = jnp.sum(received[:, BLOCK : BLOCK + 4], axis=0)
    gains = (gains[:2] + gains[2:]).reshape(1, 4, 128)
    gains = lax.all_to_all(
        jnp.broadcast_to(gains, (Y * XL * XH, 4, 128)), PLANE, 0, 0, tiled=True
    )
    gains = jnp.sum(gains.reshape(Y * XL, XH, Z, CORE * BLOCK), axis=1)
    grad_gain = jnp.transpose(gains, (1, 0, 2)).reshape(D) * scale / gain

    out_mine, out_theirs, d_tokens = rows_pass(tokens, row_gain, d_mine, d_theirs, mine, theirs)
    keys = jnp.where(first, out_mine, out_theirs)
    values = jnp.where(first, out_theirs, out_mine)
    return (keys, values, d_tokens, grads[0], grads[1], grad_gain)


def solution(mesh):
    fine = Mesh(mesh.devices.reshape(Z, Y, XL, CORE, XH), AXES)
    loop = ("z", "y", "xl", "core")
    return jax.shard_map(
        shards,
        mesh=fine,
        in_specs=(
            P(AXES, None),
            P(),
            P(loop, "xh"),
            P(loop, "xh"),
            P(AXES, None),
            P(AXES, None),
        ),
        out_specs=(
            P(AXES, None),
            P(AXES, None),
            P(AXES, None),
            P(loop, "xh"),
            P(loop, "xh"),
            P(),
        ),
        check_vma=False,
    )
```

time: 1080 us -> 190 us (0.18)
  waiting for transfers between devices: 909 us -> 67.3 us
  blocking collectives: 88.8 us -> 42.8 us
  matrix products: 34.9 us -> 0 us
  Pallas kernels: 0 us -> 32.9 us
  starting transfers between devices: 0.16 us -> 15.2 us
  local copies, waits for them, and re-layouts: 20.6 us -> 8.1 us
    unnamed x6 -> x1, waiting for transfers between devices: 523 us -> 0.02 us
    all_gather x2 -> x1, waiting for transfers between devices: 386 us -> 25.6 us  [shards(): mine = lax.all_gather(plane, 'z', axis=0, tiled=True)]
    psum x1 -> x0, blocking collectives: 76.6 us -> none  [shards(): lax.psum(jnp.sum(d_hidden * normal_rows, axis=0), ('loop', 'half')) * scale]
    all_to_all x0 -> x2, blocking collectives: none -> 42.8 us  [the longest x1 24.4 us: shards(): received = lax.all_to_all(sent, ('z', 'core'), 0, 0, tiled=True).astype(F32)]
    all_to_all x0 -> x2, waiting for transfers between devices: none -> 35.5 us  [the longest x1 29.4 us: shards(): summed = lax.all_to_all(terms, PLANE, 0, 0, tiled=True)]
    dot_general x6 -> x0, matrix products: 34.9 us -> none  [the longest x1 9.26 us: shards(): jnp.einsum('tc,dc->td', d_values, full_value, preferred_element_type=jnp....]
    pallas_call x0 -> x2, Pallas kernels: none -> 32.9 us  [the longest x1 21.4 us: rows_pass(): pl.pallas_call(rows_kernel, grid=(2 * Z,), in_specs=[whole((ROWS, D)), wh...]
    unnamed x21 -> x8, local copies, waits for them, and re-layouts: 19.8 us -> 6.39 us
  transfers between devices with their start and end apart: 4 -> 6, of which waited for: 4 -> 4; matrix products, arithmetic and copies ran while one was open for 6% -> 4% of each run, Pallas kernels for 0% -> 6%
where the time goes in v1:
time: 190 us; the launch traced here: 189 us
  waiting for transfers between devices  67.3 us (35%)
  blocking collectives  42.8 us (23%)
  Pallas kernels  32.9 us (17%)
  starting transfers between devices  15.2 us (8%)
  between operations  14.2 us (7%)
  other arithmetic  8.21 us (4%)
  local copies, waits for them, and re-layouts  8.1 us (4%)
    all_to_all x1, waiting for transfers between devices, shards(): summed = lax.all_to_all(terms, PLANE, 0, 0, tiled=True)  29.4 us
    all_gather x1, waiting for transfers between devices, shards(): mine = lax.all_gather(plane, 'z', axis=0, tiled=True)  25.6 us
    all_to_all x1, blocking collectives, shards(): received = lax.all_to_all(sent, ('z', 'core'), 0, 0, tiled=True).astype(F32)  24.4 us
    pallas_call x1, Pallas kernels, rows_pass(): pl.pallas_call(rows_kernel, grid=(2 * Z,), in_specs=[whole((ROWS, D)), wh...  21.4 us
    all_to_all x1, blocking collectives, shards(): lax.all_to_all(sent.reshape(Y * XL * CORE * XH, BLOCK, HALF), ('y', 'xl',...  18.4 us
    pallas_call x1, Pallas kernels, gradient_terms(): pl.pallas_call(grads_kernel, grid=(Z,), in_specs=[whole((ROWS, D)), whole...  11.5 us
    all_to_all x1, starting transfers between devices, shards(): lax.all_to_all(jnp.broadcast_to(gains, (Y * XL * XH, 4, 128)), PLANE, 0,...  7.65 us
    unnamed x8, local copies, waits for them, and re-layouts  6.39 us
  transfers between devices with their start and end apart: 6, of which 4 were waited for; matrix products, arithmetic and copies ran while one was open for 4% of the time, Pallas kernels for 6%

profile of v1, /device:TPU:1, one launch (start us, length us, event | category | flops | bytes accessed | tf_op | source)
XLA Modules:
  0.0 188.6 jit_solution(15481851653352806509)
XLA Ops:
  7.2 0.0 copy-start.1
  7.2 0.0 all-gather.2.cloned.1.call-start
  7.2 0.7 pad_maximum_fusion.1
  8.0 18.4 %all_to_all.20 = bf16[32,32,256]{2,1,0:T(8,128)(2,1)} all-to-all(bf16[32,32,256]{2,1,0:T(8,128)(2,1)S(1)} %bitcast.19), channel_id=1, replica_groups=mesh['z'=8,'y'=4,'xl'=2,'core'=2,'xh'=2] {'y','xl','core','xh'}, dimensions={0} | all-to-all | bytes 1048576 | tf_op jit(solution)/shard_map/all_to_all | solution.py:171
  26.4 0.0 all-gather.2.cloned.1.call-update
  26.5 2.2 %collective-permute-start.1 = (bf16[512,4096]{1,0:T(8,128)(2,1)}, bf16[512,4096]{1,0:T(8,128)(2,1)}, u32[]{:S(2)}, u32[]{:S(2)}) collective-permute-start(bf16[512,4096]{1,0:T(8,128)(2,1)} %own_ref.1), channel_id=1, source_target_pairs={{0,2},{2,0},{1,3},{3,1},{4,6},{6,4},{5,7},{7,5},{8,10},{10,8},{9,1... | collective-permute-start | bytes 12582920 | tf_op jit(solution)/shard_map/ppermute | solution.py:166
  28.7 1.3 broadcast_select_fusion.2
  30.0 0.1 collective-permute-start.2
  30.1 6.1 %collective-permute-done.2.d_other_ref = bf16[512,512]{1,0:T(8,128)(2,1)S(1)} collective-permute-done((bf16[512,512]{1,0:T(8,128)(2,1)S(1)}, bf16[512,512]{1,0:T(8,128)(2,1)S(1)}, u32[]{:S(2)}, u32[]{:S(2)}) %collective-permute-start.2) | collective-permute-done | bytes 524320 | tf_op jit(solution)/shard_map/ppermute | solution.py:166
  36.2 0.0 collective-permute-done.1.other_ref
  36.2 0.0 copy-done.1
  36.2 0.0 copy-start.2
  36.2 2.2 %copy-done.2 = bf16[512,4096]{1,0:T(8,128)(2,1)S(1)} copy-done((bf16[512,4096]{1,0:T(8,128)(2,1)S(1)}, bf16[512,4096]{1,0:T(8,128)(2,1)}, u32[]{:S(2)}) %copy-start.2) | copy-done | bytes 4194328
  38.4 11.5 %gradient_terms.1 = bf16[16,8,2,32,256]{4,3,2,1,0:T(8,128)(2,1)S(1)} custom-call(bf16[512,4096]{1,0:T(8,128)(2,1)S(1)} %copy-done.2, bf16[512,4096]{1,0:T(8,128)(2,1)} %collective-permute-done.1.other_ref, f32[1,4096]{1,0:T(1,128)S(1)} %bitcast.17, bf16[512,512]{1,0:T(8,128)(2,1)S(1)} %get-tuple-element.17.d0_ref.d_own_ref, ...), custom_call_target="tpu_custom_call" | custom-call | flops 4294967296 | bytes 13631488 | tf_op jit(solution)/shard_map/gradient_terms/pallas_call | solution.py:62
  49.9 0.0 copy-start
  49.9 2.0 %copy-done = bf16[16,8,2,32,256]{4,3,2,1,0:T(8,128)(2,1)} copy-done((bf16[16,8,2,32,256]{4,3,2,1,0:T(8,128)(2,1)}, bf16[16,8,2,32,256]{4,3,2,1,0:T(8,128)(2,1)S(1)}, u32[]{:S(2)}) %copy-start) | copy-done | bytes 4194328
  51.9 4.5 %all-to-all-start.1 = ((bf16[16,8,2,32,256]{4,3,2,1,0:T(8,128)(2,1)}), bf16[16,8,2,32,256]{4,3,2,1,0:T(8,128)(2,1)}, u32[]{:S(2)}, u32[]{:S(2)}) async-start(bf16[16,8,2,32,256]{4,3,2,1,0:T(8,128)(2,1)} %copy-done), calls=%async_computation.1 | async-start | bytes 8388608 | tf_op jit(solution)/shard_map/all_to_all | solution.py:182
  56.5 25.6 %all-gather.2.cloned.1.call-done = bf16[256,32,256]{2,1,0:T(8,128)(2,1)} async-done(((bf16[32,32,256]{2,1,0:T(8,128)(2,1)}), bf16[256,32,256]{2,1,0:T(8,128)(2,1)}) %all-gather.2.cloned.1.call-update) | async-done | bytes 4194320 | tf_op jit(solution)/shard_map/all_gather | solution.py:174
  82.1 0.7 collective-permute-start
  82.7 0.1 pad.4.clone
  82.8 29.4 %all-to-all-done.1 = bf16[16,8,2,32,256]{4,3,2,1,0:T(8,128)(2,1)} async-done(((bf16[16,8,2,32,256]{4,3,2,1,0:T(8,128)(2,1)}), bf16[16,8,2,32,256]{4,3,2,1,0:T(8,128)(2,1)}, u32[]{:S(2)}, u32[]{:S(2)}) %all-to-all-start.1) | async-done | bytes 4194336 | tf_op jit(solution)/shard_map/all_to_all | solution.py:182
  112.2 3.2 %convert_reduce_fusion = f32[8,2,32,256]{3,2,1,0:T(8,128)S(1)} fusion(bf16[16,8,2,32,256]{4,3,2,1,0:T(8,128)(2,1)} %all-to-all-done.1), kind=kLoop, calls=%fused_computation | loop fusion | flops 4063232 | bytes 4718592 | tf_op jit(solution)/shard_map/reduce_sum | solution.py:183
  115.3 1.1 fusion.1
  116.5 0.1 reshape.46
  116.6 0.1 maximum_maximum_fusion
  116.7 24.4 %all_to_all.21 = bf16[16,48,256]{2,1,0:T(8,128)(2,1)S(1)} all-to-all(bf16[16,48,256]{2,1,0:T(8,128)(2,1)S(1)} %pad_maximum_fusion), channel_id=1, replica_groups=mesh['z'=8,'y'=4,'xl'=2,'core'=2,'xh'=2] {'z','core'}, dimensions={0} | all-to-all | bytes 786432 | tf_op jit(solution)/shard_map/all_to_all | solution.py:203
  141.1 0.1 convert_element_type.36
  141.2 0.6 broadcast_in_dim.26
  141.8 7.6 %all-to-all-start.3 = ((f32[16,4,128]{2,1,0:T(4,128)}), f32[16,4,128]{2,1,0:T(4,128)S(1)}, u32[]{:S(2)}, u32[]{:S(2)}) async-start(f32[16,4,128]{2,1,0:T(4,128)} %broadcast_in_dim.26), calls=%async_computation.3 | async-start | bytes 65536 | tf_op jit(solution)/shard_map/all_to_all | solution.py:207
  149.6 0.6 slice_bitcast_fusion
  150.2 6.1 %all-to-all-done.3 = f32[16,4,128]{2,1,0:T(4,128)S(1)} async-done(((f32[16,4,128]{2,1,0:T(4,128)}), f32[16,4,128]{2,1,0:T(4,128)S(1)}, u32[]{:S(2)}, u32[]{:S(2)}) %all-to-all-start.3) | async-done | bytes 32800 | tf_op jit(solution)/shard_map/all_to_all | solution.py:207
  156.4 0.1 reshape.48
  156.5 0.1 mul.31
  156.6 0.6 div.3
  157.2 0.0 collective-permute-done.w1_ref
  157.2 0.0 copy-start.3
  157.2 2.2 %copy-done.3 = bf16[512,4096]{1,0:T(8,128)(2,1)S(1)} copy-done((bf16[512,4096]{1,0:T(8,128)(2,1)S(1)}, bf16[512,4096]{1,0:T(8,128)(2,1)}, u32[]{:S(2)}) %copy-start.3) | copy-done | bytes 4194328
  159.4 21.4 %rows_pass.1 = (bf16[512,512]{1,0:T(8,128)(2,1)S(1)}, bf16[512,512]{1,0:T(8,128)(2,1)S(1)}, bf16[512,4096]{1,0:T(8,128)(2,1)}) custom-call(bf16[512,4096]{1,0:T(8,128)(2,1)S(1)} %copy-done.3, f32[1,4096]{1,0:T(1,128)S(1)} %bitcast.18, bf16[512,512]{1,0:T(8,128)(2,1)S(1)} %get-tuple-element.17.d0_ref.d_own_ref, ...), custom_call_target="tpu_custom_call" | custom-call | flops 8589934592 | bytes 27262976 | tf_op jit(solution)/shard_map/rows_pass/pallas_call | solution.py:129
  180.8 1.0 broadcast_select_fusion
  (14 shorter events, 0.3 us)
Async XLA Ops:
  7.2 29.1 %copy-start.1 = (f32[4096]{0:T(1024)S(1)}, f32[4096]{0:T(1024)}, u32[]{:S(2)}) copy-start(f32[4096]{0:T(1024)} %param.7) | copy-start | bytes 49156
  7.2 74.9 %all-gather.2.cloned.1.call-start = ((), (), s32[]{:S(2)}) async-start(), calls=%async_computation.4 | async-start | bytes 4718592 | tf_op jit(solution)/shard_map/all_gather | solution.py:174
  26.5 9.8 %collective-permute-start.1 = (bf16[512,4096]{1,0:T(8,128)(2,1)}, bf16[512,4096]{1,0:T(8,128)(2,1)}, u32[]{:S(2)}, u32[]{:S(2)}) collective-permute-start(bf16[512,4096]{1,0:T(8,128)(2,1)} %own_ref.1), channel_id=1, source_target_pairs={{0,2},{2,0},{1,3},{3,1},{4,6},{6,4},{5,7},{7,5},{8,10},{10,8},{9,1... | collective-permute-start | bytes 12582920 | tf_op jit(solution)/shard_map/ppermute | solution.py:166
  30.0 6.3 %collective-permute-start.2 = (bf16[512,512]{1,0:T(8,128)(2,1)S(1)}, bf16[512,512]{1,0:T(8,128)(2,1)S(1)}, u32[]{:S(2)}, u32[]{:S(2)}) collective-permute-start(bf16[512,512]{1,0:T(8,128)(2,1)S(1)} %get-tuple-element.16.d1_ref), channel_id=1, source_target_pairs={{0,2},{2,0},{1,3},{3,1},{4,6},{6,4},{5,7},{7,5},{8,10},{10,8},{9,1... | collective-permute-start | bytes 1572872 | tf_op jit(solution)/shard_map/ppermute | solution.py:166
  36.2 2.2 %copy-start.2 = (bf16[512,4096]{1,0:T(8,128)(2,1)S(1)}, bf16[512,4096]{1,0:T(8,128)(2,1)}, u32[]{:S(2)}) copy-start(bf16[512,4096]{1,0:T(8,128)(2,1)} %own_ref.1) | copy-start | bytes 12582916
  49.9 2.0 %copy-start = (bf16[16,8,2,32,256]{4,3,2,1,0:T(8,128)(2,1)}, bf16[16,8,2,32,256]{4,3,2,1,0:T(8,128)(2,1)S(1)}, u32[]{:S(2)}) copy-start(bf16[16,8,2,32,256]{4,3,2,1,0:T(8,128)(2,1)S(1)} %gradient_terms.1) | copy-start | bytes 12582916
  51.9 60.2 %all-to-all-start.1 = ((bf16[16,8,2,32,256]{4,3,2,1,0:T(8,128)(2,1)}), bf16[16,8,2,32,256]{4,3,2,1,0:T(8,128)(2,1)}, u32[]{:S(2)}, u32[]{:S(2)}) async-start(bf16[16,8,2,32,256]{4,3,2,1,0:T(8,128)(2,1)} %copy-done), calls=%async_computation.1 | async-start | bytes 8388608 | tf_op jit(solution)/shard_map/all_to_all | solution.py:182
  82.1 75.1 %collective-permute-start = (bf16[128,2,32,256]{3,2,1,0:T(8,128)(2,1)}, bf16[128,2,32,256]{3,2,1,0:T(8,128)(2,1)}, u32[]{:S(2)}, u32[]{:S(2)}) collective-permute-start(bf16[128,2,32,256]{3,2,1,0:T(8,128)(2,1)} %bitcast.22), channel_id=1, source_target_pairs={{0,2},{2,0},{1,3},{3,1},{4,6},{6,4},{5,7},{7,5},{8,10},{10,8},{9,1... | collective-permute-start | bytes 12582920 | tf_op jit(solution)/shard_map/ppermute | solution.py:166
  141.8 14.5 %all-to-all-start.3 = ((f32[16,4,128]{2,1,0:T(4,128)}), f32[16,4,128]{2,1,0:T(4,128)S(1)}, u32[]{:S(2)}, u32[]{:S(2)}) async-start(f32[16,4,128]{2,1,0:T(4,128)} %broadcast_in_dim.26), calls=%async_computation.3 | async-start | bytes 65536 | tf_op jit(solution)/shard_map/all_to_all | solution.py:207
  157.2 2.2 %copy-start.3 = (bf16[512,4096]{1,0:T(8,128)(2,1)S(1)}, bf16[512,4096]{1,0:T(8,128)(2,1)}, u32[]{:S(2)}) copy-start(bf16[512,4096]{1,0:T(8,128)(2,1)} %own_ref.1) | copy-start | bytes 12582916
Sparse Core Ops, SparseCore 0:
  26.6 55.4 all-gather.1

commit v2 on v0

v2 whole, which is shorter than its diff:
```python
import math

import jax
import jax.numpy as jnp
from jax import lax
from jax.experimental import pallas as pl
from jax.experimental.pallas import tpu as pltpu
from jax.sharding import Mesh
from jax.sharding import PartitionSpec as P

Z, Y, XL, CORE, XH = 8, 4, 2, 2, 2
X = XL * XH
AXES = ("z", "y", "xl", "core", "xh")
PLANE = ("y", "xl", "xh")
ROWS = 512
D = 4096
C = 512
W = D // Z
HALF = C // XH
BLOCK = 32
PART = Z // 2
EPS = 1e-05
BF = jnp.bfloat16
F32 = jnp.float32
VMEM = 60 * 1024 * 1024
SMALL = 8 * 1024 * 1024


def params(limit=VMEM):
    return pltpu.CompilerParams(vmem_limit_bytes=limit)


def tie_kernel(a_ref, other_ref, out_ref):
    del a_ref, other_ref, out_ref


def after(a, other):
    return pl.pallas_call(
        tie_kernel,
        in_specs=[pl.BlockSpec(memory_space=pl.ANY)] * 2,
        out_specs=pl.BlockSpec(memory_space=pl.ANY),
        out_shape=jax.ShapeDtypeStruct(a.shape, a.dtype),
        input_output_aliases={0: 0},
        name="after",
    )(a, other)


def copies(pairs, sems):
    started = []
    for at, (source, target) in enumerate(pairs):
        copy = pltpu.make_async_copy(source, target, sems.at[at])
        copy.start()
        started.append(copy)
    return started


def pick(core, first, second, target, sem):
    @pl.when(core == 0)
    def _():
        pltpu.make_async_copy(first, target, sem).start()

    @pl.when(core != 0)
    def _():
        pltpu.make_async_copy(second, target, sem).start()

    return pltpu.make_async_copy(first, target, sem)


SMEM = pl.BlockSpec(memory_space=pltpu.SMEM)
ANY = pl.BlockSpec(memory_space=pl.ANY)
INNER = pl.BlockSpec(memory_space=pltpu.VMEM)


def cheap():
    return pl.CostEstimate(flops=1 << 20, bytes_accessed=1 << 20, transcendentals=0)


def inverse_kernel(x_ref, out_ref, x_buf, sems):
    rows = ROWS // 8
    parts = [pl.ds(i * rows, rows) for i in range(8)]
    started = copies([(x_ref.at[part], x_buf.at[part]) for part in parts], sems)
    for part, copy in zip(parts, started):
        copy.wait()
        squares = jnp.zeros((rows, 128), F32)
        for j in range(D // 128):
            piece = x_buf[part, j * 128 : (j + 1) * 128].astype(F32)
            squares = squares + piece * piece
        mean = jnp.sum(squares, axis=1, keepdims=True) * (1.0 / D)
        out_ref[part, :] = jnp.broadcast_to(lax.rsqrt(mean + EPS), (rows, 128))


def inverses(x):
    return pl.pallas_call(
        inverse_kernel,
        in_specs=[ANY],
        out_specs=INNER,
        out_shape=jax.ShapeDtypeStruct((ROWS, 128), F32),
        scratch_shapes=[pltpu.VMEM((ROWS, D), BF), pltpu.SemaphoreType.DMA((8,))],
        compiler_params=params(),
        cost_estimate=cheap(),
        name="inverses",
    )(x)


WIDE = 2 * W


def grads_kernel(along_x, place_ref, own_ref, other_ref, gain_ref, inv_own_ref, inv_other_ref,
                 keys_own_ref, values_own_ref, keys_other_ref, values_other_ref, *rest):
    outs = rest[:4]
    x_buf, d_buf, inv_buf, gain_buf, total_ref, out_buf, sems, out_sems = rest[4:]
    x_at, y_at, core_at = place_ref[0], place_ref[1], place_ref[2]
    start = 0 if along_x else PART * W
    parts = PART * W // WIDE
    small = copies(
        [
            (gain_ref.at[:, pl.ds(start, PART * W)], gain_buf),
            (inv_own_ref, inv_buf.at[0]),
            (inv_other_ref, inv_buf.at[1]),
        ],
        sems,
    )
    small.append(pick(core_at, keys_own_ref, values_own_ref, d_buf.at[0], sems.at[3]))
    small.append(pick(core_at, keys_other_ref, values_other_ref, d_buf.at[1], sems.at[4]))
    large = []
    for part in range(parts):
        for which, ref in enumerate((own_ref, other_ref)):
            for piece in range(2):
                lanes = pl.ds(part * WIDE + piece * W, W)
                copy = pltpu.make_async_copy(
                    ref.at[:, pl.ds(start + part * WIDE + piece * W, W)],
                    x_buf.at[which, :, lanes],
                    sems.at[5 + len(large)],
                )
                copy.start()
                large.append(copy)
    for copy in small:
        copy.wait()
    sent = []
    for part in range(parts):
        for copy in large[4 * part : 4 * part + 4]:
            copy.wait()
        lanes = slice(part * WIDE, (part + 1) * WIDE)
        total = None
        for which in range(2):
            normal = x_buf[which, :, lanes].astype(F32) * inv_buf[which, :, :1]
            hidden = (normal * gain_buf[:, lanes]).astype(BF)
            term = lax.dot_general(
                hidden, d_buf[which], (((0,), (0,)), ((), ())), preferred_element_type=F32
            )
            total = term if total is None else total + term
        total_ref[lanes, :] = total.astype(BF)
        for z in range(part * WIDE // W, (part + 1) * WIDE // W):
            for shift in range(4):
                for other in range(4):
                    if along_x:
                        x, y = lax.rem(x_at + shift, X), other
                    else:
                        x, y = other, lax.rem(y_at + shift, Y)
                    low, high = lax.rem(x, XL), lax.div(x, XL)
                    columns = pl.ds(pl.multiple_of(high * HALF, HALF), HALF)
                    for core in range(CORE):
                        first = z * W + ((y * XL + low) * CORE + core) * BLOCK
                        first = pl.multiple_of(first, BLOCK)
                        out_buf[shift, other, z, core] = total_ref[pl.ds(first, BLOCK), columns]
        zs = pl.ds(part * WIDE // W, WIDE // W)
        for shift in range(4):
            copy = pltpu.make_async_copy(
                out_buf.at[shift, :, zs], outs[shift].at[:, zs], out_sems.at[part, shift]
            )
            copy.start()
            sent.append(copy)
    for copy in sent:
        copy.wait()


def gradient_terms(toward_x, *inputs):
    shape = (4, PART, CORE, BLOCK, HALF)

    def kernel(*refs):
        grads_kernel(toward_x, *refs)

    return pl.pallas_call(
        kernel,
        in_specs=[SMEM] + [ANY] * 9,
        out_specs=[ANY] * 4,
        out_shape=[jax.ShapeDtypeStruct(shape, BF)] * 4,
        scratch_shapes=[
            pltpu.VMEM((2, ROWS, PART * W), BF),
            pltpu.VMEM((2, ROWS, C), BF),
            pltpu.VMEM((2, ROWS, 128), F32),
            pltpu.VMEM((1, PART * W), F32),
            pltpu.VMEM((PART * W, C), BF),
            pltpu.VMEM((4,) + shape, BF),
            pltpu.SemaphoreType.DMA((13,)),
            pltpu.SemaphoreType.DMA((2, 4)),
        ],
        compiler_params=params(),
        cost_estimate=pl.CostEstimate(
            flops=2 * ROWS * D * C, bytes_accessed=8 << 20, transcendentals=0
        )
        if toward_x
        else cheap(),
        name="gradient_terms_x" if toward_x else "gradient_terms_y",
    )(*inputs)


def sums_kernel(place_ref, *refs):
    ins, outs = refs[:4], refs[4:]
    for shift in range(4):
        at = lax.rem(place_ref[0] + shift, 4)
        total = ins[0][at].astype(F32)
        for ref in ins[1:]:
            total = total + ref[at].astype(F32)
        outs[shift][...] = total.astype(outs[shift].dtype)


def sums(at, pieces, name):
    shape = (PART, CORE, BLOCK, HALF)
    return pl.pallas_call(
        sums_kernel,
        in_specs=[SMEM] + [INNER] * 4,
        out_specs=[INNER] * 4,
        out_shape=[jax.ShapeDtypeStruct(shape, F32 if k == 0 else BF) for k in range(4)],
        compiler_params=params(SMALL),
        cost_estimate=pl.CostEstimate(flops=1 << 20, bytes_accessed=3 << 20, transcendentals=0),
        name=name,
    )(at.reshape(1), *pieces)


EXTRA = 16


def pack_kernel(*refs):
    x_first, y_first, w_ref, out_ref, prod_ref = refs[:4], refs[4:8], refs[8], refs[9], refs[10]
    for start, pieces in ((0, x_first), (PART, y_first)):
        for z in range(PART):
            for core in range(CORE):
                total = pieces[0][z, core]
                for ref in pieces[1:]:
                    total = total + ref[z, core].astype(F32)
                at = (start + z) * CORE + core
                out_ref[at, :BLOCK] = total.astype(BF)
                prod_ref[at * BLOCK : (at + 1) * BLOCK] = total * w_ref[at].astype(F32)
    gains = lax.dot_general(
        jnp.ones((8, HALF), F32),
        prod_ref[...],
        (((1,), (1,)), ((), ())),
        precision=lax.Precision.HIGHEST,
        preferred_element_type=F32,
    )[:1]
    upper = gains.astype(BF).astype(F32)
    lower = gains - upper
    row = lax.broadcasted_iota(jnp.int32, (EXTRA, HALF), 0)
    extra = jnp.zeros((EXTRA, HALF), F32)
    for at, line in enumerate(
        (upper[:, :HALF], upper[:, HALF:], lower[:, :HALF], lower[:, HALF:])
    ):
        extra = jnp.where(row == at, jnp.broadcast_to(line, (EXTRA, HALF)), extra)
    extra = extra.astype(BF)
    for at in range(Z * CORE):
        out_ref[at, BLOCK:] = extra


def pack(x_first, y_first, blocks):
    return pl.pallas_call(
        pack_kernel,
        in_specs=[INNER] * 9,
        out_specs=INNER,
        out_shape=jax.ShapeDtypeStruct((Z * CORE, BLOCK + EXTRA, HALF), BF),
        scratch_shapes=[pltpu.VMEM((Z * CORE * BLOCK, HALF), F32)],
        compiler_params=params(SMALL),
        cost_estimate=cheap(),
        name="pack",
    )(*x_first, *y_first, blocks)


def unpack_kernel(scale, in_ref, key_ref, value_ref, gains_ref):
    for which, ref in enumerate((key_ref, value_ref)):
        total = in_ref[which, :BLOCK].astype(F32)
        for z in range(1, Z):
            total = total + in_ref[z * 2 + which, :BLOCK].astype(F32)
        ref[...] = total * scale
    extra = in_ref[0, BLOCK:].astype(F32)
    for at in range(1, Z * CORE):
        extra = extra + in_ref[at, BLOCK:].astype(F32)
    for line in range(2):
        gains = extra[line : line + 1] + extra[line + 2 : line + 3]
        for piece in range(2):
            lanes = gains[:, piece * 128 : (piece + 1) * 128]
            for at in range(Y * XL * XH):
                gains_ref[at, line * 2 + piece : line * 2 + piece + 1] = lanes


def unpack(scale, received):
    def kernel(*refs):
        unpack_kernel(scale, *refs)

    return pl.pallas_call(
        kernel,
        in_specs=[INNER],
        out_specs=[INNER] * 3,
        out_shape=[
            jax.ShapeDtypeStruct((BLOCK, HALF), F32),
            jax.ShapeDtypeStruct((BLOCK, HALF), F32),
            jax.ShapeDtypeStruct((Y * XL * XH, 4, 128), F32),
        ],
        compiler_params=params(SMALL),
        cost_estimate=cheap(),
        name="unpack",
    )(received)


STEPS = D // WIDE


def weight_rows(buf, part):
    rows = WIDE // BLOCK
    ref = buf.at[pl.ds(part * rows, rows)]
    return jnp.concatenate([ref[:, half].reshape(WIDE, HALF) for half in range(XH)], axis=1)


def hidden_columns(x_buf, inv_buf, gain_buf, part):
    lanes = slice(part * WIDE, (part + 1) * WIDE)
    return (x_buf[:, lanes].astype(F32) * inv_buf[:, :1] * gain_buf[:, lanes]).astype(BF)


def pieces_of(x_ref, x_buf, weights):
    pairs = []
    rows = D // BLOCK // Z
    for part in range(STEPS):
        for at in range(part * WIDE // W, (part + 1) * WIDE // W):
            lanes = pl.ds(at * W, W)
            pairs.append((x_ref.at[:, lanes], x_buf.at[:, lanes]))
            for ref, buf in weights:
                block = pl.ds(at * rows, rows)
                pairs.append((ref.at[block], buf.at[block]))
    return pairs


def forward_kernel(place_ref, x_ref, gain_ref, inv_ref, keys_ref, values_ref, w_ref,
                   out_ref, along_ref, x_buf, w_buf, d_buf, inv_buf, gain_buf, sems, small_sems):
    small = copies([(gain_ref, gain_buf), (inv_ref, inv_buf)], small_sems)
    small.append(pick(place_ref[2], keys_ref, values_ref, d_buf, small_sems.at[2]))
    large = copies(pieces_of(x_ref, x_buf, [(w_ref, w_buf)]), sems)
    each = len(large) // STEPS
    for copy in small:
        copy.wait()
    total = None
    for part in range(STEPS):
        for copy in large[part * each : (part + 1) * each]:
            copy.wait()
        hidden = hidden_columns(x_buf, inv_buf, gain_buf, part)
        term = jnp.dot(hidden, weight_rows(w_buf, part), preferred_element_type=F32)
        total = term if total is None else total + term
    out_ref[...] = total.astype(BF)
    along = jnp.sum(total * d_buf[...].astype(F32), axis=1, keepdims=True) * (1.0 / D)
    along_ref[...] = jnp.broadcast_to(along, (ROWS, 128))


def forward(*inputs):
    return pl.pallas_call(
        forward_kernel,
        in_specs=[SMEM] + [ANY] * 6,
        out_specs=[INNER] * 2,
        out_shape=[
            jax.ShapeDtypeStruct((ROWS, C), BF),
            jax.ShapeDtypeStruct((ROWS, 128), F32),
        ],
        scratch_shapes=[
            pltpu.VMEM((ROWS, D), BF),
            pltpu.VMEM((D // BLOCK, XH, BLOCK, HALF), BF),
            pltpu.VMEM((ROWS, C), BF),
            pltpu.VMEM((ROWS, 128), F32),
            pltpu.VMEM((1, D), F32),
            pltpu.SemaphoreType.DMA((16,)),
            pltpu.SemaphoreType.DMA((3,)),
        ],
        compiler_params=params(),
        cost_estimate=cheap(),
        name="forward",
    )(*inputs)


def backward_kernel(place_ref, x_ref, gain_ref, inv_ref, keys_ref, values_ref, mine_ref,
                    theirs_ref, done_ref, along_ref, out_keys_ref, out_values_ref, dx_ref,
                    x_buf, mine_buf, theirs_buf, d_buf, inv_buf, gain_buf, along_buf, out_buf,
                    dx_buf, sems, small_sems, out_sems, dx_sems):
    core = place_ref[2]
    small = copies(
        [(gain_ref, gain_buf), (inv_ref, inv_buf), (along_ref, along_buf), (done_ref, out_buf.at[0])],
        small_sems,
    )
    small.append(pick(core, keys_ref, values_ref, d_buf.at[0], small_sems.at[4]))
    small.append(pick(core, values_ref, keys_ref, d_buf.at[1], small_sems.at[5]))
    large = copies(
        pieces_of(x_ref, x_buf, [(theirs_ref, theirs_buf), (mine_ref, mine_buf)]), sems
    )
    each = len(large) // STEPS
    for copy in small:
        copy.wait()
    total = None
    for part in range(STEPS):
        for copy in large[part * each : (part + 1) * each]:
            copy.wait()
        hidden = hidden_columns(x_buf, inv_buf, gain_buf, part)
        term = jnp.dot(hidden, weight_rows(theirs_buf, part), preferred_element_type=F32)
        total = term if total is None else total + term
    out_buf[1] = total.astype(BF)
    sent = []
    for which in range(2):
        refs = (out_keys_ref, out_values_ref) if which == 0 else (out_values_ref, out_keys_ref)

        @pl.when(core == 0)
        def _():
            pltpu.make_async_copy(out_buf.at[which], refs[0], out_sems.at[which]).start()

        @pl.when(core != 0)
        def _():
            pltpu.make_async_copy(out_buf.at[which], refs[1], out_sems.at[which]).start()

        sent.append(pltpu.make_async_copy(out_buf.at[which], refs[0], out_sems.at[which]))
    along = jnp.sum(total * d_buf[1].astype(F32), axis=1, keepdims=True) * (1.0 / D)
    along = along + along_buf[:, :1]
    inverse = inv_buf[:, :1]
    for part in range(STEPS):
        lanes = slice(part * WIDE, (part + 1) * WIDE)
        d_hidden = None
        for which, buf in enumerate((mine_buf, theirs_buf)):
            term = lax.dot_general(
                d_buf[which],
                weight_rows(buf, part),
                (((1,), (1,)), ((), ())),
                preferred_element_type=F32,
            )
            d_hidden = term if d_hidden is None else d_hidden + term
        normal = x_buf[:, lanes].astype(F32) * inverse
        dx_buf[:, lanes] = (inverse * (d_hidden * gain_buf[:, lanes] - normal * along)).astype(BF)
        span = pl.ds(part * WIDE, WIDE)
        copy = pltpu.make_async_copy(dx_buf.at[:, span], dx_ref.at[:, span], dx_sems.at[part])
        copy.start()
        sent.append(copy)
    for copy in sent:
        copy.wait()


def backward(*inputs):
    return pl.pallas_call(
        backward_kernel,
        in_specs=[SMEM] + [ANY] * 9,
        out_specs=[ANY] * 3,
        out_shape=[
            jax.ShapeDtypeStruct((ROWS, C), BF),
            jax.ShapeDtypeStruct((ROWS, C), BF),
            jax.ShapeDtypeStruct((ROWS, D), BF),
        ],
        scratch_shapes=[
            pltpu.VMEM((ROWS, D), BF),
            pltpu.VMEM((D // BLOCK, XH, BLOCK, HALF), BF),
            pltpu.VMEM((D // BLOCK, XH, BLOCK, HALF), BF),
            pltpu.VMEM((2, ROWS, C), BF),
            pltpu.VMEM((ROWS, 128), F32),
            pltpu.VMEM((1, D), F32),
            pltpu.VMEM((ROWS, 128), F32),
            pltpu.VMEM((2, ROWS, C), BF),
            pltpu.VMEM((ROWS, D), BF),
            pltpu.SemaphoreType.DMA((24,)),
            pltpu.SemaphoreType.DMA((6,)),
            pltpu.SemaphoreType.DMA((2,)),
            pltpu.SemaphoreType.DMA((STEPS,)),
        ],
        compiler_params=params(),
        cost_estimate=pl.CostEstimate(
            flops=6 * ROWS * D * C, bytes_accessed=18 << 20, transcendentals=0
        ),
        name="backward",
    )(*inputs)


def swap(a):
    return lax.ppermute(a, "core", [(0, 1), (1, 0)])


def x_index(at):
    return (at % XL) * XH + at // XL


def along_x(a, shift):
    pairs = [(x_index(i), x_index((i + shift) % X)) for i in range(X)]
    return lax.ppermute(a, ("xl", "xh"), pairs)


def along_y(a, shift):
    return lax.ppermute(a, "y", [(i, (i + shift) % Y) for i in range(Y)])


def spread(move, pieces):
    return [pieces[0]] + [move(pieces[shift], shift) for shift in range(1, 4)]


def shards(tokens, gain, w_key, w_value, d_keys, d_values):
    scale = 1.0 / math.sqrt(ROWS * Z * Y * XL * CORE * XH)
    y_at, low, high = lax.axis_index("y"), lax.axis_index("xl"), lax.axis_index("xh")
    x_at = high * XL + low
    place = jnp.stack([x_at, y_at, lax.axis_index("core")]).astype(jnp.int32)
    row_gain = gain.reshape(1, D)

    pair = jnp.stack([w_key, w_value])
    sent = jnp.broadcast_to(pair[None, :, None], (Y * XL, CORE, XH, BLOCK, HALF))
    plane = lax.all_to_all(
        sent.reshape(Y * XL * CORE * XH, BLOCK, HALF), ("y", "xl", "core", "xh"), 0, 0, tiled=True
    )

    inv = inverses(tokens)
    inputs = (place, tokens, swap(tokens), row_gain, inv, swap(inv))
    inputs += (d_keys, d_values, swap(d_keys), swap(d_values))
    y_first = gradient_terms(False, *inputs)
    x_first = gradient_terms(True, *inputs)
    plane = after(plane, y_first[0])
    mine = lax.all_gather(plane, "z", axis=0, tiled=True)

    x_first = spread(along_y, sums(place[1], spread(along_x, x_first), "sums_x"))
    y_first = spread(along_x, sums(place[0], spread(along_y, y_first), "sums_y"))
    blocks = lax.dynamic_slice(
        mine.reshape(Z, Y * XL, CORE, XH, BLOCK, HALF),
        (0, y_at * XL + low, 0, high, 0, 0),
        (Z, 1, CORE, 1, BLOCK, HALF),
    ).reshape(Z * CORE, BLOCK, HALF)
    sent = pack(x_first, y_first, blocks)
    received = lax.all_to_all(sent, ("z", "core"), 0, 0, tiled=True)

    mine = after(mine, sent).reshape(D // BLOCK, XH, BLOCK, HALF)
    theirs = swap(mine)
    row_inputs = (place, tokens, row_gain, inv, d_keys, d_values, mine)
    out_mine, along = forward(*row_inputs)
    grad_key, grad_value, gains = unpack(scale, after(received, along))

    keys, values, d_tokens = backward(*row_inputs, theirs, out_mine, along)
    gains = lax.all_to_all(gains, PLANE, 0, 0, tiled=True)
    gains = after(gains, d_tokens)
    gains = jnp.sum(gains.reshape(Y * XL, XH, Z, CORE * BLOCK), axis=1)
    grad_gain = jnp.transpose(gains, (1, 0, 2)).reshape(D) * scale / gain
    return (keys, values, d_tokens, grad_key, grad_value, grad_gain)


def solution(mesh):
    fine = Mesh(mesh.devices.reshape(Z, Y, XL, CORE, XH), AXES)
    loop = ("z", "y", "xl", "core")
    return jax.shard_map(
        shards,
        mesh=fine,
        in_specs=(
            P(AXES, None),
            P(),
            P(loop, "xh"),
            P(loop, "xh"),
            P(AXES, None),
            P(AXES, None),
        ),
        out_specs=(
            P(AXES, None),
            P(AXES, None),
            P(AXES, None),
            P(loop, "xh"),
            P(loop, "xh"),
            P(),
        ),
        check_vma=False,
    )
```

time: 1080 us -> 145 us (0.13)
  waiting for transfers between devices: 909 us -> 35.5 us
  blocking collectives: 88.8 us -> 0 us
  Pallas kernels: 0 us -> 42.5 us
  starting transfers between devices: 0.16 us -> 41.7 us
  matrix products: 34.9 us -> 0 us
  other arithmetic: 16 us -> 2.04 us
  local copies, waits for them, and re-layouts: 20.6 us -> 8.71 us
    unnamed x6 -> x1, waiting for transfers between devices: 523 us -> 0.02 us
    all_gather x2 -> x1, waiting for transfers between devices: 386 us -> 12.4 us  [shards(): mine = lax.all_gather(plane, 'z', axis=0, tiled=True)]
    psum x1 -> x0, blocking collectives: 76.6 us -> none  [shards(): lax.psum(jnp.sum(d_hidden * normal_rows, axis=0), ('loop', 'half')) * scale]
    pallas_call x0 -> x13, Pallas kernels: none -> 42.5 us  [the longest x1 14.7 us: backward(): pl.pallas_call(backward_kernel, in_specs=[SMEM] + [ANY] * 9, out_specs=[A...]
    dot_general x6 -> x0, matrix products: 34.9 us -> none  [the longest x1 9.26 us: shards(): jnp.einsum('tc,dc->td', d_values, full_value, preferred_element_type=jnp....]
    ppermute x0 -> x17, starting transfers between devices: none -> 25.2 us  [the longest x6 11 us: along_y(): return lax.ppermute(a, 'y', [(i, (i + shift) % Y) for i in range(Y)])]
    ppermute x0 -> x17, waiting for transfers between devices: none -> 16.7 us  [the longest x6 15.8 us: along_x(): return lax.ppermute(a, ('xl', 'xh'), pairs)]
    all_to_all x0 -> x3, starting transfers between devices: none -> 16.5 us  [the longest x1 6.54 us: shards(): gains = lax.all_to_all(gains, PLANE, 0, 0, tiled=True)]
  transfers between devices with their start and end apart: 4 -> 21, of which waited for: 4 -> 5; matrix products, arithmetic and copies ran while one was open for 6% -> 2% of each run, Pallas kernels for 0% -> 29%
where the time goes in v2:
time: 145 us
  Pallas kernels  42.5 us (29%)
  starting transfers between devices  41.7 us (29%)
  waiting for transfers between devices  35.5 us (24%)
  between operations  14.3 us (10%)
  local copies, waits for them, and re-layouts  8.71 us (6%)
  other arithmetic  2.04 us (1%)
    ppermute x6, waiting for transfers between devices, along_x(): return lax.ppermute(a, ('xl', 'xh'), pairs)  15.8 us
    pallas_call x1, Pallas kernels, backward(): pl.pallas_call(backward_kernel, in_specs=[SMEM] + [ANY] * 9, out_specs=[A...  14.7 us
    pallas_call x2, Pallas kernels, gradient_terms(): pl.pallas_call(kernel, in_specs=[SMEM] + [ANY] * 9, out_specs=[ANY] * 4,...  14.3 us
    all_gather x1, waiting for transfers between devices, shards(): mine = lax.all_gather(plane, 'z', axis=0, tiled=True)  12.4 us
    ppermute x6, starting transfers between devices, along_y(): return lax.ppermute(a, 'y', [(i, (i + shift) % Y) for i in range(Y)])  11 us
    ppermute x6, starting transfers between devices, along_x(): return lax.ppermute(a, ('xl', 'xh'), pairs)  9.41 us
    pallas_call x1, Pallas kernels, forward(): pl.pallas_call(forward_kernel, in_specs=[SMEM] + [ANY] * 6, out_specs=[IN...  8.2 us
    all_to_all x1, starting transfers between devices, shards(): gains = lax.all_to_all(gains, PLANE, 0, 0, tiled=True)  6.54 us
  transfers between devices with their start and end apart: 21, of which 5 were waited for; matrix products, arithmetic and copies ran while one was open for 2% of the time, Pallas kernels for 29%

profile of v2, /device:TPU:1, one launch (start us, length us, event | category | flops | bytes accessed | tf_op | source)
XLA Modules:
  0.0 144.7 jit_solution(9558569160460780988)
XLA Ops:
  7.2 3.3 %collective-permute-start = (bf16[512,4096]{1,0:T(8,128)(2,1)}, bf16[512,4096]{1,0:T(8,128)(2,1)}, u32[]{:S(2)}, u32[]{:S(2)}) collective-permute-start(bf16[512,4096]{1,0:T(8,128)(2,1)} %x_ref.5), channel_id=1, source_target_pairs={{0,2},{2,0},{1,3},{3,1},{4,6},{6,4},{5,7},{7,5},{8,10},{10,8},{9,1... | collective-permute-start | bytes 12582920 | tf_op jit(solution)/shard_map/ppermute | solution.py:481
  10.5 0.1 collective-permute-start.2
  10.6 0.4 collective-permute-start.3
  11.0 0.7 pad_maximum_fusion
  11.7 0.9 broadcast_in_dim.2
  12.6 5.5 %all-to-all-start = ((bf16[32,32,256]{2,1,0:T(8,128)(2,1)}), bf16[32,32,256]{2,1,0:T(8,128)(2,1)S(1)}, u32[]{:S(2)}, u32[]{:S(2)}) async-start(bf16[32,32,256]{2,1,0:T(8,128)(2,1)} %bitcast.6), calls=%async_computation | async-start | bytes 1048576 | tf_op jit(solution)/shard_map/all_to_all | solution.py:510
  18.1 0.0 all-gather.2.cloned.1.call-start
  18.1 3.4 %inverses.1.refs_4_.inv_ref = f32[512,128]{1,0:T(8,128)} custom-call(bf16[512,4096]{1,0:T(8,128)(2,1)} %x_ref.5), custom_call_target="tpu_custom_call" | custom-call | flops 1048576 | bytes 1048576 | tf_op jit(solution)/shard_map/inverses/pallas_call | solution.py:93
  21.6 0.3 collective-permute-start.1
  21.9 0.7 pad_add_fusion.refs_0_.place_ref
  22.6 0.8 collective-permute-done.1.refs_5_
  23.4 0.0 collective-permute-done.2.refs_8_
  23.4 0.0 collective-permute-done.3.refs_9_
  23.4 0.0 copy-start.7
  23.4 0.0 collective-permute-done.refs_2_
  23.4 0.7 copy-done.8
  24.1 0.2 copy-done.6
  24.3 0.2 copy-done.7
  24.4 7.0 %gradient_terms_y.1 = (bf16[4,4,2,32,256]{4,3,2,1,0:T(8,128)(2,1)}, bf16[4,4,2,32,256]{4,3,2,1,0:T(8,128)(2,1)}, bf16[4,4,2,32,256]{4,3,2,1,0:T(8,128)(2,1)}, bf16[4,4,2,32,256]{4,3,2,1,0:T(8,128)(2,1)}) custom-call(s32[3]{0:T(128)} %pad_add_fusion.refs_0_.place_ref, bf16[512,4096]{1,0:T(8,128)(2,1)} %x_ref.5, ...), custom_call_target="tpu_custom_call" | custom-call | flops 1048576 | bytes 1048576 | tf_op jit(solution)/shard_map/gradient_terms_y/pallas_call | solution.py:183
  31.5 0.0 all-to-all-done.a_ref
  31.5 0.0 copy-start.5
  31.5 0.8 copy-done.5
  32.3 0.0 all-gather.2.cloned.1.call-update
  32.3 7.3 %gradient_terms_x.1 = (bf16[4,4,2,32,256]{4,3,2,1,0:T(8,128)(2,1)}, bf16[4,4,2,32,256]{4,3,2,1,0:T(8,128)(2,1)}, bf16[4,4,2,32,256]{4,3,2,1,0:T(8,128)(2,1)}, bf16[4,4,2,32,256]{4,3,2,1,0:T(8,128)(2,1)}) custom-call(s32[3]{0:T(128)} %pad_add_fusion.refs_0_.place_ref, bf16[512,4096]{1,0:T(8,128)(2,1)} %x_ref.5, ...), custom_call_target="tpu_custom_call" | custom-call | flops 2147483648 | bytes 8388608 | tf_op jit(solution)/shard_map/gradient_terms_x/pallas_call | solution.py:183
  39.6 1.5 %collective-permute-start.4 = (bf16[4,4,2,32,256]{4,3,2,1,0:T(8,128)(2,1)}, bf16[4,4,2,32,256]{4,3,2,1,0:T(8,128)(2,1)S(1)}, u32[]{:S(2)}, u32[]{:S(2)}) collective-permute-start(bf16[4,4,2,32,256]{4,3,2,1,0:T(8,128)(2,1)} %get-tuple-element.32), channel_id=1, source_target_pairs={{0,4},{4,1},{1,5},{5,0},{2,6},{6,3},{3,7},{7,2},{8,12},{12,9},{9,1... | collective-permute-start | bytes 1572872 | tf_op jit(solution)/shard_map/ppermute | solution.py:490
  41.1 2.4 %collective-permute-start.5 = (bf16[4,4,2,32,256]{4,3,2,1,0:T(8,128)(2,1)}, bf16[4,4,2,32,256]{4,3,2,1,0:T(8,128)(2,1)S(1)}, u32[]{:S(2)}, u32[]{:S(2)}) collective-permute-start(bf16[4,4,2,32,256]{4,3,2,1,0:T(8,128)(2,1)} %get-tuple-element.33), channel_id=1, source_target_pairs={{0,1},{4,5},{1,0},{5,4},{2,3},{6,7},{3,2},{7,6},{8,9},{12,13},{9,8... | collective-permute-start | bytes 1572872 | tf_op jit(solution)/shard_map/ppermute | solution.py:490
  43.5 1.2 collective-permute-start.6
  44.7 1.2 collective-permute-start.10
  45.9 2.4 %collective-permute-start.11 = (bf16[4,4,2,32,256]{4,3,2,1,0:T(8,128)(2,1)S(1)}, bf16[4,4,2,32,256]{4,3,2,1,0:T(8,128)(2,1)S(1)}, u32[]{:S(2)}, u32[]{:S(2)}) collective-permute-start(bf16[4,4,2,32,256]{4,3,2,1,0:T(8,128)(2,1)S(1)} %copy-done.12), channel_id=1, source_target_pairs={{0,16},{8,24},{16,0},{24,8},{1,17},{9,25},{17,1},{25,9},{2,18},{10... | collective-permute-start | bytes 1572872 | tf_op jit(solution)/shard_map/ppermute | solution.py:494
  48.3 6.2 %collective-permute-done.4.refs_1_ = bf16[4,4,2,32,256]{4,3,2,1,0:T(8,128)(2,1)S(1)} collective-permute-done((bf16[4,4,2,32,256]{4,3,2,1,0:T(8,128)(2,1)}, bf16[4,4,2,32,256]{4,3,2,1,0:T(8,128)(2,1)S(1)}, u32[]{:S(2)}, u32[]{:S(2)}) %collective-permute-start.4) | collective-permute-done | bytes 524320 | tf_op jit(solution)/shard_map/ppermute | solution.py:490
  54.6 2.5 %collective-permute-start.12 = (bf16[4,4,2,32,256]{4,3,2,1,0:T(8,128)(2,1)S(1)}, bf16[4,4,2,32,256]{4,3,2,1,0:T(8,128)(2,1)S(1)}, u32[]{:S(2)}, u32[]{:S(2)}) collective-permute-start(bf16[4,4,2,32,256]{4,3,2,1,0:T(8,128)(2,1)S(1)} %copy-done.11), channel_id=1, source_target_pairs={{0,24},{8,0},{16,8},{24,16},{1,25},{9,1},{17,9},{25,17},{2,26},{10... | collective-permute-start | bytes 1572872 | tf_op jit(solution)/shard_map/ppermute | solution.py:494
  57.1 9.6 %collective-permute-done.5.refs_2_ = bf16[4,4,2,32,256]{4,3,2,1,0:T(8,128)(2,1)S(1)} collective-permute-done((bf16[4,4,2,32,256]{4,3,2,1,0:T(8,128)(2,1)}, bf16[4,4,2,32,256]{4,3,2,1,0:T(8,128)(2,1)S(1)}, u32[]{:S(2)}, u32[]{:S(2)}) %collective-permute-start.5) | collective-permute-done | bytes 524320 | tf_op jit(solution)/shard_map/ppermute | solution.py:490
  66.7 0.0 collective-permute-done.6.refs_3_
  66.7 1.0 copy-done.4
  67.7 0.3 sums_x.1
  68.0 1.2 collective-permute-start.7
  69.2 2.5 %collective-permute-start.8 = (bf16[4,2,32,256]{3,2,1,0:T(8,128)(2,1)S(1)}, bf16[4,2,32,256]{3,2,1,0:T(8,128)(2,1)S(1)}, u32[]{:S(2)}, u32[]{:S(2)}) collective-permute-start(bf16[4,2,32,256]{3,2,1,0:T(8,128)(2,1)S(1)} %get-tuple-element.37), channel_id=1, source_target_pairs={{0,16},{8,24},{16,0},{24,8},{1,17},{9,25},{17,1},{25,9},{2,18},{10... | collective-permute-start | bytes 393224 | tf_op jit(solution)/shard_map/ppermute | solution.py:494
  71.7 0.0 collective-permute-done.10.refs_1_
  71.7 1.1 collective-permute-start.9
  72.8 0.0 collective-permute-done.11.refs_2_
  72.8 0.0 collective-permute-done.12.refs_3_
  72.8 0.3 sums_y.1
  73.1 1.3 collective-permute-start.13
  74.4 2.8 %collective-permute-start.14 = (bf16[4,2,32,256]{3,2,1,0:T(8,128)(2,1)S(1)}, bf16[4,2,32,256]{3,2,1,0:T(8,128)(2,1)S(1)}, u32[]{:S(2)}, u32[]{:S(2)}) collective-permute-start(bf16[4,2,32,256]{3,2,1,0:T(8,128)(2,1)S(1)} %get-tuple-element.44), channel_id=1, source_target_pairs={{0,1},{4,5},{1,0},{5,4},{2,3},{6,7},{3,2},{7,6},{8,9},{12,13},{9,8... | collective-permute-start | bytes 393224 | tf_op jit(solution)/shard_map/ppermute | solution.py:490
  77.2 0.3 collective-permute-start.15
  77.5 12.4 %all-gather.2.cloned.1.call-done.a_ref = bf16[256,32,256]{2,1,0:T(8,128)(2,1)} async-done(((bf16[32,32,256]{2,1,0:T(8,128)(2,1)}), bf16[256,32,256]{2,1,0:T(8,128)(2,1)}) %all-gather.2.cloned.1.call-update) | async-done | bytes 4194320 | tf_op jit(solution)/shard_map/all_gather | solution.py:520
  89.9 1.0 constant_dynamic-slice_fusion
  90.9 0.7 pack.1.other_ref
  91.5 0.0 copy-start
  91.6 0.7 copy-done
  92.3 0.7 collective-permute-start.16
  93.0 4.4 %all-to-all-start.1 = ((bf16[16,48,256]{2,1,0:T(8,128)(2,1)}), bf16[16,48,256]{2,1,0:T(8,128)(2,1)S(1)}, u32[]{:S(2)}, u32[]{:S(2)}) async-start(bf16[16,48,256]{2,1,0:T(8,128)(2,1)} %copy-done), calls=%async_computation.1 | async-start | bytes 786432 | tf_op jit(solution)/shard_map/all_to_all | solution.py:530
  97.4 8.2 %forward.1 = (bf16[512,512]{1,0:T(8,128)(2,1)}, f32[512,128]{1,0:T(8,128)}) custom-call(s32[3]{0:T(128)} %pad_add_fusion.refs_0_.place_ref, bf16[512,4096]{1,0:T(8,128)(2,1)} %x_ref.5, f32[1,4096]{1,0:T(1,128)} %bitcast.21, f32[512,128]{1,0:T(8,128)} %inverses.1.refs_4_.inv_ref, bf16[512,512]{1,0:T(8,128)(2,1)} %keys_ref.3, bf16[512,512]{1,0:T(8,128)(2,1)} %values_ref.3, ...), custom_call_target="tpu_custom_call" | custom-call | flops 1048576 | bytes 1048576 | tf_op jit(solution)/shard_map/forward/pallas_call | solution.py:362
  105.6 6.3 %all-to-all-done.1.a_ref = bf16[16,48,256]{2,1,0:T(8,128)(2,1)S(1)} async-done(((bf16[16,48,256]{2,1,0:T(8,128)(2,1)}), bf16[16,48,256]{2,1,0:T(8,128)(2,1)S(1)}, u32[]{:S(2)}, u32[]{:S(2)}) %all-to-all-start.1) | async-done | bytes 393248 | tf_op jit(solution)/shard_map/all_to_all | solution.py:530
  112.0 0.7 copy-done.1
  112.7 1.0 copy-done.2
  113.7 0.7 unpack.1
  114.4 6.5 %all-to-all-start.2 = ((f32[16,4,128]{2,1,0:T(4,128)}), f32[16,4,128]{2,1,0:T(4,128)S(1)}, u32[]{:S(2)}, u32[]{:S(2)}) async-start(f32[16,4,128]{2,1,0:T(4,128)} %get-tuple-element.53), calls=%async_computation.2 | async-start | bytes 65536 | tf_op jit(solution)/shard_map/all_to_all | solution.py:539
  121.0 14.7 %backward.1 = (bf16[512,512]{1,0:T(8,128)(2,1)}, bf16[512,512]{1,0:T(8,128)(2,1)}, bf16[512,4096]{1,0:T(8,128)(2,1)}) custom-call(s32[3]{0:T(128)} %pad_add_fusion.refs_0_.place_ref, bf16[512,4096]{1,0:T(8,128)(2,1)} %x_ref.5, f32[1,4096]{1,0:T(1,128)} %bitcast.22, f32[512,128]{1,0:T(8,128)} %inverses.1.refs_4_.inv_ref, bf16[512,512]{1,0:T(8,128)(2,1)} %keys_ref.3, ...), custom_call_target="tpu_custom_call" | custom-call | flops 6442450944 | bytes 18874368 | tf_op jit(solution)/shard_map/backward/pallas_call | solution.py:448
  135.7 0.0 copy-start.10
  135.7 0.6 copy-done.9
  136.3 0.8 reshape.39
  137.2 0.1 mul.23
  137.3 0.6 div.3
  (30 shorter events, 0.1 us)
Async XLA Ops:
  7.2 16.3 %collective-permute-start = (bf16[512,4096]{1,0:T(8,128)(2,1)}, bf16[512,4096]{1,0:T(8,128)(2,1)}, u32[]{:S(2)}, u32[]{:S(2)}) collective-permute-start(bf16[512,4096]{1,0:T(8,128)(2,1)} %x_ref.5), channel_id=1, source_target_pairs={{0,2},{2,0},{1,3},{3,1},{4,6},{6,4},{5,7},{7,5},{8,10},{10,8},{9,1... | collective-permute-start | bytes 12582920 | tf_op jit(solution)/shard_map/ppermute | solution.py:481
  10.5 12.9 %collective-permute-start.2 = (bf16[512,512]{1,0:T(8,128)(2,1)}, bf16[512,512]{1,0:T(8,128)(2,1)S(1)}, u32[]{:S(2)}, u32[]{:S(2)}) collective-permute-start(bf16[512,512]{1,0:T(8,128)(2,1)} %keys_ref.3), channel_id=1, source_target_pairs={{0,2},{2,0},{1,3},{3,1},{4,6},{6,4},{5,7},{7,5},{8,10},{10,8},{9,1... | collective-permute-start | bytes 1572872 | tf_op jit(solution)/shard_map/ppermute | solution.py:481
  10.6 12.8 %collective-permute-start.3 = (bf16[512,512]{1,0:T(8,128)(2,1)}, bf16[512,512]{1,0:T(8,128)(2,1)S(1)}, u32[]{:S(2)}, u32[]{:S(2)}) collective-permute-start(bf16[512,512]{1,0:T(8,128)(2,1)} %values_ref.3), channel_id=1, source_target_pairs={{0,2},{2,0},{1,3},{3,1},{4,6},{6,4},{5,7},{7,5},{8,10},{10,8},{9,1... | collective-permute-start | bytes 1572872 | tf_op jit(solution)/shard_map/ppermute | solution.py:481
  12.6 18.9 %all-to-all-start = ((bf16[32,32,256]{2,1,0:T(8,128)(2,1)}), bf16[32,32,256]{2,1,0:T(8,128)(2,1)S(1)}, u32[]{:S(2)}, u32[]{:S(2)}) async-start(bf16[32,32,256]{2,1,0:T(8,128)(2,1)} %bitcast.6), calls=%async_computation | async-start | bytes 1048576 | tf_op jit(solution)/shard_map/all_to_all | solution.py:510
  18.1 71.8 %all-gather.2.cloned.1.call-start = ((), (), s32[]{:S(2)}) async-start(), calls=%async_computation.3 | async-start | bytes 4718592 | tf_op jit(solution)/shard_map/all_gather | solution.py:520
  21.6 1.8 %collective-permute-start.1 = (f32[512,128]{1,0:T(8,128)}, f32[512,128]{1,0:T(8,128)S(1)}, u32[]{:S(2)}, u32[]{:S(2)}) collective-permute-start(f32[512,128]{1,0:T(8,128)} %inverses.1.refs_4_.inv_ref), channel_id=1, source_target_pairs={{0,2},{2,0},{1,3},{3,1},{4,6},{6,4},{5,7},{7,5},{8,10},{10,8},{9,1... | collective-permute-start | bytes 786440 | tf_op jit(solution)/shard_map/ppermute | solution.py:481
  23.4 0.7 copy-start.8
  23.4 0.9 copy-start.6
  23.4 1.0 copy-start.7
  31.5 0.8 copy-start.5
  32.3 12.4 %copy-start.13 = (bf16[4,4,2,32,256]{4,3,2,1,0:T(8,128)(2,1)S(1)}, bf16[4,4,2,32,256]{4,3,2,1,0:T(8,128)(2,1)}, u32[]{:S(2)}) copy-start(bf16[4,4,2,32,256]{4,3,2,1,0:T(8,128)(2,1)} %get-tuple-element.39) | copy-start | bytes 1572868
  32.3 13.6 %copy-start.12 = (bf16[4,4,2,32,256]{4,3,2,1,0:T(8,128)(2,1)S(1)}, bf16[4,4,2,32,256]{4,3,2,1,0:T(8,128)(2,1)}, u32[]{:S(2)}) copy-start(bf16[4,4,2,32,256]{4,3,2,1,0:T(8,128)(2,1)} %get-tuple-element.40) | copy-start | bytes 1572868
  32.3 22.3 %copy-start.11 = (bf16[4,4,2,32,256]{4,3,2,1,0:T(8,128)(2,1)S(1)}, bf16[4,4,2,32,256]{4,3,2,1,0:T(8,128)(2,1)}, u32[]{:S(2)}) copy-start(bf16[4,4,2,32,256]{4,3,2,1,0:T(8,128)(2,1)} %get-tuple-element.41) | copy-start | bytes 1572868
  32.3 40.5 %copy-start.3 = (bf16[4,4,2,32,256]{4,3,2,1,0:T(8,128)(2,1)S(1)}, bf16[4,4,2,32,256]{4,3,2,1,0:T(8,128)(2,1)}, u32[]{:S(2)}) copy-start(bf16[4,4,2,32,256]{4,3,2,1,0:T(8,128)(2,1)} %get-tuple-element.30.other_ref.refs_0_) | copy-start | bytes 1572868
  39.6 14.9 %collective-permute-start.4 = (bf16[4,4,2,32,256]{4,3,2,1,0:T(8,128)(2,1)}, bf16[4,4,2,32,256]{4,3,2,1,0:T(8,128)(2,1)S(1)}, u32[]{:S(2)}, u32[]{:S(2)}) collective-permute-start(bf16[4,4,2,32,256]{4,3,2,1,0:T(8,128)(2,1)} %get-tuple-element.32), channel_id=1, source_target_pairs={{0,4},{4,1},{1,5},{5,0},{2,6},{6,3},{3,7},{7,2},{8,12},{12,9},{9,1... | collective-permute-start | bytes 1572872 | tf_op jit(solution)/shard_map/ppermute | solution.py:490
  41.1 25.6 %collective-permute-start.5 = (bf16[4,4,2,32,256]{4,3,2,1,0:T(8,128)(2,1)}, bf16[4,4,2,32,256]{4,3,2,1,0:T(8,128)(2,1)S(1)}, u32[]{:S(2)}, u32[]{:S(2)}) collective-permute-start(bf16[4,4,2,32,256]{4,3,2,1,0:T(8,128)(2,1)} %get-tuple-element.33), channel_id=1, source_target_pairs={{0,1},{4,5},{1,0},{5,4},{2,3},{6,7},{3,2},{7,6},{8,9},{12,13},{9,8... | collective-permute-start | bytes 1572872 | tf_op jit(solution)/shard_map/ppermute | solution.py:490
  43.5 23.2 %collective-permute-start.6 = (bf16[4,4,2,32,256]{4,3,2,1,0:T(8,128)(2,1)}, bf16[4,4,2,32,256]{4,3,2,1,0:T(8,128)(2,1)S(1)}, u32[]{:S(2)}, u32[]{:S(2)}) collective-permute-start(bf16[4,4,2,32,256]{4,3,2,1,0:T(8,128)(2,1)} %get-tuple-element.34), channel_id=1, source_target_pairs={{0,5},{4,0},{1,4},{5,1},{2,7},{6,2},{3,6},{7,3},{8,13},{12,8},{9,1... | collective-permute-start | bytes 1572872 | tf_op jit(solution)/shard_map/ppermute | solution.py:490
  44.7 27.0 %collective-permute-start.10 = (bf16[4,4,2,32,256]{4,3,2,1,0:T(8,128)(2,1)S(1)}, bf16[4,4,2,32,256]{4,3,2,1,0:T(8,128)(2,1)S(1)}, u32[]{:S(2)}, u32[]{:S(2)}) collective-permute-start(bf16[4,4,2,32,256]{4,3,2,1,0:T(8,128)(2,1)S(1)} %copy-done.13), channel_id=1, source_target_pairs={{0,8},{8,16},{16,24},{24,0},{1,9},{9,17},{17,25},{25,1},{2,10},{10... | collective-permute-start | bytes 1572872 | tf_op jit(solution)/shard_map/ppermute | solution.py:494
  45.9 26.9 %collective-permute-start.11 = (bf16[4,4,2,32,256]{4,3,2,1,0:T(8,128)(2,1)S(1)}, bf16[4,4,2,32,256]{4,3,2,1,0:T(8,128)(2,1)S(1)}, u32[]{:S(2)}, u32[]{:S(2)}) collective-permute-start(bf16[4,4,2,32,256]{4,3,2,1,0:T(8,128)(2,1)S(1)} %copy-done.12), channel_id=1, source_target_pairs={{0,16},{8,24},{16,0},{24,8},{1,17},{9,25},{17,1},{25,9},{2,18},{10... | collective-permute-start | bytes 1572872 | tf_op jit(solution)/shard_map/ppermute | solution.py:494
  54.6 18.3 %collective-permute-start.12 = (bf16[4,4,2,32,256]{4,3,2,1,0:T(8,128)(2,1)S(1)}, bf16[4,4,2,32,256]{4,3,2,1,0:T(8,128)(2,1)S(1)}, u32[]{:S(2)}, u32[]{:S(2)}) collective-permute-start(bf16[4,4,2,32,256]{4,3,2,1,0:T(8,128)(2,1)S(1)} %copy-done.11), channel_id=1, source_target_pairs={{0,24},{8,0},{16,8},{24,16},{1,25},{9,1},{17,9},{25,17},{2,26},{10... | collective-permute-start | bytes 1572872 | tf_op jit(solution)/shard_map/ppermute | solution.py:494
  66.7 1.0 copy-start.4
  68.0 9.2 %collective-permute-start.7 = (bf16[4,2,32,256]{3,2,1,0:T(8,128)(2,1)S(1)}, bf16[4,2,32,256]{3,2,1,0:T(8,128)(2,1)S(1)}, u32[]{:S(2)}, u32[]{:S(2)}) collective-permute-start(bf16[4,2,32,256]{3,2,1,0:T(8,128)(2,1)S(1)} %get-tuple-element.36), channel_id=1, source_target_pairs={{0,8},{8,16},{16,24},{24,0},{1,9},{9,17},{17,25},{25,1},{2,10},{10... | collective-permute-start | bytes 393224 | tf_op jit(solution)/shard_map/ppermute | solution.py:494
  69.2 21.6 %collective-permute-start.8 = (bf16[4,2,32,256]{3,2,1,0:T(8,128)(2,1)S(1)}, bf16[4,2,32,256]{3,2,1,0:T(8,128)(2,1)S(1)}, u32[]{:S(2)}, u32[]{:S(2)}) collective-permute-start(bf16[4,2,32,256]{3,2,1,0:T(8,128)(2,1)S(1)} %get-tuple-element.37), channel_id=1, source_target_pairs={{0,16},{8,24},{16,0},{24,8},{1,17},{9,25},{17,1},{25,9},{2,18},{10... | collective-permute-start | bytes 393224 | tf_op jit(solution)/shard_map/ppermute | solution.py:494
  71.7 19.2 %collective-permute-start.9 = (bf16[4,2,32,256]{3,2,1,0:T(8,128)(2,1)S(1)}, bf16[4,2,32,256]{3,2,1,0:T(8,128)(2,1)S(1)}, u32[]{:S(2)}, u32[]{:S(2)}) collective-permute-start(bf16[4,2,32,256]{3,2,1,0:T(8,128)(2,1)S(1)} %get-tuple-element.38), channel_id=1, source_target_pairs={{0,24},{8,0},{16,8},{24,16},{1,25},{9,1},{17,9},{25,17},{2,26},{10... | collective-permute-start | bytes 393224 | tf_op jit(solution)/shard_map/ppermute | solution.py:494
  73.1 17.8 %collective-permute-start.13 = (bf16[4,2,32,256]{3,2,1,0:T(8,128)(2,1)S(1)}, bf16[4,2,32,256]{3,2,1,0:T(8,128)(2,1)S(1)}, u32[]{:S(2)}, u32[]{:S(2)}) collective-permute-start(bf16[4,2,32,256]{3,2,1,0:T(8,128)(2,1)S(1)} %get-tuple-element.43), channel_id=1, source_target_pairs={{0,4},{4,1},{1,5},{5,0},{2,6},{6,3},{3,7},{7,2},{8,12},{12,9},{9,1... | collective-permute-start | bytes 393224 | tf_op jit(solution)/shard_map/ppermute | solution.py:490
  74.4 16.4 %collective-permute-start.14 = (bf16[4,2,32,256]{3,2,1,0:T(8,128)(2,1)S(1)}, bf16[4,2,32,256]{3,2,1,0:T(8,128)(2,1)S(1)}, u32[]{:S(2)}, u32[]{:S(2)}) collective-permute-start(bf16[4,2,32,256]{3,2,1,0:T(8,128)(2,1)S(1)} %get-tuple-element.44), channel_id=1, source_target_pairs={{0,1},{4,5},{1,0},{5,4},{2,3},{6,7},{3,2},{7,6},{8,9},{12,13},{9,8... | collective-permute-start | bytes 393224 | tf_op jit(solution)/shard_map/ppermute | solution.py:490
  77.2 13.7 %collective-permute-start.15 = (bf16[4,2,32,256]{3,2,1,0:T(8,128)(2,1)S(1)}, bf16[4,2,32,256]{3,2,1,0:T(8,128)(2,1)S(1)}, u32[]{:S(2)}, u32[]{:S(2)}) collective-permute-start(bf16[4,2,32,256]{3,2,1,0:T(8,128)(2,1)S(1)} %get-tuple-element.45), channel_id=1, source_target_pairs={{0,5},{4,0},{1,4},{5,1},{2,7},{6,2},{3,6},{7,3},{8,13},{12,8},{9,1... | collective-permute-start | bytes 393224 | tf_op jit(solution)/shard_map/ppermute | solution.py:490
  91.5 0.7 copy-start
  92.3 28.6 %collective-permute-start.16 = (bf16[128,2,32,256]{3,2,1,0:T(8,128)(2,1)}, bf16[128,2,32,256]{3,2,1,0:T(8,128)(2,1)}, u32[]{:S(2)}, u32[]{:S(2)}) collective-permute-start(bf16[128,2,32,256]{3,2,1,0:T(8,128)(2,1)} %bitcast.16), channel_id=1, source_target_pairs={{0,2},{2,0},{1,3},{3,1},{4,6},{6,4},{5,7},{7,5},{8,10},{10,8},{9,1... | collective-permute-start | bytes 12582920 | tf_op jit(solution)/shard_map/ppermute | solution.py:481
  93.0 19.0 %all-to-all-start.1 = ((bf16[16,48,256]{2,1,0:T(8,128)(2,1)}), bf16[16,48,256]{2,1,0:T(8,128)(2,1)S(1)}, u32[]{:S(2)}, u32[]{:S(2)}) async-start(bf16[16,48,256]{2,1,0:T(8,128)(2,1)} %copy-done), calls=%async_computation.1 | async-start | bytes 786432 | tf_op jit(solution)/shard_map/all_to_all | solution.py:530
  112.0 0.7 copy-start.1
  112.7 1.0 copy-start.2
  114.4 21.3 %all-to-all-start.2 = ((f32[16,4,128]{2,1,0:T(4,128)}), f32[16,4,128]{2,1,0:T(4,128)S(1)}, u32[]{:S(2)}, u32[]{:S(2)}) async-start(f32[16,4,128]{2,1,0:T(4,128)} %get-tuple-element.53), calls=%async_computation.2 | async-start | bytes 65536 | tf_op jit(solution)/shard_map/all_to_all | solution.py:539
  135.7 1.6 %copy-start.10 = (f32[4096]{0:T(1024)S(1)}, f32[4096]{0:T(1024)}, u32[]{:S(2)}) copy-start(f32[4096]{0:T(1024)} %param.7) | copy-start | bytes 49156
  135.7 0.6 copy-start.9
Sparse Core Ops, SparseCore 0:
  32.4 57.3 all-gather.1

commit v3 on v2

v3 whole, which is shorter than its diff:
```python
import math

import jax
import jax.numpy as jnp
from jax import lax
from jax.experimental import pallas as pl
from jax.experimental.pallas import tpu as pltpu
from jax.sharding import Mesh
from jax.sharding import PartitionSpec as P

Z, Y, XL, CORE, XH = 8, 4, 2, 2, 2
AXES = ("z", "y", "xl", "core", "xh")
PLANE = ("y", "xl", "xh")
ROWS = 512
D = 4096
C = 512
W = D // Z
HALF = C // XH
BLOCK = 32
EPS = 1e-05
BF = jnp.bfloat16
F32 = jnp.float32
VMEM = 60 * 1024 * 1024
SMALL = 8 * 1024 * 1024


def params(limit=VMEM):
    return pltpu.CompilerParams(vmem_limit_bytes=limit)


def tie_kernel(a_ref, other_ref, out_ref):
    del a_ref, other_ref, out_ref


def after(a, other):
    return pl.pallas_call(
        tie_kernel,
        in_specs=[pl.BlockSpec(memory_space=pl.ANY)] * 2,
        out_specs=pl.BlockSpec(memory_space=pl.ANY),
        out_shape=jax.ShapeDtypeStruct(a.shape, a.dtype),
        input_output_aliases={0: 0},
        cost_estimate=pl.CostEstimate(flops=0, bytes_accessed=0, transcendentals=0),
        name="after",
    )(a, other)


def copies(pairs, sems):
    started = []
    for at, (source, target) in enumerate(pairs):
        copy = pltpu.make_async_copy(source, target, sems.at[at])
        copy.start()
        started.append(copy)
    return started


def pick(core, first, second, target, sem):
    @pl.when(core == 0)
    def _():
        pltpu.make_async_copy(first, target, sem).start()

    @pl.when(core != 0)
    def _():
        pltpu.make_async_copy(second, target, sem).start()

    return pltpu.make_async_copy(first, target, sem)


SMEM = pl.BlockSpec(memory_space=pltpu.SMEM)
ANY = pl.BlockSpec(memory_space=pl.ANY)
INNER = pl.BlockSpec(memory_space=pltpu.VMEM)


def cheap():
    return pl.CostEstimate(flops=1 << 20, bytes_accessed=1 << 20, transcendentals=0)


WIDE = 2 * W
STEPS = D // WIDE
GROUPS = Y * XL


def inverse_rows(x_buf, which, inv_buf):
    rows = 64
    for at in range(ROWS // rows):
        part = slice(at * rows, (at + 1) * rows)
        squares = jnp.zeros((rows, 128), F32)
        for j in range(D // 128):
            piece = x_buf[which, part, j * 128 : (j + 1) * 128].astype(F32)
            squares = squares + piece * piece
        mean = jnp.sum(squares, axis=1, keepdims=True) * (1.0 / D)
        inv_buf[which, part, :] = jnp.broadcast_to(lax.rsqrt(mean + EPS), (rows, 128))


def grads_kernel(place_ref, own_ref, other_ref, gain_ref, keys_own_ref, values_own_ref,
                 keys_other_ref, values_other_ref, out_ref, inv_ref,
                 x_buf, d_buf, inv_buf, gain_buf, out_buf, sems, small_sems, out_sems):
    core_at = place_ref[0]
    large = []
    for which, ref in enumerate((own_ref, other_ref)):
        rows = [pl.ds(i * (ROWS // 8), ROWS // 8) for i in range(8)]
        large.append(
            copies([(ref.at[part], x_buf.at[which, part]) for part in rows], sems.at[which])
        )
    small = copies([(gain_ref, gain_buf)], small_sems)
    small.append(pick(core_at, keys_own_ref, values_own_ref, d_buf.at[0], small_sems.at[1]))
    small.append(pick(core_at, keys_other_ref, values_other_ref, d_buf.at[1], small_sems.at[2]))
    for which in range(2):
        for copy in large[which]:
            copy.wait()
        inverse_rows(x_buf, which, inv_buf)
    for copy in small:
        copy.wait()
    sent = [pltpu.make_async_copy(inv_buf.at[0], inv_ref, small_sems.at[3])]
    sent[0].start()
    for part in range(STEPS):
        lanes = slice(part * WIDE, (part + 1) * WIDE)
        total = None
        for which in range(2):
            normal = x_buf[which, :, lanes].astype(F32) * inv_buf[which, :, :1]
            hidden = (normal * gain_buf[:, lanes]).astype(BF)
            term = lax.dot_general(
                hidden, d_buf[which], (((0,), (0,)), ((), ())), preferred_element_type=F32
            )
            total = term if total is None else total + term
        total = total.astype(BF)
        for z in range(WIDE // W):
            for group in range(GROUPS):
                for half in range(XH):
                    for core in range(CORE):
                        first = z * W + (group * CORE + core) * BLOCK
                        out_buf[group * XH + half, part * (WIDE // W) + z, core] = total[
                            first : first + BLOCK, half * HALF : (half + 1) * HALF
                        ]
        zs = pl.ds(part * (WIDE // W), WIDE // W)
        for piece in range(4):
            places = pl.ds(piece * GROUPS * XH // 4, GROUPS * XH // 4)
            copy = pltpu.make_async_copy(
                out_buf.at[places, zs], out_ref.at[places, zs], out_sems.at[part, piece]
            )
            copy.start()
            sent.append(copy)
    for copy in sent:
        copy.wait()


def gradient_terms(*inputs):
    shape = (GROUPS * XH, Z, CORE, BLOCK, HALF)
    return pl.pallas_call(
        grads_kernel,
        in_specs=[SMEM] + [ANY] * 7,
        out_specs=[ANY] * 2,
        out_shape=[
            jax.ShapeDtypeStruct(shape, BF),
            jax.ShapeDtypeStruct((ROWS, 128), F32),
        ],
        scratch_shapes=[
            pltpu.VMEM((2, ROWS, D), BF),
            pltpu.VMEM((2, ROWS, C), BF),
            pltpu.VMEM((2, ROWS, 128), F32),
            pltpu.VMEM((1, D), F32),
            pltpu.VMEM(shape, BF),
            pltpu.SemaphoreType.DMA((2, 8)),
            pltpu.SemaphoreType.DMA((4,)),
            pltpu.SemaphoreType.DMA((STEPS, 4)),
        ],
        compiler_params=params(),
        cost_estimate=cheap(),
        name="gradient_terms",
    )(*inputs)


RING = [(r, 0, GROUPS) for r in range(Z) if r != 4]
RING[4:4] = [(4, 0, GROUPS // 2), (4, GROUPS // 2, GROUPS // 2)]


EXTRA = 16


def pack_kernel(place_ref, in_ref, *refs):
    w_refs = refs[: len(RING)]
    out_ref, prod_ref, w_buf, in_buf, sems, in_sems = refs[len(RING) :]
    group, half = place_ref[2], place_ref[3]
    terms = copies([(in_ref.at[:, z], in_buf.at[:, z]) for z in range(Z)], in_sems)
    waits = []
    for (distance, first, groups), ref in zip(RING, w_refs):
        z = lax.rem(place_ref[1] + Z - distance, Z)
        inside = lax.rem(group, groups)
        copy = pltpu.make_async_copy(
            ref.at[inside, :, half], w_buf.at[pl.ds(z * CORE, CORE)], sems.at[distance]
        )
        if groups == GROUPS:
            copy.start()
        else:
            pl.when(lax.div(group, groups) == first // groups)(copy.start)
        if first == 0:
            waits.append(copy)
    for z in range(Z):
        terms[z].wait()
        for core in range(CORE):
            at = z * CORE + core
            total = in_buf[0, z, core].astype(F32)
            for source in range(1, GROUPS * XH):
                total = total + in_buf[source, z, core].astype(F32)
            out_ref[at, :BLOCK] = total.astype(BF)
            prod_ref[at * BLOCK : (at + 1) * BLOCK] = total
    for copy in waits:
        copy.wait()
    for at in range(Z * CORE):
        rows = slice(at * BLOCK, (at + 1) * BLOCK)
        prod_ref[rows] = prod_ref[rows] * w_buf[at].astype(F32)
    gains = lax.dot_general(
        jnp.ones((8, HALF), F32),
        prod_ref[...],
        (((1,), (1,)), ((), ())),
        precision=lax.Precision.HIGHEST,
        preferred_element_type=F32,
    )[:1]
    upper = gains.astype(BF).astype(F32)
    lower = gains - upper
    row = lax.broadcasted_iota(jnp.int32, (EXTRA, HALF), 0)
    extra = jnp.zeros((EXTRA, HALF), F32)
    for at, line in enumerate(
        (upper[:, :HALF], upper[:, HALF:], lower[:, :HALF], lower[:, HALF:])
    ):
        extra = jnp.where(row == at, jnp.broadcast_to(line, (EXTRA, HALF)), extra)
    extra = extra.astype(BF)
    for at in range(Z * CORE):
        out_ref[at, BLOCK:] = extra


def pack(place, terms, blocks):
    return pl.pallas_call(
        pack_kernel,
        in_specs=[SMEM] + [ANY] * (1 + len(RING)),
        out_specs=INNER,
        out_shape=jax.ShapeDtypeStruct((Z * CORE, BLOCK + EXTRA, HALF), BF),
        scratch_shapes=[
            pltpu.VMEM((Z * CORE * BLOCK, HALF), F32),
            pltpu.VMEM((Z * CORE, BLOCK, HALF), BF),
            pltpu.VMEM(terms.shape, BF),
            pltpu.SemaphoreType.DMA((Z,)),
            pltpu.SemaphoreType.DMA((Z,)),
        ],
        compiler_params=params(),
        cost_estimate=cheap(),
        name="pack",
    )(place, terms, *blocks)


def unpack_kernel(scale, in_ref, key_ref, value_ref, gains_ref):
    for which, ref in enumerate((key_ref, value_ref)):
        total = in_ref[which, :BLOCK].astype(F32)
        for z in range(1, Z):
            total = total + in_ref[z * 2 + which, :BLOCK].astype(F32)
        ref[...] = total * scale
    extra = in_ref[0, BLOCK:].astype(F32)
    for at in range(1, Z * CORE):
        extra = extra + in_ref[at, BLOCK:].astype(F32)
    for line in range(2):
        gains = extra[line : line + 1] + extra[line + 2 : line + 3]
        for piece in range(2):
            lanes = gains[:, piece * 128 : (piece + 1) * 128]
            for at in range(Y * XL * XH):
                gains_ref[at, line * 2 + piece : line * 2 + piece + 1] = lanes


def unpack(scale, received):
    def kernel(*refs):
        unpack_kernel(scale, *refs)

    return pl.pallas_call(
        kernel,
        in_specs=[INNER],
        out_specs=[INNER] * 3,
        out_shape=[
            jax.ShapeDtypeStruct((BLOCK, HALF), F32),
            jax.ShapeDtypeStruct((BLOCK, HALF), F32),
            jax.ShapeDtypeStruct((Y * XL * XH, 4, 128), F32),
        ],
        compiler_params=params(SMALL),
        cost_estimate=cheap(),
        name="unpack",
    )(received)


def weight_rows(buf, part):
    rows = WIDE // BLOCK
    ref = buf.at[pl.ds(part * rows, rows)]
    return jnp.concatenate([ref[:, half].reshape(WIDE, HALF) for half in range(XH)], axis=1)


def rows_kernel(place_ref, x_ref, gain_ref, inv_ref, keys_ref, values_ref, *rest):
    mine, theirs = rest[: len(RING)], rest[len(RING) : 2 * len(RING)]
    (out_keys_ref, out_values_ref, dx_ref, x_buf, w_buf, d_buf, inv_buf, gain_buf, out_buf, dx_buf,
     sems, small_sems, out_sems, dx_sems) = rest[2 * len(RING) :]
    core = place_ref[0]
    rows = W // BLOCK

    def columns(at):
        z = lax.rem(place_ref[1] + Z - at, Z)
        return pl.ds(pl.multiple_of(z * W, W), W)

    def fetch(part):
        pairs = []
        for at in range(part * WIDE // W, (part + 1) * WIDE // W):
            lanes = pl.ds(at * W, W)
            pairs.append((x_ref.at[:, columns(at)], x_buf.at[:, lanes]))
            pairs.append((gain_ref.at[:, columns(at)], gain_buf.at[:, lanes]))
            for which, refs in enumerate((mine, theirs)):
                for (distance, first, groups), ref in zip(RING, refs):
                    if distance == at:
                        block = pl.ds(at * rows + first * CORE, groups * CORE)
                        pairs.append((ref, w_buf.at[which, block]))
        return copies(pairs, sems.at[part])

    large = [fetch(0)]
    small = copies([(inv_ref, inv_buf)], small_sems)
    small.append(pick(core, keys_ref, values_ref, d_buf.at[0], small_sems.at[1]))
    small.append(pick(core, values_ref, keys_ref, d_buf.at[1], small_sems.at[2]))
    large.append(fetch(1))
    small[0].wait()
    totals = [None, None]
    for part in range(STEPS):
        for copy in large[part]:
            copy.wait()
        if part + 2 < STEPS:
            large.append(fetch(part + 2))
        lanes = slice(part * WIDE, (part + 1) * WIDE)
        normal = x_buf[:, lanes].astype(F32) * inv_buf[:, :1]
        hidden = (normal * gain_buf[:, lanes]).astype(BF)
        for which in range(2):
            weights = weight_rows(w_buf.at[which], part)
            term = jnp.dot(hidden, weights, preferred_element_type=F32)
            totals[which] = term if totals[which] is None else totals[which] + term
    for copy in small[1:]:
        copy.wait()
    sent = []
    along = None
    for which in range(2):
        out_buf[which] = totals[which].astype(BF)
        refs = (out_keys_ref, out_values_ref) if which == 0 else (out_values_ref, out_keys_ref)

        @pl.when(core == 0)
        def _():
            pltpu.make_async_copy(out_buf.at[which], refs[0], out_sems.at[which]).start()

        @pl.when(core != 0)
        def _():
            pltpu.make_async_copy(out_buf.at[which], refs[1], out_sems.at[which]).start()

        sent.append(pltpu.make_async_copy(out_buf.at[which], refs[0], out_sems.at[which]))
        term = jnp.sum(totals[which] * d_buf[which].astype(F32), axis=1, keepdims=True)
        along = term if along is None else along + term
    along = along * (1.0 / D)
    inverse = inv_buf[:, :1]
    for part in range(STEPS):
        lanes = slice(part * WIDE, (part + 1) * WIDE)
        d_hidden = None
        for which in range(2):
            term = lax.dot_general(
                d_buf[which],
                weight_rows(w_buf.at[which], part),
                (((1,), (1,)), ((), ())),
                preferred_element_type=F32,
            )
            d_hidden = term if d_hidden is None else d_hidden + term
        normal = x_buf[:, lanes].astype(F32) * inverse
        dx_buf[:, lanes] = (inverse * (d_hidden * gain_buf[:, lanes] - normal * along)).astype(BF)
        for piece in range(WIDE // W):
            at = part * (WIDE // W) + piece
            copy = pltpu.make_async_copy(
                dx_buf.at[:, pl.ds(at * W, W)], dx_ref.at[:, columns(at)], dx_sems.at[part, piece]
            )
            copy.start()
            sent.append(copy)
    for copy in sent:
        copy.wait()


def rows_pass(*inputs):
    return pl.pallas_call(
        rows_kernel,
        in_specs=[SMEM] + [ANY] * (5 + 2 * len(RING)),
        out_specs=[ANY] * 3,
        out_shape=[
            jax.ShapeDtypeStruct((ROWS, C), BF),
            jax.ShapeDtypeStruct((ROWS, C), BF),
            jax.ShapeDtypeStruct((ROWS, D), BF),
        ],
        scratch_shapes=[
            pltpu.VMEM((ROWS, D), BF),
            pltpu.VMEM((2, D // BLOCK, XH, BLOCK, HALF), BF),
            pltpu.VMEM((2, ROWS, C), BF),
            pltpu.VMEM((ROWS, 128), F32),
            pltpu.VMEM((1, D), F32),
            pltpu.VMEM((2, ROWS, C), BF),
            pltpu.VMEM((ROWS, D), BF),
            pltpu.SemaphoreType.DMA((STEPS, 10)),
            pltpu.SemaphoreType.DMA((3,)),
            pltpu.SemaphoreType.DMA((2,)),
            pltpu.SemaphoreType.DMA((STEPS, WIDE // W)),
        ],
        compiler_params=params(),
        cost_estimate=pl.CostEstimate(
            flops=8 * ROWS * D * C, bytes_accessed=18 << 20, transcendentals=0
        ),
        name="rows_pass",
    )(*inputs)


def finish_kernel(scale, in_ref, gain_ref, out_ref):
    sums_of = [in_ref[at * XH] + in_ref[at * XH + 1] for at in range(Y * XL)]
    for z in range(Z):
        line, lanes = z // 2, slice(z % 2 * 64, z % 2 * 64 + 64)
        for at in range(0, Y * XL, 2):
            first, second = (sums_of[at + i][line : line + 1, lanes] for i in range(2))
            tile = jnp.concatenate([first, second], axis=1) * scale
            span = slice(z * W + at * 64, z * W + at * 64 + 128)
            out_ref[:, span] = tile / gain_ref[:, span]


def finish(scale, gains, gain):
    def kernel(*refs):
        finish_kernel(scale, *refs)

    return pl.pallas_call(
        kernel,
        in_specs=[INNER] * 2,
        out_specs=INNER,
        out_shape=jax.ShapeDtypeStruct((1, D), F32),
        compiler_params=params(SMALL),
        cost_estimate=cheap(),
        name="finish",
    )(gains, gain)


def swap(a):
    return lax.ppermute(a, "core", [(0, 1), (1, 0)])


def along_z(a, step):
    return lax.ppermute(a, "z", [(i, (i + step) % Z) for i in range(Z)])


def around(own):
    up, down = [own], [own]
    for _ in range(3):
        up.append(along_z(up[-1], 1))
        down.append(along_z(down[-1], -1))
    last = [along_z(up[3][: GROUPS // 2], 1), along_z(down[3][GROUPS // 2 :], -1)]
    return up + last + down[:0:-1]


def shards(tokens, gain, w_key, w_value, d_keys, d_values):
    scale = 1.0 / math.sqrt(ROWS * Z * Y * XL * CORE * XH)
    y_at, low, high = lax.axis_index("y"), lax.axis_index("xl"), lax.axis_index("xh")
    core, z_at = lax.axis_index("core"), lax.axis_index("z")
    place = jnp.stack([core, z_at, y_at * XL + low, high]).astype(jnp.int32)
    row_gain = gain.reshape(1, D)

    pair = jnp.stack([w_key, w_value])
    sent = jnp.broadcast_to(pair[None, :, None], (Y * XL, CORE, XH, BLOCK, HALF))
    plane = lax.all_to_all(
        sent.reshape(Y * XL * CORE * XH, BLOCK, HALF), ("y", "xl", "core", "xh"), 0, 0, tiled=True
    )

    inputs = (place, tokens, swap(tokens), row_gain, d_keys, d_values, swap(d_keys), swap(d_values))
    terms, inv = gradient_terms(*inputs)
    plane = after(plane, inv).reshape(GROUPS, CORE, XH, BLOCK, HALF)
    mine = around(plane)
    theirs = [swap(block) for block in mine]

    sent = pack(place, lax.all_to_all(terms, PLANE, 0, 0, tiled=True), mine)
    received = lax.all_to_all(sent, ("z", "core"), 0, 0, tiled=True)

    flat = [block.reshape(-1, XH, BLOCK, HALF) for block in mine + theirs]
    keys, values, d_tokens = rows_pass(place, tokens, row_gain, inv, d_keys, d_values, *flat)
    grad_key, grad_value, gains = unpack(scale, after(received, d_tokens))
    gains = lax.all_to_all(gains, PLANE, 0, 0, tiled=True)
    grad_gain = finish(scale, gains, row_gain).reshape(D)
    return (keys, values, d_tokens, grad_key, grad_value, grad_gain)


def solution(mesh):
    fine = Mesh(mesh.devices.reshape(Z, Y, XL, CORE, XH), AXES)
    loop = ("z", "y", "xl", "core")
    return jax.shard_map(
        shards,
        mesh=fine,
        in_specs=(
            P(AXES, None),
            P(),
            P(loop, "xh"),
            P(loop, "xh"),
            P(AXES, None),
            P(AXES, None),
        ),
        out_specs=(
            P(AXES, None),
            P(AXES, None),
            P(AXES, None),
            P(loop, "xh"),
            P(loop, "xh"),
            P(),
        ),
        check_vma=False,
    )
```

time: 145 us -> 135 us (0.931)
  blocking collectives: 0 us -> 13.6 us
  between operations: 14.3 us -> 0.89 us
  Pallas kernels: 42.5 us -> 33.1 us
  starting transfers between devices: 41.7 us -> 47.9 us
  local copies, waits for them, and re-layouts: 8.71 us -> 4.06 us
  waiting for transfers between devices: 35.5 us -> 33.4 us
    ppermute x12 -> x8, waiting for transfers between devices: 15.9 us -> 33 us  [along_z(): return lax.ppermute(a, 'z', [(i, (i + step) % Z) for i in range(Z)])]
    all_to_all x0 -> x1, blocking collectives: none -> 13.6 us  [shards(): gains = lax.all_to_all(gains, PLANE, 0, 0, tiled=True)]
    all_gather x1 -> x0, waiting for transfers between devices: 12.4 us -> none  [shards(): mine = lax.all_gather(plane, 'z', axis=0, tiled=True)]
    ppermute x5 -> x12, starting transfers between devices: 4.84 us -> 16.8 us  [swap(): return lax.ppermute(a, 'core', [(0, 1), (1, 0)])]
    pallas_call x8 -> x4, Pallas kernels: 41.8 us -> 32.5 us  [the longest x1 15.4 us: rows_pass(): pl.pallas_call(rows_kernel, in_specs=[SMEM] + [ANY] * (5 + 2 * len(RING))...]
    ppermute x12 -> x8, starting transfers between devices: 20.4 us -> 13.8 us  [along_z(): return lax.ppermute(a, 'z', [(i, (i + step) % Z) for i in range(Z)])]
    all_to_all x1, waiting for transfers between devices: 6.34 us -> 0.01 us  [shards(): received = lax.all_to_all(sent, ('z', 'core'), 0, 0, tiled=True)]
    unnamed x28 -> x32, local copies, waits for them, and re-layouts: 5.96 us -> 3.17 us
  transfers between devices with their start and end apart: 21 -> 23, of which waited for: 5 -> 7; matrix products, arithmetic and copies ran while one was open for 2% -> 2% of each run, Pallas kernels for 29% -> 24%
where the time goes in v3:
time: 135 us; the launch traced here: 134 us
  starting transfers between devices  47.9 us (35%)
  waiting for transfers between devices  33.4 us (25%)
  Pallas kernels  33.1 us (25%)
  blocking collectives  13.6 us (10%)
  local copies, waits for them, and re-layouts  4.06 us (3%)
  other arithmetic  1.39 us (1%)
    ppermute x8, waiting for transfers between devices, along_z(): return lax.ppermute(a, 'z', [(i, (i + step) % Z) for i in range(Z)])  33 us
    ppermute x12, starting transfers between devices, swap(): return lax.ppermute(a, 'core', [(0, 1), (1, 0)])  16.8 us
    pallas_call x1, Pallas kernels, rows_pass(): pl.pallas_call(rows_kernel, in_specs=[SMEM] + [ANY] * (5 + 2 * len(RING))...  15.4 us
    ppermute x8, starting transfers between devices, along_z(): return lax.ppermute(a, 'z', [(i, (i + step) % Z) for i in range(Z)])  13.8 us
    all_to_all x1, blocking collectives, shards(): gains = lax.all_to_all(gains, PLANE, 0, 0, tiled=True)  13.6 us
    pallas_call x1, Pallas kernels, gradient_terms(): pl.pallas_call(grads_kernel, in_specs=[SMEM] + [ANY] * 7, out_specs=[ANY]...  11.9 us
    all_to_all x1, starting transfers between devices, shards(): sent = pack(place, lax.all_to_all(terms, PLANE, 0, 0, tiled=True), mine)  6.72 us
    all_to_all x1, starting transfers between devices, shards(): lax.all_to_all(sent.reshape(Y * XL * CORE * XH, BLOCK, HALF), ('y', 'xl',...  5.49 us
  transfers between devices with their start and end apart: 23, of which 7 were waited for; matrix products, arithmetic and copies ran while one was open for 2% of the time, Pallas kernels for 24%

profile of v3, /device:TPU:1, one launch (start us, length us, event | category | flops | bytes accessed | tf_op | source)
XLA Modules:
  0.0 134.3 jit_solution(4743941027597830792)
XLA Ops:
  0.6 3.3 %collective-permute-start = (bf16[512,4096]{1,0:T(8,128)(2,1)}, bf16[512,4096]{1,0:T(8,128)(2,1)}, u32[]{:S(2)}, u32[]{:S(2)}) collective-permute-start(bf16[512,4096]{1,0:T(8,128)(2,1)} %x_ref.1), channel_id=1, source_target_pairs={{0,2},{2,0},{1,3},{3,1},{4,6},{6,4},{5,7},{7,5},{8,10},{10,8},{9,1... | collective-permute-start | bytes 12582920 | tf_op jit(solution)/shard_map/ppermute | solution.py:438
  4.0 0.1 collective-permute-start.1
  4.1 0.4 collective-permute-start.2
  4.5 0.7 pad_maximum_fusion
  5.2 0.9 broadcast_in_dim.2
  6.1 5.5 %all-to-all-start = ((bf16[32,32,256]{2,1,0:T(8,128)(2,1)}), bf16[32,32,256]{2,1,0:T(8,128)(2,1)S(1)}, u32[]{:S(2)}, u32[]{:S(2)}) async-start(bf16[32,32,256]{2,1,0:T(8,128)(2,1)} %bitcast.7), calls=%async_computation | async-start | bytes 1048576 | tf_op jit(solution)/shard_map/all_to_all | solution.py:463
  11.6 0.7 pad_add_fusion.place_ref
  12.2 0.0 collective-permute-done.1.keys_other_ref
  12.2 0.1 collective-permute-done.2.values_other_ref
  12.3 0.3 collective-permute-done.other_ref
  12.6 0.4 copy-done.10
  13.0 0.2 copy-done.11
  13.2 11.9 %gradient_terms.1 = (bf16[16,8,2,32,256]{4,3,2,1,0:T(8,128)(2,1)}, f32[512,128]{1,0:T(8,128)}) custom-call(s32[4]{0:T(128)} %pad_add_fusion.place_ref, bf16[512,4096]{1,0:T(8,128)(2,1)} %x_ref.1, bf16[512,4096]{1,0:T(8,128)(2,1)} %collective-permute-done.other_ref, f32[1,4096]{1,0:T(1,128)} %bitcast.28, bf16[512,512]{1,0:T(8,128)(2,1)} %keys_ref.1, ...), custom_call_target="tpu_custom_call" | custom-call | flops 1048576 | bytes 1048576 | tf_op jit(solution)/shard_map/gradient_terms/pallas_call | solution.py:148
  25.1 0.0 all-to-all-done.a_ref
  25.1 0.0 copy-start.3
  25.1 0.8 copy-done.3
  25.9 6.7 %all-to-all-start.1 = ((bf16[16,8,2,32,256]{4,3,2,1,0:T(8,128)(2,1)}), bf16[16,8,2,32,256]{4,3,2,1,0:T(8,128)(2,1)}, u32[]{:S(2)}, u32[]{:S(2)}) async-start(bf16[16,8,2,32,256]{4,3,2,1,0:T(8,128)(2,1)} %get-tuple-element.18), calls=%async_computation.1 | async-start | bytes 8388608 | tf_op jit(solution)/shard_map/all_to_all | solution.py:473
  32.6 5.7 %collective-permute-start.7 = (bf16[8,2,2,32,256]{4,3,2,1,0:T(8,128)(2,1)}, bf16[8,2,2,32,256]{4,3,2,1,0:T(8,128)(2,1)S(1)}, u32[]{:S(2)}, u32[]{:S(2)}) collective-permute-start(bf16[8,2,2,32,256]{4,3,2,1,0:T(8,128)(2,1)} %bitcast.31), channel_id=1, source_target_pairs={{0,224},{32,0},{64,32},{96,64},{128,96},{160,128},{192,160},{224,1... | collective-permute-start | bytes 1572872 | tf_op jit(solution)/shard_map/ppermute | solution.py:442
  38.3 0.0 collective-permute-start.3
  38.3 10.8 %collective-permute-done.7.refs_8_ = bf16[8,2,2,32,256]{4,3,2,1,0:T(8,128)(2,1)S(1)} collective-permute-done((bf16[8,2,2,32,256]{4,3,2,1,0:T(8,128)(2,1)}, bf16[8,2,2,32,256]{4,3,2,1,0:T(8,128)(2,1)S(1)}, u32[]{:S(2)}, u32[]{:S(2)}) %collective-permute-start.7) | collective-permute-done | bytes 524320 | tf_op jit(solution)/shard_map/ppermute | solution.py:442
  49.0 3.4 %collective-permute-start.8 = (bf16[8,2,2,32,256]{4,3,2,1,0:T(8,128)(2,1)S(1)}, bf16[8,2,2,32,256]{4,3,2,1,0:T(8,128)(2,1)S(1)}, u32[]{:S(2)}, u32[]{:S(2)}) collective-permute-start(bf16[8,2,2,32,256]{4,3,2,1,0:T(8,128)(2,1)S(1)} %collective-permute-done.7.refs_8_), channel_id=1, source_target_pairs={{0,224},{32,0},{64,32},{96,64},{128,96},{160,128},{192,160},{224,1... | collective-permute-start | bytes 1572872 | tf_op jit(solution)/shard_map/ppermute | solution.py:442
  52.4 0.0 collective-permute-done.3.refs_1_
  52.4 0.0 collective-permute-start.4
  52.5 9.6 %collective-permute-done.8.refs_7_ = bf16[8,2,2,32,256]{4,3,2,1,0:T(8,128)(2,1)S(1)} collective-permute-done((bf16[8,2,2,32,256]{4,3,2,1,0:T(8,128)(2,1)S(1)}, bf16[8,2,2,32,256]{4,3,2,1,0:T(8,128)(2,1)S(1)}, u32[]{:S(2)}, u32[]{:S(2)}) %collective-permute-start.8) | collective-permute-done | bytes 524320 | tf_op jit(solution)/shard_map/ppermute | solution.py:442
  62.1 3.5 %collective-permute-start.9 = (bf16[8,2,2,32,256]{4,3,2,1,0:T(8,128)(2,1)S(1)}, bf16[8,2,2,32,256]{4,3,2,1,0:T(8,128)(2,1)S(1)}, u32[]{:S(2)}, u32[]{:S(2)}) collective-permute-start(bf16[8,2,2,32,256]{4,3,2,1,0:T(8,128)(2,1)S(1)} %collective-permute-done.8.refs_7_), channel_id=1, source_target_pairs={{0,224},{32,0},{64,32},{96,64},{128,96},{160,128},{192,160},{224,1... | collective-permute-start | bytes 1572872 | tf_op jit(solution)/shard_map/ppermute | solution.py:442
  65.6 0.0 collective-permute-done.4.refs_2_
  65.6 0.0 collective-permute-start.5
  65.6 2.8 %collective-permute-start.11 = (bf16[8,2,2,32,256]{4,3,2,1,0:T(8,128)(2,1)}, bf16[8,2,2,32,256]{4,3,2,1,0:T(8,128)(2,1)S(1)}, u32[]{:S(2)}, u32[]{:S(2)}) collective-permute-start(bf16[8,2,2,32,256]{4,3,2,1,0:T(8,128)(2,1)} %bitcast.33), channel_id=1, source_target_pairs={{0,2},{2,0},{1,3},{3,1},{4,6},{6,4},{5,7},{7,5},{8,10},{10,8},{9,1... | collective-permute-start | bytes 1572872 | tf_op jit(solution)/shard_map/ppermute | solution.py:438
  68.4 0.1 collective-permute-start.19
  68.5 0.4 collective-permute-start.12
  68.9 5.5 %collective-permute-done.9.refs_6_ = bf16[8,2,2,32,256]{4,3,2,1,0:T(8,128)(2,1)S(1)} collective-permute-done((bf16[8,2,2,32,256]{4,3,2,1,0:T(8,128)(2,1)S(1)}, bf16[8,2,2,32,256]{4,3,2,1,0:T(8,128)(2,1)S(1)}, u32[]{:S(2)}, u32[]{:S(2)}) %collective-permute-start.9) | collective-permute-done | bytes 524320 | tf_op jit(solution)/shard_map/ppermute | solution.py:442
  74.4 3.3 %collective-permute-start.18 = (bf16[8,2,2,32,256]{4,3,2,1,0:T(8,128)(2,1)S(1)}, bf16[8,2,2,32,256]{4,3,2,1,0:T(8,128)(2,1)S(1)}, u32[]{:S(2)}, u32[]{:S(2)}) collective-permute-start(bf16[8,2,2,32,256]{4,3,2,1,0:T(8,128)(2,1)S(1)} %collective-permute-done.8.refs_7_), channel_id=1, source_target_pairs={{0,2},{2,0},{1,3},{3,1},{4,6},{6,4},{5,7},{7,5},{8,10},{10,8},{9,1... | collective-permute-start | bytes 1572872 | tf_op jit(solution)/shard_map/ppermute | solution.py:438
  77.8 0.0 collective-permute-done.5.refs_3_
  77.8 0.0 copy-start.5
  77.8 3.4 %collective-permute-start.13 = (bf16[8,2,2,32,256]{4,3,2,1,0:T(8,128)(2,1)S(1)}, bf16[8,2,2,32,256]{4,3,2,1,0:T(8,128)(2,1)}, u32[]{:S(2)}, u32[]{:S(2)}) collective-permute-start(bf16[8,2,2,32,256]{4,3,2,1,0:T(8,128)(2,1)S(1)} %collective-permute-done.4.refs_2_), channel_id=1, source_target_pairs={{0,2},{2,0},{1,3},{3,1},{4,6},{6,4},{5,7},{7,5},{8,10},{10,8},{9,1... | collective-permute-start | bytes 1572872 | tf_op jit(solution)/shard_map/ppermute | solution.py:438
  81.2 0.0 collective-permute-done.11
  81.2 0.2 collective-permute-start.10
  81.4 0.0 collective-permute-done.19
  81.4 0.8 collective-permute-start.17
  82.2 0.0 collective-permute-done.12
  82.2 0.1 collective-permute-start.14
  82.3 0.0 collective-permute-done.18
  82.3 1.0 collective-permute-start.6
  83.3 6.0 %collective-permute-done.10.refs_5_ = bf16[4,2,2,32,256]{4,3,2,1,0:T(8,128)(2,1)} collective-permute-done((bf16[4,2,2,32,256]{4,3,2,1,0:T(8,128)(2,1)S(1)}, bf16[4,2,2,32,256]{4,3,2,1,0:T(8,128)(2,1)}, u32[]{:S(2)}, u32[]{:S(2)}) %collective-permute-start.10) | collective-permute-done | bytes 262176 | tf_op jit(solution)/shard_map/ppermute | solution.py:442
  89.3 0.8 collective-permute-start.16
  90.1 1.0 collective-permute-done.6.refs_4_
  91.1 0.0 copy-done.15
  91.1 1.3 collective-permute-start.15
  92.5 0.0 all-to-all-done.1.in_ref
  92.5 4.5 %pack.1 = bf16[16,48,256]{2,1,0:T(8,128)(2,1)} custom-call(s32[4]{0:T(128)} %pad_add_fusion.place_ref, bf16[16,8,2,32,256]{4,3,2,1,0:T(8,128)(2,1)} %all-to-all-done.1.in_ref, bf16[8,2,2,32,256]{4,3,2,1,0:T(8,128)(2,1)} %bitcast.34, bf16[8,2,2,32,256]{4,3,2,1,0:T(8,128)(2,1)} %copy-done.7, bf16[8,2,2,32,256]{4,3,2,1,0:T(8,128)(2,1)} %copy-done.9, ...), custom_call_target="tpu_custom_call" | custom-call | flops 1048576 | bytes 1048576 | tf_op jit(solution)/shard_map/pack/pallas_call | solution.py:232
  97.0 5.1 %all-to-all-start.2 = ((bf16[16,48,256]{2,1,0:T(8,128)(2,1)}), bf16[16,48,256]{2,1,0:T(8,128)(2,1)S(1)}, u32[]{:S(2)}, u32[]{:S(2)}) async-start(bf16[16,48,256]{2,1,0:T(8,128)(2,1)} %pack.1), calls=%async_computation.2 | async-start | bytes 786432 | tf_op jit(solution)/shard_map/all_to_all | solution.py:474
  102.1 0.0 collective-permute-done.13
  102.1 0.0 collective-permute-done.17
  102.1 0.0 collective-permute-done.14
  102.1 0.0 collective-permute-done.16
  102.1 0.0 collective-permute-done.15
  102.1 15.4 %rows_pass.1 = (bf16[512,512]{1,0:T(8,128)(2,1)}, bf16[512,512]{1,0:T(8,128)(2,1)}, bf16[512,4096]{1,0:T(8,128)(2,1)}) custom-call(s32[4]{0:T(128)} %pad_add_fusion.place_ref, bf16[512,4096]{1,0:T(8,128)(2,1)} %x_ref.1, f32[1,4096]{1,0:T(1,128)} %bitcast.29, f32[512,128]{1,0:T(8,128)} %get-tuple-element.14.other_ref.inv_ref, bf16[512,512]{1,0:T(8,128)(2,1)} %keys_ref.1, ...), custom_call_target="tpu_custom_call" | custom-call | flops 8589934592 | bytes 18874368 | tf_op jit(solution)/shard_map/rows_pass/pallas_call | solution.py:381
  117.6 0.0 copy-start.2
  117.6 0.0 all-to-all-done.2.a_ref
  117.6 0.7 copy-done
  118.4 1.0 copy-done.1
  119.3 0.7 unpack.1
  120.0 13.6 %all_to_all.20.refs_0_ = f32[16,4,128]{2,1,0:T(4,128)S(1)} all-to-all(f32[16,4,128]{2,1,0:T(4,128)S(1)} %get-tuple-element.21), channel_id=1, replica_groups=mesh['z'=8,'y'=4,'xl'=2,'core'=2,'xh'=2] {'y','xl','xh'}, dimensions={0} | all-to-all | bytes 65536 | tf_op jit(solution)/shard_map/all_to_all | solution.py:479
  133.6 0.7 finish.1
  (27 shorter events, 0.1 us)
Async XLA Ops:
  0.6 12.0 %collective-permute-start = (bf16[512,4096]{1,0:T(8,128)(2,1)}, bf16[512,4096]{1,0:T(8,128)(2,1)}, u32[]{:S(2)}, u32[]{:S(2)}) collective-permute-start(bf16[512,4096]{1,0:T(8,128)(2,1)} %x_ref.1), channel_id=1, source_target_pairs={{0,2},{2,0},{1,3},{3,1},{4,6},{6,4},{5,7},{7,5},{8,10},{10,8},{9,1... | collective-permute-start | bytes 12582920 | tf_op jit(solution)/shard_map/ppermute | solution.py:438
  4.0 8.3 %collective-permute-start.1 = (bf16[512,512]{1,0:T(8,128)(2,1)}, bf16[512,512]{1,0:T(8,128)(2,1)S(1)}, u32[]{:S(2)}, u32[]{:S(2)}) collective-permute-start(bf16[512,512]{1,0:T(8,128)(2,1)} %keys_ref.1), channel_id=1, source_target_pairs={{0,2},{2,0},{1,3},{3,1},{4,6},{6,4},{5,7},{7,5},{8,10},{10,8},{9,1... | collective-permute-start | bytes 1572872 | tf_op jit(solution)/shard_map/ppermute | solution.py:438
  4.1 8.3 %collective-permute-start.2 = (bf16[512,512]{1,0:T(8,128)(2,1)}, bf16[512,512]{1,0:T(8,128)(2,1)S(1)}, u32[]{:S(2)}, u32[]{:S(2)}) collective-permute-start(bf16[512,512]{1,0:T(8,128)(2,1)} %values_ref.1), channel_id=1, source_target_pairs={{0,2},{2,0},{1,3},{3,1},{4,6},{6,4},{5,7},{7,5},{8,10},{10,8},{9,1... | collective-permute-start | bytes 1572872 | tf_op jit(solution)/shard_map/ppermute | solution.py:438
  6.1 19.0 %all-to-all-start = ((bf16[32,32,256]{2,1,0:T(8,128)(2,1)}), bf16[32,32,256]{2,1,0:T(8,128)(2,1)S(1)}, u32[]{:S(2)}, u32[]{:S(2)}) async-start(bf16[32,32,256]{2,1,0:T(8,128)(2,1)} %bitcast.7), calls=%async_computation | async-start | bytes 1048576 | tf_op jit(solution)/shard_map/all_to_all | solution.py:463
  12.2 0.8 copy-start.10
  12.3 0.9 copy-start.11
  25.1 0.8 copy-start.3
  25.9 66.6 %all-to-all-start.1 = ((bf16[16,8,2,32,256]{4,3,2,1,0:T(8,128)(2,1)}), bf16[16,8,2,32,256]{4,3,2,1,0:T(8,128)(2,1)}, u32[]{:S(2)}, u32[]{:S(2)}) async-start(bf16[16,8,2,32,256]{4,3,2,1,0:T(8,128)(2,1)} %get-tuple-element.18), calls=%async_computation.1 | async-start | bytes 8388608 | tf_op jit(solution)/shard_map/all_to_all | solution.py:473
  32.6 16.4 %collective-permute-start.7 = (bf16[8,2,2,32,256]{4,3,2,1,0:T(8,128)(2,1)}, bf16[8,2,2,32,256]{4,3,2,1,0:T(8,128)(2,1)S(1)}, u32[]{:S(2)}, u32[]{:S(2)}) collective-permute-start(bf16[8,2,2,32,256]{4,3,2,1,0:T(8,128)(2,1)} %bitcast.31), channel_id=1, source_target_pairs={{0,224},{32,0},{64,32},{96,64},{128,96},{160,128},{192,160},{224,1... | collective-permute-start | bytes 1572872 | tf_op jit(solution)/shard_map/ppermute | solution.py:442
  38.3 14.2 %collective-permute-start.3 = (bf16[8,2,2,32,256]{4,3,2,1,0:T(8,128)(2,1)}, bf16[8,2,2,32,256]{4,3,2,1,0:T(8,128)(2,1)S(1)}, u32[]{:S(2)}, u32[]{:S(2)}) collective-permute-start(bf16[8,2,2,32,256]{4,3,2,1,0:T(8,128)(2,1)} %bitcast.32), channel_id=1, source_target_pairs={{0,32},{32,64},{64,96},{96,128},{128,160},{160,192},{192,224},{224... | collective-permute-start | bytes 1572872 | tf_op jit(solution)/shard_map/ppermute | solution.py:442
  49.0 43.4 %copy-start.6 = (bf16[8,2,2,32,256]{4,3,2,1,0:T(8,128)(2,1)}, bf16[8,2,2,32,256]{4,3,2,1,0:T(8,128)(2,1)S(1)}, u32[]{:S(2)}) copy-start(bf16[8,2,2,32,256]{4,3,2,1,0:T(8,128)(2,1)S(1)} %collective-permute-done.7.refs_8_) | copy-start | bytes 1572868
  49.0 13.0 %collective-permute-start.8 = (bf16[8,2,2,32,256]{4,3,2,1,0:T(8,128)(2,1)S(1)}, bf16[8,2,2,32,256]{4,3,2,1,0:T(8,128)(2,1)S(1)}, u32[]{:S(2)}, u32[]{:S(2)}) collective-permute-start(bf16[8,2,2,32,256]{4,3,2,1,0:T(8,128)(2,1)S(1)} %collective-permute-done.7.refs_8_), channel_id=1, source_target_pairs={{0,224},{32,0},{64,32},{96,64},{128,96},{160,128},{192,160},{224,1... | collective-permute-start | bytes 1572872 | tf_op jit(solution)/shard_map/ppermute | solution.py:442
  52.4 40.0 %copy-start.7 = (bf16[8,2,2,32,256]{4,3,2,1,0:T(8,128)(2,1)}, bf16[8,2,2,32,256]{4,3,2,1,0:T(8,128)(2,1)S(1)}, u32[]{:S(2)}) copy-start(bf16[8,2,2,32,256]{4,3,2,1,0:T(8,128)(2,1)S(1)} %collective-permute-done.3.refs_1_) | copy-start | bytes 1572868
  52.4 13.2 %collective-permute-start.4 = (bf16[8,2,2,32,256]{4,3,2,1,0:T(8,128)(2,1)S(1)}, bf16[8,2,2,32,256]{4,3,2,1,0:T(8,128)(2,1)S(1)}, u32[]{:S(2)}, u32[]{:S(2)}) collective-permute-start(bf16[8,2,2,32,256]{4,3,2,1,0:T(8,128)(2,1)S(1)} %collective-permute-done.3.refs_1_), channel_id=1, source_target_pairs={{0,32},{32,64},{64,96},{96,128},{128,160},{160,192},{192,224},{224... | collective-permute-start | bytes 1572872 | tf_op jit(solution)/shard_map/ppermute | solution.py:442
  62.1 30.4 %copy-start.8 = (bf16[8,2,2,32,256]{4,3,2,1,0:T(8,128)(2,1)}, bf16[8,2,2,32,256]{4,3,2,1,0:T(8,128)(2,1)S(1)}, u32[]{:S(2)}) copy-start(bf16[8,2,2,32,256]{4,3,2,1,0:T(8,128)(2,1)S(1)} %collective-permute-done.8.refs_7_) | copy-start | bytes 1572868
  62.1 12.3 %collective-permute-start.9 = (bf16[8,2,2,32,256]{4,3,2,1,0:T(8,128)(2,1)S(1)}, bf16[8,2,2,32,256]{4,3,2,1,0:T(8,128)(2,1)S(1)}, u32[]{:S(2)}, u32[]{:S(2)}) collective-permute-start(bf16[8,2,2,32,256]{4,3,2,1,0:T(8,128)(2,1)S(1)} %collective-permute-done.8.refs_7_), channel_id=1, source_target_pairs={{0,224},{32,0},{64,32},{96,64},{128,96},{160,128},{192,160},{224,1... | collective-permute-start | bytes 1572872 | tf_op jit(solution)/shard_map/ppermute | solution.py:442
  65.6 26.9 %copy-start.9 = (bf16[8,2,2,32,256]{4,3,2,1,0:T(8,128)(2,1)}, bf16[8,2,2,32,256]{4,3,2,1,0:T(8,128)(2,1)S(1)}, u32[]{:S(2)}) copy-start(bf16[8,2,2,32,256]{4,3,2,1,0:T(8,128)(2,1)S(1)} %collective-permute-done.4.refs_2_) | copy-start | bytes 1572868
  65.6 12.2 %collective-permute-start.5 = (bf16[8,2,2,32,256]{4,3,2,1,0:T(8,128)(2,1)S(1)}, bf16[8,2,2,32,256]{4,3,2,1,0:T(8,128)(2,1)S(1)}, u32[]{:S(2)}, u32[]{:S(2)}) collective-permute-start(bf16[8,2,2,32,256]{4,3,2,1,0:T(8,128)(2,1)S(1)} %collective-permute-done.4.refs_2_), channel_id=1, source_target_pairs={{0,32},{32,64},{64,96},{96,128},{128,160},{160,192},{192,224},{224... | collective-permute-start | bytes 1572872 | tf_op jit(solution)/shard_map/ppermute | solution.py:442
  65.6 15.6 %collective-permute-start.11 = (bf16[8,2,2,32,256]{4,3,2,1,0:T(8,128)(2,1)}, bf16[8,2,2,32,256]{4,3,2,1,0:T(8,128)(2,1)S(1)}, u32[]{:S(2)}, u32[]{:S(2)}) collective-permute-start(bf16[8,2,2,32,256]{4,3,2,1,0:T(8,128)(2,1)} %bitcast.33), channel_id=1, source_target_pairs={{0,2},{2,0},{1,3},{3,1},{4,6},{6,4},{5,7},{7,5},{8,10},{10,8},{9,1... | collective-permute-start | bytes 1572872 | tf_op jit(solution)/shard_map/ppermute | solution.py:438
  68.4 13.1 %collective-permute-start.19 = (bf16[8,2,2,32,256]{4,3,2,1,0:T(8,128)(2,1)S(1)}, bf16[8,2,2,32,256]{4,3,2,1,0:T(8,128)(2,1)S(1)}, u32[]{:S(2)}, u32[]{:S(2)}) collective-permute-start(bf16[8,2,2,32,256]{4,3,2,1,0:T(8,128)(2,1)S(1)} %collective-permute-done.7.refs_8_), channel_id=1, source_target_pairs={{0,2},{2,0},{1,3},{3,1},{4,6},{6,4},{5,7},{7,5},{8,10},{10,8},{9,1... | collective-permute-start | bytes 1572872 | tf_op jit(solution)/shard_map/ppermute | solution.py:438
  68.5 13.7 %collective-permute-start.12 = (bf16[8,2,2,32,256]{4,3,2,1,0:T(8,128)(2,1)S(1)}, bf16[8,2,2,32,256]{4,3,2,1,0:T(8,128)(2,1)S(1)}, u32[]{:S(2)}, u32[]{:S(2)}) collective-permute-start(bf16[8,2,2,32,256]{4,3,2,1,0:T(8,128)(2,1)S(1)} %collective-permute-done.3.refs_1_), channel_id=1, source_target_pairs={{0,2},{2,0},{1,3},{3,1},{4,6},{6,4},{5,7},{7,5},{8,10},{10,8},{9,1... | collective-permute-start | bytes 1572872 | tf_op jit(solution)/shard_map/ppermute | solution.py:438
  74.4 18.1 %copy-start.4 = (bf16[8,2,2,32,256]{4,3,2,1,0:T(8,128)(2,1)}, bf16[8,2,2,32,256]{4,3,2,1,0:T(8,128)(2,1)S(1)}, u32[]{:S(2)}) copy-start(bf16[8,2,2,32,256]{4,3,2,1,0:T(8,128)(2,1)S(1)} %collective-permute-done.9.refs_6_) | copy-start | bytes 1572868
  74.4 7.9 %collective-permute-start.18 = (bf16[8,2,2,32,256]{4,3,2,1,0:T(8,128)(2,1)S(1)}, bf16[8,2,2,32,256]{4,3,2,1,0:T(8,128)(2,1)S(1)}, u32[]{:S(2)}, u32[]{:S(2)}) collective-permute-start(bf16[8,2,2,32,256]{4,3,2,1,0:T(8,128)(2,1)S(1)} %collective-permute-done.8.refs_7_), channel_id=1, source_target_pairs={{0,2},{2,0},{1,3},{3,1},{4,6},{6,4},{5,7},{7,5},{8,10},{10,8},{9,1... | collective-permute-start | bytes 1572872 | tf_op jit(solution)/shard_map/ppermute | solution.py:438
  77.8 14.7 %copy-start.5 = (bf16[8,2,2,32,256]{4,3,2,1,0:T(8,128)(2,1)}, bf16[8,2,2,32,256]{4,3,2,1,0:T(8,128)(2,1)S(1)}, u32[]{:S(2)}) copy-start(bf16[8,2,2,32,256]{4,3,2,1,0:T(8,128)(2,1)S(1)} %collective-permute-done.5.refs_3_) | copy-start | bytes 1572868
  77.8 24.3 %collective-permute-start.13 = (bf16[8,2,2,32,256]{4,3,2,1,0:T(8,128)(2,1)S(1)}, bf16[8,2,2,32,256]{4,3,2,1,0:T(8,128)(2,1)}, u32[]{:S(2)}, u32[]{:S(2)}) collective-permute-start(bf16[8,2,2,32,256]{4,3,2,1,0:T(8,128)(2,1)S(1)} %collective-permute-done.4.refs_2_), channel_id=1, source_target_pairs={{0,2},{2,0},{1,3},{3,1},{4,6},{6,4},{5,7},{7,5},{8,10},{10,8},{9,1... | collective-permute-start | bytes 1572872 | tf_op jit(solution)/shard_map/ppermute | solution.py:438
  81.2 9.9 %copy-start.12 = (bf16[8,2,2,32,256]{4,3,2,1,0:T(8,128)(2,1)}, bf16[8,2,2,32,256]{4,3,2,1,0:T(8,128)(2,1)S(1)}, u32[]{:S(2)}) copy-start(bf16[8,2,2,32,256]{4,3,2,1,0:T(8,128)(2,1)S(1)} %collective-permute-done.11) | copy-start | bytes 1572868
  81.2 8.1 %collective-permute-start.10 = (bf16[4,2,2,32,256]{4,3,2,1,0:T(8,128)(2,1)S(1)}, bf16[4,2,2,32,256]{4,3,2,1,0:T(8,128)(2,1)}, u32[]{:S(2)}, u32[]{:S(2)}) collective-permute-start(bf16[4,2,2,32,256]{4,3,2,1,0:T(8,128)(2,1)S(1)} %slice.9), channel_id=1, source_target_pairs={{0,224},{32,0},{64,32},{96,64},{128,96},{160,128},{192,160},{224,1... | collective-permute-start | bytes 786440 | tf_op jit(solution)/shard_map/ppermute | solution.py:442
  81.4 9.7 %copy-start.13 = (bf16[8,2,2,32,256]{4,3,2,1,0:T(8,128)(2,1)}, bf16[8,2,2,32,256]{4,3,2,1,0:T(8,128)(2,1)S(1)}, u32[]{:S(2)}) copy-start(bf16[8,2,2,32,256]{4,3,2,1,0:T(8,128)(2,1)S(1)} %collective-permute-done.19) | copy-start | bytes 1572868
  81.4 20.7 %collective-permute-start.17 = (bf16[8,2,2,32,256]{4,3,2,1,0:T(8,128)(2,1)S(1)}, bf16[8,2,2,32,256]{4,3,2,1,0:T(8,128)(2,1)}, u32[]{:S(2)}, u32[]{:S(2)}) collective-permute-start(bf16[8,2,2,32,256]{4,3,2,1,0:T(8,128)(2,1)S(1)} %collective-permute-done.9.refs_6_), channel_id=1, source_target_pairs={{0,2},{2,0},{1,3},{3,1},{4,6},{6,4},{5,7},{7,5},{8,10},{10,8},{9,1... | collective-permute-start | bytes 1572872 | tf_op jit(solution)/shard_map/ppermute | solution.py:438
  82.2 8.9 %copy-start.14 = (bf16[8,2,2,32,256]{4,3,2,1,0:T(8,128)(2,1)}, bf16[8,2,2,32,256]{4,3,2,1,0:T(8,128)(2,1)S(1)}, u32[]{:S(2)}) copy-start(bf16[8,2,2,32,256]{4,3,2,1,0:T(8,128)(2,1)S(1)} %collective-permute-done.12) | copy-start | bytes 1572868
  82.2 19.9 %collective-permute-start.14 = (bf16[8,2,2,32,256]{4,3,2,1,0:T(8,128)(2,1)S(1)}, bf16[8,2,2,32,256]{4,3,2,1,0:T(8,128)(2,1)}, u32[]{:S(2)}, u32[]{:S(2)}) collective-permute-start(bf16[8,2,2,32,256]{4,3,2,1,0:T(8,128)(2,1)S(1)} %collective-permute-done.5.refs_3_), channel_id=1, source_target_pairs={{0,2},{2,0},{1,3},{3,1},{4,6},{6,4},{5,7},{7,5},{8,10},{10,8},{9,1... | collective-permute-start | bytes 1572872 | tf_op jit(solution)/shard_map/ppermute | solution.py:438
  82.3 8.8 %copy-start.15 = (bf16[8,2,2,32,256]{4,3,2,1,0:T(8,128)(2,1)}, bf16[8,2,2,32,256]{4,3,2,1,0:T(8,128)(2,1)S(1)}, u32[]{:S(2)}) copy-start(bf16[8,2,2,32,256]{4,3,2,1,0:T(8,128)(2,1)S(1)} %collective-permute-done.18) | copy-start | bytes 1572868
  82.3 8.8 %collective-permute-start.6 = (bf16[4,2,2,32,256]{4,3,2,1,0:T(8,128)(2,1)S(1)}, bf16[4,2,2,32,256]{4,3,2,1,0:T(8,128)(2,1)}, u32[]{:S(2)}, u32[]{:S(2)}) collective-permute-start(bf16[4,2,2,32,256]{4,3,2,1,0:T(8,128)(2,1)S(1)} %slice.8), channel_id=1, source_target_pairs={{0,32},{32,64},{64,96},{96,128},{128,160},{160,192},{192,224},{224... | collective-permute-start | bytes 786440 | tf_op jit(solution)/shard_map/ppermute | solution.py:442
  89.3 12.8 %collective-permute-start.16 = (bf16[4,2,2,32,256]{4,3,2,1,0:T(8,128)(2,1)}, bf16[4,2,2,32,256]{4,3,2,1,0:T(8,128)(2,1)}, u32[]{:S(2)}, u32[]{:S(2)}) collective-permute-start(bf16[4,2,2,32,256]{4,3,2,1,0:T(8,128)(2,1)} %collective-permute-done.10.refs_5_), channel_id=1, source_target_pairs={{0,2},{2,0},{1,3},{3,1},{4,6},{6,4},{5,7},{7,5},{8,10},{10,8},{9,1... | collective-permute-start | bytes 786440 | tf_op jit(solution)/shard_map/ppermute | solution.py:438
  91.1 11.0 %collective-permute-start.15 = (bf16[4,2,2,32,256]{4,3,2,1,0:T(8,128)(2,1)}, bf16[4,2,2,32,256]{4,3,2,1,0:T(8,128)(2,1)}, u32[]{:S(2)}, u32[]{:S(2)}) collective-permute-start(bf16[4,2,2,32,256]{4,3,2,1,0:T(8,128)(2,1)} %collective-permute-done.6.refs_4_), channel_id=1, source_target_pairs={{0,2},{2,0},{1,3},{3,1},{4,6},{6,4},{5,7},{7,5},{8,10},{10,8},{9,1... | collective-permute-start | bytes 786440 | tf_op jit(solution)/shard_map/ppermute | solution.py:438
  97.0 20.6 %all-to-all-start.2 = ((bf16[16,48,256]{2,1,0:T(8,128)(2,1)}), bf16[16,48,256]{2,1,0:T(8,128)(2,1)S(1)}, u32[]{:S(2)}, u32[]{:S(2)}) async-start(bf16[16,48,256]{2,1,0:T(8,128)(2,1)} %pack.1), calls=%async_computation.2 | async-start | bytes 786432 | tf_op jit(solution)/shard_map/all_to_all | solution.py:474
  117.6 16.0 %copy-start.2 = (f32[4096]{0:T(1024)S(1)}, f32[4096]{0:T(1024)}, u32[]{:S(2)}) copy-start(f32[4096]{0:T(1024)} %param.7) | copy-start | bytes 49156
  117.6 0.7 copy-start
  118.3 1.0 copy-start.1

commit v4 on v3

--- a/solution.py
+++ b/solution.py
@@ -65,7 +65,6 @@
     return pltpu.make_async_copy(first, target, sem)
 
 
-SMEM = pl.BlockSpec(memory_space=pltpu.SMEM)
 ANY = pl.BlockSpec(memory_space=pl.ANY)
 INNER = pl.BlockSpec(memory_space=pltpu.VMEM)
 
@@ -91,10 +90,10 @@
         inv_buf[which, part, :] = jnp.broadcast_to(lax.rsqrt(mean + EPS), (rows, 128))
 
 
-def grads_kernel(place_ref, own_ref, other_ref, gain_ref, keys_own_ref, values_own_ref,
+def grads_kernel(own_ref, other_ref, gain_ref, keys_own_ref, values_own_ref,
                  keys_other_ref, values_other_ref, out_ref, inv_ref,
                  x_buf, d_buf, inv_buf, gain_buf, out_buf, sems, small_sems, out_sems):
-    core_at = place_ref[0]
+    core_at = lax.axis_index("core")
     large = []
     for which, ref in enumerate((own_ref, other_ref)):
         rows = [pl.ds(i * (ROWS // 8), ROWS // 8) for i in range(8)]
@@ -147,7 +146,7 @@
     shape = (GROUPS * XH, Z, CORE, BLOCK, HALF)
     return pl.pallas_call(
         grads_kernel,
-        in_specs=[SMEM] + [ANY] * 7,
+        in_specs=[ANY] * 7,
         out_specs=[ANY] * 2,
         out_shape=[
             jax.ShapeDtypeStruct(shape, BF),
@@ -176,14 +175,15 @@
 EXTRA = 16
 
 
-def pack_kernel(place_ref, in_ref, *refs):
+def pack_kernel(in_ref, *refs):
     w_refs = refs[: len(RING)]
     out_ref, prod_ref, w_buf, in_buf, sems, in_sems = refs[len(RING) :]
-    group, half = place_ref[2], place_ref[3]
+    group = lax.axis_index("y") * XL + lax.axis_index("xl")
+    half, z_at = lax.axis_index("xh"), lax.axis_index("z")
     terms = copies([(in_ref.at[:, z], in_buf.at[:, z]) for z in range(Z)], in_sems)
     waits = []
     for (distance, first, groups), ref in zip(RING, w_refs):
-        z = lax.rem(place_ref[1] + Z - distance, Z)
+        z = lax.rem(z_at + Z - distance, Z)
         inside = lax.rem(group, groups)
         copy = pltpu.make_async_copy(
             ref.at[inside, :, half], w_buf.at[pl.ds(z * CORE, CORE)], sems.at[distance]
@@ -228,10 +228,10 @@
         out_ref[at, BLOCK:] = extra
 
 
-def pack(place, terms, blocks):
+def pack(terms, blocks):
     return pl.pallas_call(
         pack_kernel,
-        in_specs=[SMEM] + [ANY] * (1 + len(RING)),
+        in_specs=[ANY] * (1 + len(RING)),
         out_specs=INNER,
         out_shape=jax.ShapeDtypeStruct((Z * CORE, BLOCK + EXTRA, HALF), BF),
         scratch_shapes=[
@@ -244,10 +244,10 @@
         compiler_params=params(),
         cost_estimate=cheap(),
         name="pack",
-    )(place, terms, *blocks)
-
-
-def unpack_kernel(scale, in_ref, key_ref, value_ref, gains_ref):
+    )(terms, *blocks)
+
+
+def unpack_kernel(scale, in_ref, rows_ref, key_ref, value_ref, gains_ref):
     for which, ref in enumerate((key_ref, value_ref)):
         total = in_ref[which, :BLOCK].astype(F32)
         for z in range(1, Z):
@@ -264,23 +264,23 @@
                 gains_ref[at, line * 2 + piece : line * 2 + piece + 1] = lanes
 
 
-def unpack(scale, received):
+def unpack(scale, received, rows):
     def kernel(*refs):
         unpack_kernel(scale, *refs)
 
     return pl.pallas_call(
         kernel,
-        in_specs=[INNER],
+        in_specs=[INNER, ANY],
         out_specs=[INNER] * 3,
         out_shape=[
             jax.ShapeDtypeStruct((BLOCK, HALF), F32),
             jax.ShapeDtypeStruct((BLOCK, HALF), F32),
             jax.ShapeDtypeStruct((Y * XL * XH, 4, 128), F32),
         ],
-        compiler_params=params(SMALL),
+        compiler_params=params(),
         cost_estimate=cheap(),
         name="unpack",
-    )(received)
+    )(received, rows)
 
 
 def weight_rows(buf, part):
@@ -289,15 +289,15 @@
     return jnp.concatenate([ref[:, half].reshape(WIDE, HALF) for half in range(XH)], axis=1)
 
 
-def rows_kernel(place_ref, x_ref, gain_ref, inv_ref, keys_ref, values_ref, *rest):
+def rows_kernel(x_ref, gain_ref, inv_ref, keys_ref, values_ref, *rest):
     mine, theirs = rest[: len(RING)], rest[len(RING) : 2 * len(RING)]
     (out_keys_ref, out_values_ref, dx_ref, x_buf, w_buf, d_buf, inv_buf, gain_buf, out_buf, dx_buf,
      sems, small_sems, out_sems, dx_sems) = rest[2 * len(RING) :]
-    core = place_ref[0]
+    core = lax.axis_index("core")
     rows = W // BLOCK
 
     def columns(at):
-        z = lax.rem(place_ref[1] + Z - at, Z)
+        z = lax.rem(lax.axis_index("z") + Z - at, Z)
         return pl.ds(pl.multiple_of(z * W, W), W)
 
     def fetch(part):
@@ -380,7 +380,7 @@
 def rows_pass(*inputs):
     return pl.pallas_call(
         rows_kernel,
-        in_specs=[SMEM] + [ANY] * (5 + 2 * len(RING)),
+        in_specs=[ANY] * (5 + 2 * len(RING)),
         out_specs=[ANY] * 3,
         out_shape=[
             jax.ShapeDtypeStruct((ROWS, C), BF),
@@ -453,29 +453,26 @@
 
 def shards(tokens, gain, w_key, w_value, d_keys, d_values):
     scale = 1.0 / math.sqrt(ROWS * Z * Y * XL * CORE * XH)
-    y_at, low, high = lax.axis_index("y"), lax.axis_index("xl"), lax.axis_index("xh")
-    core, z_at = lax.axis_index("core"), lax.axis_index("z")
-    place = jnp.stack([core, z_at, y_at * XL + low, high]).astype(jnp.int32)
     row_gain = gain.reshape(1, D)
 
-    pair = jnp.stack([w_key, w_value])
-    sent = jnp.broadcast_to(pair[None, :, None], (Y * XL, CORE, XH, BLOCK, HALF))
+    which = lax.broadcasted_iota(jnp.int32, (Y * XL, CORE, XH, BLOCK, HALF), 1)
+    sent = jnp.where(which == 0, w_key[None, None, None], w_value[None, None, None])
     plane = lax.all_to_all(
         sent.reshape(Y * XL * CORE * XH, BLOCK, HALF), ("y", "xl", "core", "xh"), 0, 0, tiled=True
     )
 
-    inputs = (place, tokens, swap(tokens), row_gain, d_keys, d_values, swap(d_keys), swap(d_values))
+    inputs = (tokens, swap(tokens), row_gain, d_keys, d_values, swap(d_keys), swap(d_values))
     terms, inv = gradient_terms(*inputs)
-    plane = after(plane, inv).reshape(GROUPS, CORE, XH, BLOCK, HALF)
+    plane = plane.reshape(GROUPS, CORE, XH, BLOCK, HALF)
     mine = around(plane)
     theirs = [swap(block) for block in mine]
 
-    sent = pack(place, lax.all_to_all(terms, PLANE, 0, 0, tiled=True), mine)
+    sent = pack(lax.all_to_all(terms, PLANE, 0, 0, tiled=True), mine)
     received = lax.all_to_all(sent, ("z", "core"), 0, 0, tiled=True)
 
     flat = [block.reshape(-1, XH, BLOCK, HALF) for block in mine + theirs]
-    keys, values, d_tokens = rows_pass(place, tokens, row_gain, inv, d_keys, d_values, *flat)
-    grad_key, grad_value, gains = unpack(scale, after(received, d_tokens))
+    keys, values, d_tokens = rows_pass(tokens, row_gain, inv, d_keys, d_values, *flat)
+    grad_key, grad_value, gains = unpack(scale, received, keys)
     gains = lax.all_to_all(gains, PLANE, 0, 0, tiled=True)
     grad_gain = finish(scale, gains, row_gain).reshape(D)
     return (keys, values, d_tokens, grad_key, grad_value, grad_gain)

time: 135 us -> 132 us (0.978)
  local copies, waits for them, and re-layouts: 4.06 us -> 1.54 us
    unnamed x32, local copies, waits for them, and re-layouts: 3.17 us -> 1.33 us
    ppermute x8, starting transfers between devices: 13.8 us -> 15.4 us  [along_z(): return lax.ppermute(a, 'z', [(i, (i + step) % Z) for i in range(Z)])]
    ppermute x8, waiting for transfers between devices: 33 us -> 31.3 us  [along_z(): return lax.ppermute(a, 'z', [(i, (i + step) % Z) for i in range(Z)])]
    select_n x0 -> x1, other arithmetic: none -> 1.64 us  [shards(): jnp.where(which == 0, w_key[None, None, None], w_value[None, None, None])]
    ppermute x12, starting transfers between devices: 16.8 us -> 15.4 us  [swap(): return lax.ppermute(a, 'core', [(0, 1), (1, 0)])]
    another operation x2 -> x0, other arithmetic: 1.39 us -> none  [the longest x1 0.74 us: shards(): pair = jnp.stack([w_key, w_value])]
    all_to_all x1, starting transfers between devices: 5.1 us -> 6.45 us  [shards(): received = lax.all_to_all(sent, ('z', 'core'), 0, 0, tiled=True)]
    pallas_call x6 -> x4, Pallas kernels: 32.4 us -> 31.4 us  [the longest x1 14.8 us: rows_pass(): pl.pallas_call(rows_kernel, in_specs=[ANY] * (5 + 2 * len(RING)), out_spe...]
  transfers between devices with their start and end apart: 23 -> 23, of which waited for: 7 -> 6; matrix products, arithmetic and copies ran while one was open for 2% -> 1% of each run, Pallas kernels for 24% -> 23%
where the time goes in v4:
time: 132 us; the launch traced here: 131 us
  starting transfers between devices  49.1 us (37%)
  waiting for transfers between devices  32.1 us (24%)
  Pallas kernels  32.1 us (24%)
  blocking collectives  13.8 us (10%)
  other arithmetic  1.65 us (1%)
  local copies, waits for them, and re-layouts  1.54 us (1%)
    ppermute x8, waiting for transfers between devices, along_z(): return lax.ppermute(a, 'z', [(i, (i + step) % Z) for i in range(Z)])  31.3 us
    ppermute x8, starting transfers between devices, along_z(): return lax.ppermute(a, 'z', [(i, (i + step) % Z) for i in range(Z)])  15.4 us
    ppermute x12, starting transfers between devices, swap(): return lax.ppermute(a, 'core', [(0, 1), (1, 0)])  15.4 us
    pallas_call x1, Pallas kernels, rows_pass(): pl.pallas_call(rows_kernel, in_specs=[ANY] * (5 + 2 * len(RING)), out_spe...  14.8 us
    all_to_all x1, blocking collectives, shards(): gains = lax.all_to_all(gains, PLANE, 0, 0, tiled=True)  13.8 us
    pallas_call x1, Pallas kernels, gradient_terms(): pl.pallas_call(grads_kernel, in_specs=[ANY] * 7, out_specs=[ANY] * 2, out...  11.2 us
    all_to_all x1, starting transfers between devices, shards(): received = lax.all_to_all(sent, ('z', 'core'), 0, 0, tiled=True)  6.45 us
    all_to_all x1, starting transfers between devices, shards(): sent = pack(lax.all_to_all(terms, PLANE, 0, 0, tiled=True), mine)  6.38 us
  transfers between devices with their start and end apart: 23, of which 6 were waited for; matrix products, arithmetic and copies ran while one was open for 1% of the time, Pallas kernels for 23%

profile of v4, /device:TPU:1, one launch (start us, length us, event | category | flops | bytes accessed | tf_op | source)
XLA Modules:
  0.0 131.3 jit_solution(13397026795389344445)
XLA Ops:
  0.6 3.3 %collective-permute-start = (bf16[512,4096]{1,0:T(8,128)(2,1)}, bf16[512,4096]{1,0:T(8,128)(2,1)}, u32[]{:S(2)}, u32[]{:S(2)}) collective-permute-start(bf16[512,4096]{1,0:T(8,128)(2,1)} %x_ref.1), channel_id=1, source_target_pairs={{0,2},{2,0},{1,3},{3,1},{4,6},{6,4},{5,7},{7,5},{8,10},{10,8},{9,1... | collective-permute-start | bytes 12582920 | tf_op jit(solution)/shard_map/ppermute | solution.py:438
  4.0 0.1 collective-permute-start.1
  4.1 0.4 collective-permute-start.2
  4.5 0.1 iota.11
  4.6 0.1 iota.12
  4.7 1.6 %broadcast_select_fusion = bf16[32,32,256]{2,1,0:T(8,128)(2,1)} fusion(pred[32]{0:T(512)(128)(4,1)S(1)} %iota.12, bf16[32,256]{1,0:T(8,128)(2,1)} %param.9, bf16[32,256]{1,0:T(8,128)(2,1)} %param.8), kind=kLoop, calls=%fused_computation | loop fusion | flops 262144 | bytes 557088 | tf_op jit(solution)/shard_map/jit(_where)/select_n | solution.py:459
  6.3 5.5 %all-to-all-start = ((bf16[32,32,256]{2,1,0:T(8,128)(2,1)}), bf16[32,32,256]{2,1,0:T(8,128)(2,1)S(1)}, u32[]{:S(2)}, u32[]{:S(2)}) async-start(bf16[32,32,256]{2,1,0:T(8,128)(2,1)} %broadcast_select_fusion), calls=%async_computation | async-start | bytes 1048576 | tf_op jit(solution)/shard_map/all_to_all | solution.py:460
  11.8 0.0 collective-permute-done.1.keys_other_ref
  11.8 0.0 copy-start.9
  11.8 0.5 collective-permute-done.2.values_other_ref
  12.3 0.3 collective-permute-done.other_ref
  12.6 0.0 copy-done.9
  12.6 0.5 copy-done.10
  13.1 11.2 %gradient_terms.1 = (bf16[16,8,2,32,256]{4,3,2,1,0:T(8,128)(2,1)}, f32[512,128]{1,0:T(8,128)}) custom-call(bf16[512,4096]{1,0:T(8,128)(2,1)} %x_ref.1, bf16[512,4096]{1,0:T(8,128)(2,1)} %collective-permute-done.other_ref, f32[1,4096]{1,0:T(1,128)} %bitcast.21, bf16[512,512]{1,0:T(8,128)(2,1)} %keys_ref.1, bf16[512,512]{1,0:T(8,128)(2,1)} %values_ref.1, ...), custom_call_target="tpu_custom_call" | custom-call | flops 1048576 | bytes 1048576 | tf_op jit(solution)/shard_map/gradient_terms/pallas_call | solution.py:147
  24.3 0.0 all-to-all-done
  24.3 0.0 copy-start.1
  24.3 6.4 %all-to-all-start.1 = ((bf16[16,8,2,32,256]{4,3,2,1,0:T(8,128)(2,1)}), bf16[16,8,2,32,256]{4,3,2,1,0:T(8,128)(2,1)}, u32[]{:S(2)}, u32[]{:S(2)}) async-start(bf16[16,8,2,32,256]{4,3,2,1,0:T(8,128)(2,1)} %get-tuple-element.18), calls=%async_computation.1 | async-start | bytes 8388608 | tf_op jit(solution)/shard_map/all_to_all | solution.py:470
  30.7 5.7 %collective-permute-start.7 = (bf16[8,2,2,32,256]{4,3,2,1,0:T(8,128)(2,1)S(1)}, bf16[8,2,2,32,256]{4,3,2,1,0:T(8,128)(2,1)S(1)}, u32[]{:S(2)}, u32[]{:S(2)}) collective-permute-start(bf16[8,2,2,32,256]{4,3,2,1,0:T(8,128)(2,1)S(1)} %bitcast.24), channel_id=1, source_target_pairs={{0,224},{32,0},{64,32},{96,64},{128,96},{160,128},{192,160},{224,1... | collective-permute-start | bytes 1572872 | tf_op jit(solution)/shard_map/ppermute | solution.py:442
  36.4 0.0 collective-permute-start.3
  36.4 10.4 %collective-permute-done.7.refs_8_ = bf16[8,2,2,32,256]{4,3,2,1,0:T(8,128)(2,1)S(1)} collective-permute-done((bf16[8,2,2,32,256]{4,3,2,1,0:T(8,128)(2,1)S(1)}, bf16[8,2,2,32,256]{4,3,2,1,0:T(8,128)(2,1)S(1)}, u32[]{:S(2)}, u32[]{:S(2)}) %collective-permute-start.7) | collective-permute-done | bytes 524320 | tf_op jit(solution)/shard_map/ppermute | solution.py:442
  46.8 3.5 %collective-permute-start.8 = (bf16[8,2,2,32,256]{4,3,2,1,0:T(8,128)(2,1)S(1)}, bf16[8,2,2,32,256]{4,3,2,1,0:T(8,128)(2,1)S(1)}, u32[]{:S(2)}, u32[]{:S(2)}) collective-permute-start(bf16[8,2,2,32,256]{4,3,2,1,0:T(8,128)(2,1)S(1)} %collective-permute-done.7.refs_8_), channel_id=1, source_target_pairs={{0,224},{32,0},{64,32},{96,64},{128,96},{160,128},{192,160},{224,1... | collective-permute-start | bytes 1572872 | tf_op jit(solution)/shard_map/ppermute | solution.py:442
  50.3 0.0 collective-permute-done.3.refs_1_
  50.3 0.0 collective-permute-start.4
  50.3 9.6 %collective-permute-done.8.refs_7_ = bf16[8,2,2,32,256]{4,3,2,1,0:T(8,128)(2,1)S(1)} collective-permute-done((bf16[8,2,2,32,256]{4,3,2,1,0:T(8,128)(2,1)S(1)}, bf16[8,2,2,32,256]{4,3,2,1,0:T(8,128)(2,1)S(1)}, u32[]{:S(2)}, u32[]{:S(2)}) %collective-permute-start.8) | collective-permute-done | bytes 524320 | tf_op jit(solution)/shard_map/ppermute | solution.py:442
  60.0 3.5 %collective-permute-start.9 = (bf16[8,2,2,32,256]{4,3,2,1,0:T(8,128)(2,1)S(1)}, bf16[8,2,2,32,256]{4,3,2,1,0:T(8,128)(2,1)S(1)}, u32[]{:S(2)}, u32[]{:S(2)}) collective-permute-start(bf16[8,2,2,32,256]{4,3,2,1,0:T(8,128)(2,1)S(1)} %collective-permute-done.8.refs_7_), channel_id=1, source_target_pairs={{0,224},{32,0},{64,32},{96,64},{128,96},{160,128},{192,160},{224,1... | collective-permute-start | bytes 1572872 | tf_op jit(solution)/shard_map/ppermute | solution.py:442
  63.5 0.0 collective-permute-done.4.refs_2_
  63.5 0.0 collective-permute-start.5
  63.5 0.0 copy-done.1
  63.5 2.8 %collective-permute-start.11 = (bf16[8,2,2,32,256]{4,3,2,1,0:T(8,128)(2,1)S(1)}, bf16[8,2,2,32,256]{4,3,2,1,0:T(8,128)(2,1)S(1)}, u32[]{:S(2)}, u32[]{:S(2)}) collective-permute-start(bf16[8,2,2,32,256]{4,3,2,1,0:T(8,128)(2,1)S(1)} %bitcast.26), channel_id=1, source_target_pairs={{0,2},{2,0},{1,3},{3,1},{4,6},{6,4},{5,7},{7,5},{8,10},{10,8},{9,1... | collective-permute-start | bytes 1572872 | tf_op jit(solution)/shard_map/ppermute | solution.py:438
  66.3 0.1 collective-permute-start.12
  66.4 0.4 collective-permute-start.19
  66.8 5.5 %collective-permute-done.9.refs_6_ = bf16[8,2,2,32,256]{4,3,2,1,0:T(8,128)(2,1)S(1)} collective-permute-done((bf16[8,2,2,32,256]{4,3,2,1,0:T(8,128)(2,1)S(1)}, bf16[8,2,2,32,256]{4,3,2,1,0:T(8,128)(2,1)S(1)}, u32[]{:S(2)}, u32[]{:S(2)}) %collective-permute-start.9) | collective-permute-done | bytes 524320 | tf_op jit(solution)/shard_map/ppermute | solution.py:442
  72.3 3.3 %collective-permute-start.13 = (bf16[8,2,2,32,256]{4,3,2,1,0:T(8,128)(2,1)S(1)}, bf16[8,2,2,32,256]{4,3,2,1,0:T(8,128)(2,1)S(1)}, u32[]{:S(2)}, u32[]{:S(2)}) collective-permute-start(bf16[8,2,2,32,256]{4,3,2,1,0:T(8,128)(2,1)S(1)} %collective-permute-done.4.refs_2_), channel_id=1, source_target_pairs={{0,2},{2,0},{1,3},{3,1},{4,6},{6,4},{5,7},{7,5},{8,10},{10,8},{9,1... | collective-permute-start | bytes 1572872 | tf_op jit(solution)/shard_map/ppermute | solution.py:438
  75.6 0.0 collective-permute-done.5.refs_3_
  75.7 3.4 %collective-permute-start.18 = (bf16[8,2,2,32,256]{4,3,2,1,0:T(8,128)(2,1)S(1)}, bf16[8,2,2,32,256]{4,3,2,1,0:T(8,128)(2,1)}, u32[]{:S(2)}, u32[]{:S(2)}) collective-permute-start(bf16[8,2,2,32,256]{4,3,2,1,0:T(8,128)(2,1)S(1)} %collective-permute-done.8.refs_7_), channel_id=1, source_target_pairs={{0,2},{2,0},{1,3},{3,1},{4,6},{6,4},{5,7},{7,5},{8,10},{10,8},{9,1... | collective-permute-start | bytes 1572872 | tf_op jit(solution)/shard_map/ppermute | solution.py:438
  79.1 0.0 collective-permute-done.11
  79.1 0.1 collective-permute-start.6
  79.2 0.0 collective-permute-done.12
  79.2 2.6 %collective-permute-start.10 = (bf16[4,2,2,32,256]{4,3,2,1,0:T(8,128)(2,1)S(1)}, bf16[4,2,2,32,256]{4,3,2,1,0:T(8,128)(2,1)}, u32[]{:S(2)}, u32[]{:S(2)}) collective-permute-start(bf16[4,2,2,32,256]{4,3,2,1,0:T(8,128)(2,1)S(1)} %slice.9), channel_id=1, source_target_pairs={{0,224},{32,0},{64,32},{96,64},{128,96},{160,128},{192,160},{224,1... | collective-permute-start | bytes 786440 | tf_op jit(solution)/shard_map/ppermute | solution.py:442
  81.8 0.0 collective-permute-done.19
  81.8 0.6 collective-permute-start.14
  82.4 0.0 copy-done.8
  82.4 0.0 collective-permute-done.13
  82.4 0.1 collective-permute-start.17
  82.5 5.8 %collective-permute-done.6.refs_4_ = bf16[4,2,2,32,256]{4,3,2,1,0:T(8,128)(2,1)S(1)} collective-permute-done((bf16[4,2,2,32,256]{4,3,2,1,0:T(8,128)(2,1)S(1)}, bf16[4,2,2,32,256]{4,3,2,1,0:T(8,128)(2,1)S(1)}, u32[]{:S(2)}, u32[]{:S(2)}) %collective-permute-start.6) | collective-permute-done | bytes 262176 | tf_op jit(solution)/shard_map/ppermute | solution.py:442
  88.3 0.8 collective-permute-start.15
  89.1 0.0 collective-permute-done.10.refs_5_
  89.1 0.1 collective-permute-start.16
  89.2 0.0 all-to-all-done.1.in_ref
  89.3 3.8 %pack.1 = bf16[16,48,256]{2,1,0:T(8,128)(2,1)} custom-call(bf16[16,8,2,32,256]{4,3,2,1,0:T(8,128)(2,1)} %all-to-all-done.1.in_ref, bf16[8,2,2,32,256]{4,3,2,1,0:T(8,128)(2,1)} %bitcast.27, bf16[8,2,2,32,256]{4,3,2,1,0:T(8,128)(2,1)} %copy-done.6, bf16[8,2,2,32,256]{4,3,2,1,0:T(8,128)(2,1)} %copy-done.8, bf16[8,2,2,32,256]{4,3,2,1,0:T(8,128)(2,1)} %copy-done.4, ...), custom_call_target="tpu_custom_call" | custom-call | flops 1048576 | bytes 1048576 | tf_op jit(solution)/shard_map/pack/pallas_call | solution.py:232
  93.1 6.5 %all-to-all-start.2 = ((bf16[16,48,256]{2,1,0:T(8,128)(2,1)}), bf16[16,48,256]{2,1,0:T(8,128)(2,1)S(1)}, u32[]{:S(2)}, u32[]{:S(2)}) async-start(bf16[16,48,256]{2,1,0:T(8,128)(2,1)} %pack.1), calls=%async_computation.2 | async-start | bytes 786432 | tf_op jit(solution)/shard_map/all_to_all | solution.py:471
  99.5 0.0 collective-permute-done.18
  99.5 0.0 collective-permute-done.15
  99.6 0.0 collective-permute-done.16
  99.6 0.0 collective-permute-done.14
  99.6 0.0 collective-permute-done.17
  99.6 0.0 copy-start
  99.6 14.8 %rows_pass.1 = (bf16[512,512]{1,0:T(8,128)(2,1)}, bf16[512,512]{1,0:T(8,128)(2,1)}, bf16[512,4096]{1,0:T(8,128)(2,1)}) custom-call(bf16[512,4096]{1,0:T(8,128)(2,1)} %x_ref.1, f32[1,4096]{1,0:T(1,128)} %bitcast.22, f32[512,128]{1,0:T(8,128)} %get-tuple-element.14.inv_ref, bf16[512,512]{1,0:T(8,128)(2,1)} %keys_ref.1, bf16[512,512]{1,0:T(8,128)(2,1)} %values_ref.1, ...), custom_call_target="tpu_custom_call" | custom-call | flops 8589934592 | bytes 18874368 | tf_op jit(solution)/shard_map/rows_pass/pallas_call | solution.py:381
  114.4 0.0 all-to-all-done.2.refs_0_
  114.4 0.0 copy-start.2
  114.4 0.7 copy-done.2
  115.1 1.7 %unpack.1 = (f32[32,256]{1,0:T(8,128)}, f32[32,256]{1,0:T(8,128)}, f32[16,4,128]{2,1,0:T(4,128)}) custom-call(bf16[16,48,256]{2,1,0:T(8,128)(2,1)} %copy-done.2, bf16[512,512]{1,0:T(8,128)(2,1)} %get-tuple-element.8.refs_1_), custom_call_target="tpu_custom_call" | custom-call | flops 1048576 | bytes 1048576 | tf_op jit(solution)/shard_map/unpack/pallas_call | solution.py:271
  116.8 13.8 %all_to_all.20.refs_0_ = f32[16,4,128]{2,1,0:T(4,128)S(1)} all-to-all(f32[16,4,128]{2,1,0:T(4,128)} %get-tuple-element.21), channel_id=1, replica_groups=mesh['z'=8,'y'=4,'xl'=2,'core'=2,'xh'=2] {'y','xl','xh'}, dimensions={0} | all-to-all | bytes 65536 | tf_op jit(solution)/shard_map/all_to_all | solution.py:476
  130.6 0.7 finish.1
  (26 shorter events, 0.1 us)
Async XLA Ops:
  0.6 12.0 %collective-permute-start = (bf16[512,4096]{1,0:T(8,128)(2,1)}, bf16[512,4096]{1,0:T(8,128)(2,1)}, u32[]{:S(2)}, u32[]{:S(2)}) collective-permute-start(bf16[512,4096]{1,0:T(8,128)(2,1)} %x_ref.1), channel_id=1, source_target_pairs={{0,2},{2,0},{1,3},{3,1},{4,6},{6,4},{5,7},{7,5},{8,10},{10,8},{9,1... | collective-permute-start | bytes 12582920 | tf_op jit(solution)/shard_map/ppermute | solution.py:438
  4.0 7.8 %collective-permute-start.1 = (bf16[512,512]{1,0:T(8,128)(2,1)}, bf16[512,512]{1,0:T(8,128)(2,1)S(1)}, u32[]{:S(2)}, u32[]{:S(2)}) collective-permute-start(bf16[512,512]{1,0:T(8,128)(2,1)} %keys_ref.1), channel_id=1, source_target_pairs={{0,2},{2,0},{1,3},{3,1},{4,6},{6,4},{5,7},{7,5},{8,10},{10,8},{9,1... | collective-permute-start | bytes 1572872 | tf_op jit(solution)/shard_map/ppermute | solution.py:438
  4.1 8.3 %collective-permute-start.2 = (bf16[512,512]{1,0:T(8,128)(2,1)}, bf16[512,512]{1,0:T(8,128)(2,1)S(1)}, u32[]{:S(2)}, u32[]{:S(2)}) collective-permute-start(bf16[512,512]{1,0:T(8,128)(2,1)} %values_ref.1), channel_id=1, source_target_pairs={{0,2},{2,0},{1,3},{3,1},{4,6},{6,4},{5,7},{7,5},{8,10},{10,8},{9,1... | collective-permute-start | bytes 1572872 | tf_op jit(solution)/shard_map/ppermute | solution.py:438
  6.3 18.0 %all-to-all-start = ((bf16[32,32,256]{2,1,0:T(8,128)(2,1)}), bf16[32,32,256]{2,1,0:T(8,128)(2,1)S(1)}, u32[]{:S(2)}, u32[]{:S(2)}) async-start(bf16[32,32,256]{2,1,0:T(8,128)(2,1)} %broadcast_select_fusion), calls=%async_computation | async-start | bytes 1048576 | tf_op jit(solution)/shard_map/all_to_all | solution.py:460
  11.8 0.8 copy-start.9
  12.3 0.8 copy-start.10
  24.3 39.2 %copy-start.1 = (bf16[32,32,256]{2,1,0:T(8,128)(2,1)}, bf16[32,32,256]{2,1,0:T(8,128)(2,1)S(1)}, u32[]{:S(2)}) copy-start(bf16[32,32,256]{2,1,0:T(8,128)(2,1)S(1)} %all-to-all-done) | copy-start | bytes 1572868
  24.3 64.9 %all-to-all-start.1 = ((bf16[16,8,2,32,256]{4,3,2,1,0:T(8,128)(2,1)}), bf16[16,8,2,32,256]{4,3,2,1,0:T(8,128)(2,1)}, u32[]{:S(2)}, u32[]{:S(2)}) async-start(bf16[16,8,2,32,256]{4,3,2,1,0:T(8,128)(2,1)} %get-tuple-element.18), calls=%async_computation.1 | async-start | bytes 8388608 | tf_op jit(solution)/shard_map/all_to_all | solution.py:470
  30.7 16.1 %collective-permute-start.7 = (bf16[8,2,2,32,256]{4,3,2,1,0:T(8,128)(2,1)S(1)}, bf16[8,2,2,32,256]{4,3,2,1,0:T(8,128)(2,1)S(1)}, u32[]{:S(2)}, u32[]{:S(2)}) collective-permute-start(bf16[8,2,2,32,256]{4,3,2,1,0:T(8,128)(2,1)S(1)} %bitcast.24), channel_id=1, source_target_pairs={{0,224},{32,0},{64,32},{96,64},{128,96},{160,128},{192,160},{224,1... | collective-permute-start | bytes 1572872 | tf_op jit(solution)/shard_map/ppermute | solution.py:442
  36.4 14.0 %collective-permute-start.3 = (bf16[8,2,2,32,256]{4,3,2,1,0:T(8,128)(2,1)S(1)}, bf16[8,2,2,32,256]{4,3,2,1,0:T(8,128)(2,1)S(1)}, u32[]{:S(2)}, u32[]{:S(2)}) collective-permute-start(bf16[8,2,2,32,256]{4,3,2,1,0:T(8,128)(2,1)S(1)} %bitcast.25), channel_id=1, source_target_pairs={{0,32},{32,64},{64,96},{96,128},{128,160},{160,192},{192,224},{224... | collective-permute-start | bytes 1572872 | tf_op jit(solution)/shard_map/ppermute | solution.py:442
  46.8 42.4 %copy-start.5 = (bf16[8,2,2,32,256]{4,3,2,1,0:T(8,128)(2,1)}, bf16[8,2,2,32,256]{4,3,2,1,0:T(8,128)(2,1)S(1)}, u32[]{:S(2)}) copy-start(bf16[8,2,2,32,256]{4,3,2,1,0:T(8,128)(2,1)S(1)} %collective-permute-done.7.refs_8_) | copy-start | bytes 1572868
  46.8 13.1 %collective-permute-start.8 = (bf16[8,2,2,32,256]{4,3,2,1,0:T(8,128)(2,1)S(1)}, bf16[8,2,2,32,256]{4,3,2,1,0:T(8,128)(2,1)S(1)}, u32[]{:S(2)}, u32[]{:S(2)}) collective-permute-start(bf16[8,2,2,32,256]{4,3,2,1,0:T(8,128)(2,1)S(1)} %collective-permute-done.7.refs_8_), channel_id=1, source_target_pairs={{0,224},{32,0},{64,32},{96,64},{128,96},{160,128},{192,160},{224,1... | collective-permute-start | bytes 1572872 | tf_op jit(solution)/shard_map/ppermute | solution.py:442
  50.3 38.9 %copy-start.6 = (bf16[8,2,2,32,256]{4,3,2,1,0:T(8,128)(2,1)}, bf16[8,2,2,32,256]{4,3,2,1,0:T(8,128)(2,1)S(1)}, u32[]{:S(2)}) copy-start(bf16[8,2,2,32,256]{4,3,2,1,0:T(8,128)(2,1)S(1)} %collective-permute-done.3.refs_1_) | copy-start | bytes 1572868
  50.3 13.1 %collective-permute-start.4 = (bf16[8,2,2,32,256]{4,3,2,1,0:T(8,128)(2,1)S(1)}, bf16[8,2,2,32,256]{4,3,2,1,0:T(8,128)(2,1)S(1)}, u32[]{:S(2)}, u32[]{:S(2)}) collective-permute-start(bf16[8,2,2,32,256]{4,3,2,1,0:T(8,128)(2,1)S(1)} %collective-permute-done.3.refs_1_), channel_id=1, source_target_pairs={{0,32},{32,64},{64,96},{96,128},{128,160},{160,192},{192,224},{224... | collective-permute-start | bytes 1572872 | tf_op jit(solution)/shard_map/ppermute | solution.py:442
  60.0 29.3 %copy-start.7 = (bf16[8,2,2,32,256]{4,3,2,1,0:T(8,128)(2,1)}, bf16[8,2,2,32,256]{4,3,2,1,0:T(8,128)(2,1)S(1)}, u32[]{:S(2)}) copy-start(bf16[8,2,2,32,256]{4,3,2,1,0:T(8,128)(2,1)S(1)} %collective-permute-done.8.refs_7_) | copy-start | bytes 1572868
  60.0 12.3 %collective-permute-start.9 = (bf16[8,2,2,32,256]{4,3,2,1,0:T(8,128)(2,1)S(1)}, bf16[8,2,2,32,256]{4,3,2,1,0:T(8,128)(2,1)S(1)}, u32[]{:S(2)}, u32[]{:S(2)}) collective-permute-start(bf16[8,2,2,32,256]{4,3,2,1,0:T(8,128)(2,1)S(1)} %collective-permute-done.8.refs_7_), channel_id=1, source_target_pairs={{0,224},{32,0},{64,32},{96,64},{128,96},{160,128},{192,160},{224,1... | collective-permute-start | bytes 1572872 | tf_op jit(solution)/shard_map/ppermute | solution.py:442
  63.5 18.9 %copy-start.8 = (bf16[8,2,2,32,256]{4,3,2,1,0:T(8,128)(2,1)}, bf16[8,2,2,32,256]{4,3,2,1,0:T(8,128)(2,1)S(1)}, u32[]{:S(2)}) copy-start(bf16[8,2,2,32,256]{4,3,2,1,0:T(8,128)(2,1)S(1)} %collective-permute-done.4.refs_2_) | copy-start | bytes 1572868
  63.5 12.2 %collective-permute-start.5 = (bf16[8,2,2,32,256]{4,3,2,1,0:T(8,128)(2,1)S(1)}, bf16[8,2,2,32,256]{4,3,2,1,0:T(8,128)(2,1)S(1)}, u32[]{:S(2)}, u32[]{:S(2)}) collective-permute-start(bf16[8,2,2,32,256]{4,3,2,1,0:T(8,128)(2,1)S(1)} %collective-permute-done.4.refs_2_), channel_id=1, source_target_pairs={{0,32},{32,64},{64,96},{96,128},{128,160},{160,192},{192,224},{224... | collective-permute-start | bytes 1572872 | tf_op jit(solution)/shard_map/ppermute | solution.py:442
  63.5 15.6 %collective-permute-start.11 = (bf16[8,2,2,32,256]{4,3,2,1,0:T(8,128)(2,1)S(1)}, bf16[8,2,2,32,256]{4,3,2,1,0:T(8,128)(2,1)S(1)}, u32[]{:S(2)}, u32[]{:S(2)}) collective-permute-start(bf16[8,2,2,32,256]{4,3,2,1,0:T(8,128)(2,1)S(1)} %bitcast.26), channel_id=1, source_target_pairs={{0,2},{2,0},{1,3},{3,1},{4,6},{6,4},{5,7},{7,5},{8,10},{10,8},{9,1... | collective-permute-start | bytes 1572872 | tf_op jit(solution)/shard_map/ppermute | solution.py:438
  66.3 12.9 %collective-permute-start.12 = (bf16[8,2,2,32,256]{4,3,2,1,0:T(8,128)(2,1)S(1)}, bf16[8,2,2,32,256]{4,3,2,1,0:T(8,128)(2,1)S(1)}, u32[]{:S(2)}, u32[]{:S(2)}) collective-permute-start(bf16[8,2,2,32,256]{4,3,2,1,0:T(8,128)(2,1)S(1)} %collective-permute-done.3.refs_1_), channel_id=1, source_target_pairs={{0,2},{2,0},{1,3},{3,1},{4,6},{6,4},{5,7},{7,5},{8,10},{10,8},{9,1... | collective-permute-start | bytes 1572872 | tf_op jit(solution)/shard_map/ppermute | solution.py:438
  66.4 15.5 %collective-permute-start.19 = (bf16[8,2,2,32,256]{4,3,2,1,0:T(8,128)(2,1)S(1)}, bf16[8,2,2,32,256]{4,3,2,1,0:T(8,128)(2,1)S(1)}, u32[]{:S(2)}, u32[]{:S(2)}) collective-permute-start(bf16[8,2,2,32,256]{4,3,2,1,0:T(8,128)(2,1)S(1)} %collective-permute-done.7.refs_8_), channel_id=1, source_target_pairs={{0,2},{2,0},{1,3},{3,1},{4,6},{6,4},{5,7},{7,5},{8,10},{10,8},{9,1... | collective-permute-start | bytes 1572872 | tf_op jit(solution)/shard_map/ppermute | solution.py:438
  72.3 17.0 %copy-start.3 = (bf16[8,2,2,32,256]{4,3,2,1,0:T(8,128)(2,1)}, bf16[8,2,2,32,256]{4,3,2,1,0:T(8,128)(2,1)S(1)}, u32[]{:S(2)}) copy-start(bf16[8,2,2,32,256]{4,3,2,1,0:T(8,128)(2,1)S(1)} %collective-permute-done.9.refs_6_) | copy-start | bytes 1572868
  72.3 10.1 %collective-permute-start.13 = (bf16[8,2,2,32,256]{4,3,2,1,0:T(8,128)(2,1)S(1)}, bf16[8,2,2,32,256]{4,3,2,1,0:T(8,128)(2,1)S(1)}, u32[]{:S(2)}, u32[]{:S(2)}) collective-permute-start(bf16[8,2,2,32,256]{4,3,2,1,0:T(8,128)(2,1)S(1)} %collective-permute-done.4.refs_2_), channel_id=1, source_target_pairs={{0,2},{2,0},{1,3},{3,1},{4,6},{6,4},{5,7},{7,5},{8,10},{10,8},{9,1... | collective-permute-start | bytes 1572872 | tf_op jit(solution)/shard_map/ppermute | solution.py:438
  75.7 13.6 %copy-start.4 = (bf16[8,2,2,32,256]{4,3,2,1,0:T(8,128)(2,1)}, bf16[8,2,2,32,256]{4,3,2,1,0:T(8,128)(2,1)S(1)}, u32[]{:S(2)}) copy-start(bf16[8,2,2,32,256]{4,3,2,1,0:T(8,128)(2,1)S(1)} %collective-permute-done.5.refs_3_) | copy-start | bytes 1572868
  75.7 23.9 %collective-permute-start.18 = (bf16[8,2,2,32,256]{4,3,2,1,0:T(8,128)(2,1)S(1)}, bf16[8,2,2,32,256]{4,3,2,1,0:T(8,128)(2,1)}, u32[]{:S(2)}, u32[]{:S(2)}) collective-permute-start(bf16[8,2,2,32,256]{4,3,2,1,0:T(8,128)(2,1)S(1)} %collective-permute-done.8.refs_7_), channel_id=1, source_target_pairs={{0,2},{2,0},{1,3},{3,1},{4,6},{6,4},{5,7},{7,5},{8,10},{10,8},{9,1... | collective-permute-start | bytes 1572872 | tf_op jit(solution)/shard_map/ppermute | solution.py:438
  79.1 10.0 %copy-start.12 = (bf16[8,2,2,32,256]{4,3,2,1,0:T(8,128)(2,1)}, bf16[8,2,2,32,256]{4,3,2,1,0:T(8,128)(2,1)S(1)}, u32[]{:S(2)}) copy-start(bf16[8,2,2,32,256]{4,3,2,1,0:T(8,128)(2,1)S(1)} %collective-permute-done.11) | copy-start | bytes 1572868
  79.1 9.2 %collective-permute-start.6 = (bf16[4,2,2,32,256]{4,3,2,1,0:T(8,128)(2,1)S(1)}, bf16[4,2,2,32,256]{4,3,2,1,0:T(8,128)(2,1)S(1)}, u32[]{:S(2)}, u32[]{:S(2)}) collective-permute-start(bf16[4,2,2,32,256]{4,3,2,1,0:T(8,128)(2,1)S(1)} %slice.8), channel_id=1, source_target_pairs={{0,32},{32,64},{64,96},{96,128},{128,160},{160,192},{192,224},{224... | collective-permute-start | bytes 786440 | tf_op jit(solution)/shard_map/ppermute | solution.py:442
  79.2 9.9 %copy-start.13 = (bf16[8,2,2,32,256]{4,3,2,1,0:T(8,128)(2,1)}, bf16[8,2,2,32,256]{4,3,2,1,0:T(8,128)(2,1)S(1)}, u32[]{:S(2)}) copy-start(bf16[8,2,2,32,256]{4,3,2,1,0:T(8,128)(2,1)S(1)} %collective-permute-done.12) | copy-start | bytes 1572868
  79.2 9.9 %collective-permute-start.10 = (bf16[4,2,2,32,256]{4,3,2,1,0:T(8,128)(2,1)S(1)}, bf16[4,2,2,32,256]{4,3,2,1,0:T(8,128)(2,1)}, u32[]{:S(2)}, u32[]{:S(2)}) collective-permute-start(bf16[4,2,2,32,256]{4,3,2,1,0:T(8,128)(2,1)S(1)} %slice.9), channel_id=1, source_target_pairs={{0,224},{32,0},{64,32},{96,64},{128,96},{160,128},{192,160},{224,1... | collective-permute-start | bytes 786440 | tf_op jit(solution)/shard_map/ppermute | solution.py:442
  81.8 7.3 %copy-start.14 = (bf16[8,2,2,32,256]{4,3,2,1,0:T(8,128)(2,1)}, bf16[8,2,2,32,256]{4,3,2,1,0:T(8,128)(2,1)S(1)}, u32[]{:S(2)}) copy-start(bf16[8,2,2,32,256]{4,3,2,1,0:T(8,128)(2,1)S(1)} %collective-permute-done.19) | copy-start | bytes 1572868
  81.8 17.7 %collective-permute-start.14 = (bf16[8,2,2,32,256]{4,3,2,1,0:T(8,128)(2,1)S(1)}, bf16[8,2,2,32,256]{4,3,2,1,0:T(8,128)(2,1)}, u32[]{:S(2)}, u32[]{:S(2)}) collective-permute-start(bf16[8,2,2,32,256]{4,3,2,1,0:T(8,128)(2,1)S(1)} %collective-permute-done.5.refs_3_), channel_id=1, source_target_pairs={{0,2},{2,0},{1,3},{3,1},{4,6},{6,4},{5,7},{7,5},{8,10},{10,8},{9,1... | collective-permute-start | bytes 1572872 | tf_op jit(solution)/shard_map/ppermute | solution.py:438
  82.4 6.7 %copy-start.15 = (bf16[8,2,2,32,256]{4,3,2,1,0:T(8,128)(2,1)}, bf16[8,2,2,32,256]{4,3,2,1,0:T(8,128)(2,1)S(1)}, u32[]{:S(2)}) copy-start(bf16[8,2,2,32,256]{4,3,2,1,0:T(8,128)(2,1)S(1)} %collective-permute-done.13) | copy-start | bytes 1572868
  82.4 17.2 %collective-permute-start.17 = (bf16[8,2,2,32,256]{4,3,2,1,0:T(8,128)(2,1)S(1)}, bf16[8,2,2,32,256]{4,3,2,1,0:T(8,128)(2,1)}, u32[]{:S(2)}, u32[]{:S(2)}) collective-permute-start(bf16[8,2,2,32,256]{4,3,2,1,0:T(8,128)(2,1)S(1)} %collective-permute-done.9.refs_6_), channel_id=1, source_target_pairs={{0,2},{2,0},{1,3},{3,1},{4,6},{6,4},{5,7},{7,5},{8,10},{10,8},{9,1... | collective-permute-start | bytes 1572872 | tf_op jit(solution)/shard_map/ppermute | solution.py:438
  88.3 1.0 copy-start.11
  88.3 11.2 %collective-permute-start.15 = (bf16[4,2,2,32,256]{4,3,2,1,0:T(8,128)(2,1)S(1)}, bf16[4,2,2,32,256]{4,3,2,1,0:T(8,128)(2,1)}, u32[]{:S(2)}, u32[]{:S(2)}) collective-permute-start(bf16[4,2,2,32,256]{4,3,2,1,0:T(8,128)(2,1)S(1)} %collective-permute-done.6.refs_4_), channel_id=1, source_target_pairs={{0,2},{2,0},{1,3},{3,1},{4,6},{6,4},{5,7},{7,5},{8,10},{10,8},{9,1... | collective-permute-start | bytes 786440 | tf_op jit(solution)/shard_map/ppermute | solution.py:438
  89.1 10.4 %collective-permute-start.16 = (bf16[4,2,2,32,256]{4,3,2,1,0:T(8,128)(2,1)}, bf16[4,2,2,32,256]{4,3,2,1,0:T(8,128)(2,1)}, u32[]{:S(2)}, u32[]{:S(2)}) collective-permute-start(bf16[4,2,2,32,256]{4,3,2,1,0:T(8,128)(2,1)} %collective-permute-done.10.refs_5_), channel_id=1, source_target_pairs={{0,2},{2,0},{1,3},{3,1},{4,6},{6,4},{5,7},{7,5},{8,10},{10,8},{9,1... | collective-permute-start | bytes 786440 | tf_op jit(solution)/shard_map/ppermute | solution.py:438
  93.1 21.3 %all-to-all-start.2 = ((bf16[16,48,256]{2,1,0:T(8,128)(2,1)}), bf16[16,48,256]{2,1,0:T(8,128)(2,1)S(1)}, u32[]{:S(2)}, u32[]{:S(2)}) async-start(bf16[16,48,256]{2,1,0:T(8,128)(2,1)} %pack.1), calls=%async_computation.2 | async-start | bytes 786432 | tf_op jit(solution)/shard_map/all_to_all | solution.py:471
  99.6 31.0 %copy-start = (f32[4096]{0:T(1024)S(1)}, f32[4096]{0:T(1024)}, u32[]{:S(2)}) copy-start(f32[4096]{0:T(1024)} %param.7) | copy-start | bytes 49156
  114.4 0.7 copy-start.2

commit v5 on v4

--- a/solution.py
+++ b/solution.py
@@ -90,9 +90,9 @@
         inv_buf[which, part, :] = jnp.broadcast_to(lax.rsqrt(mean + EPS), (rows, 128))
 
 
-def grads_kernel(own_ref, other_ref, gain_ref, keys_own_ref, values_own_ref,
+def grads_kernel(own_ref, other_ref, keys_own_ref, values_own_ref,
                  keys_other_ref, values_other_ref, out_ref, inv_ref,
-                 x_buf, d_buf, inv_buf, gain_buf, out_buf, sems, small_sems, out_sems):
+                 x_buf, d_buf, scaled_buf, inv_buf, out_buf, sems, small_sems, out_sems):
     core_at = lax.axis_index("core")
     large = []
     for which, ref in enumerate((own_ref, other_ref)):
@@ -100,25 +100,27 @@
         large.append(
             copies([(ref.at[part], x_buf.at[which, part]) for part in rows], sems.at[which])
         )
-    small = copies([(gain_ref, gain_buf)], small_sems)
-    small.append(pick(core_at, keys_own_ref, values_own_ref, d_buf.at[0], small_sems.at[1]))
-    small.append(pick(core_at, keys_other_ref, values_other_ref, d_buf.at[1], small_sems.at[2]))
+    small = [
+        pick(core_at, keys_own_ref, values_own_ref, d_buf.at[0], small_sems.at[0]),
+        pick(core_at, keys_other_ref, values_other_ref, d_buf.at[1], small_sems.at[1]),
+    ]
     for which in range(2):
         for copy in large[which]:
             copy.wait()
         inverse_rows(x_buf, which, inv_buf)
-    for copy in small:
-        copy.wait()
-    sent = [pltpu.make_async_copy(inv_buf.at[0], inv_ref, small_sems.at[3])]
+        small[which].wait()
+        scaled_buf[which] = (d_buf[which].astype(F32) * inv_buf[which, :, :1]).astype(BF)
+    sent = [pltpu.make_async_copy(inv_buf.at[0], inv_ref, small_sems.at[2])]
     sent[0].start()
     for part in range(STEPS):
         lanes = slice(part * WIDE, (part + 1) * WIDE)
         total = None
         for which in range(2):
-            normal = x_buf[which, :, lanes].astype(F32) * inv_buf[which, :, :1]
-            hidden = (normal * gain_buf[:, lanes]).astype(BF)
             term = lax.dot_general(
-                hidden, d_buf[which], (((0,), (0,)), ((), ())), preferred_element_type=F32
+                x_buf[which, :, lanes],
+                scaled_buf[which],
+                (((0,), (0,)), ((), ())),
+                preferred_element_type=F32,
             )
             total = term if total is None else total + term
         total = total.astype(BF)
@@ -146,7 +148,7 @@
     shape = (GROUPS * XH, Z, CORE, BLOCK, HALF)
     return pl.pallas_call(
         grads_kernel,
-        in_specs=[ANY] * 7,
+        in_specs=[ANY] * 6,
         out_specs=[ANY] * 2,
         out_shape=[
             jax.ShapeDtypeStruct(shape, BF),
@@ -155,11 +157,11 @@
         scratch_shapes=[
             pltpu.VMEM((2, ROWS, D), BF),
             pltpu.VMEM((2, ROWS, C), BF),
+            pltpu.VMEM((2, ROWS, C), BF),
             pltpu.VMEM((2, ROWS, 128), F32),
-            pltpu.VMEM((1, D), F32),
             pltpu.VMEM(shape, BF),
             pltpu.SemaphoreType.DMA((2, 8)),
-            pltpu.SemaphoreType.DMA((4,)),
+            pltpu.SemaphoreType.DMA((3,)),
             pltpu.SemaphoreType.DMA((STEPS, 4)),
         ],
         compiler_params=params(),
@@ -247,12 +249,12 @@
     )(terms, *blocks)
 
 
-def unpack_kernel(scale, in_ref, rows_ref, key_ref, value_ref, gains_ref):
+def unpack_kernel(scale, in_ref, gain_ref, rows_ref, key_ref, value_ref, gains_ref):
     for which, ref in enumerate((key_ref, value_ref)):
         total = in_ref[which, :BLOCK].astype(F32)
         for z in range(1, Z):
             total = total + in_ref[z * 2 + which, :BLOCK].astype(F32)
-        ref[...] = total * scale
+        ref[...] = total * (gain_ref[...] * scale)
     extra = in_ref[0, BLOCK:].astype(F32)
     for at in range(1, Z * CORE):
         extra = extra + in_ref[at, BLOCK:].astype(F32)
@@ -264,13 +266,13 @@
                 gains_ref[at, line * 2 + piece : line * 2 + piece + 1] = lanes
 
 
-def unpack(scale, received, rows):
+def unpack(scale, received, gain_rows, rows):
     def kernel(*refs):
         unpack_kernel(scale, *refs)
 
     return pl.pallas_call(
         kernel,
-        in_specs=[INNER, ANY],
+        in_specs=[INNER, INNER, ANY],
         out_specs=[INNER] * 3,
         out_shape=[
             jax.ShapeDtypeStruct((BLOCK, HALF), F32),
@@ -280,7 +282,7 @@
         compiler_params=params(),
         cost_estimate=cheap(),
         name="unpack",
-    )(received, rows)
+    )(received, gain_rows, rows)
 
 
 def weight_rows(buf, part):
@@ -408,7 +410,7 @@
     )(*inputs)
 
 
-def finish_kernel(scale, in_ref, gain_ref, out_ref):
+def finish_kernel(scale, in_ref, out_ref):
     sums_of = [in_ref[at * XH] + in_ref[at * XH + 1] for at in range(Y * XL)]
     for z in range(Z):
         line, lanes = z // 2, slice(z % 2 * 64, z % 2 * 64 + 64)
@@ -416,22 +418,22 @@
             first, second = (sums_of[at + i][line : line + 1, lanes] for i in range(2))
             tile = jnp.concatenate([first, second], axis=1) * scale
             span = slice(z * W + at * 64, z * W + at * 64 + 128)
-            out_ref[:, span] = tile / gain_ref[:, span]
-
-
-def finish(scale, gains, gain):
+            out_ref[:, span] = tile
+
+
+def finish(scale, gains):
     def kernel(*refs):
         finish_kernel(scale, *refs)
 
     return pl.pallas_call(
         kernel,
-        in_specs=[INNER] * 2,
+        in_specs=[INNER],
         out_specs=INNER,
         out_shape=jax.ShapeDtypeStruct((1, D), F32),
         compiler_params=params(SMALL),
         cost_estimate=cheap(),
         name="finish",
-    )(gains, gain)
+    )(gains)
 
 
 def swap(a):
@@ -454,6 +456,9 @@
 def shards(tokens, gain, w_key, w_value, d_keys, d_values):
     scale = 1.0 / math.sqrt(ROWS * Z * Y * XL * CORE * XH)
     row_gain = gain.reshape(1, D)
+    block = lax.axis_index(("z", "y", "xl", "core"))
+    gain_rows = lax.dynamic_slice(gain, (block * BLOCK,), (BLOCK,))
+    gain_rows = jnp.broadcast_to(gain_rows[:, None], (BLOCK, HALF))
 
     which = lax.broadcasted_iota(jnp.int32, (Y * XL, CORE, XH, BLOCK, HALF), 1)
     sent = jnp.where(which == 0, w_key[None, None, None], w_value[None, None, None])
@@ -461,7 +466,7 @@
         sent.reshape(Y * XL * CORE * XH, BLOCK, HALF), ("y", "xl", "core", "xh"), 0, 0, tiled=True
     )
 
-    inputs = (tokens, swap(tokens), row_gain, d_keys, d_values, swap(d_keys), swap(d_values))
+    inputs = (tokens, swap(tokens), d_keys, d_values, swap(d_keys), swap(d_values))
     terms, inv = gradient_terms(*inputs)
     plane = plane.reshape(GROUPS, CORE, XH, BLOCK, HALF)
     mine = around(plane)
@@ -472,9 +477,9 @@
 
     flat = [block.reshape(-1, XH, BLOCK, HALF) for block in mine + theirs]
     keys, values, d_tokens = rows_pass(tokens, row_gain, inv, d_keys, d_values, *flat)
-    grad_key, grad_value, gains = unpack(scale, received, keys)
+    grad_key, grad_value, gains = unpack(scale, received, gain_rows, keys)
     gains = lax.all_to_all(gains, PLANE, 0, 0, tiled=True)
-    grad_gain = finish(scale, gains, row_gain).reshape(D)
+    grad_gain = finish(scale, gains).reshape(D)
     return (keys, values, d_tokens, grad_key, grad_value, grad_gain)
 
 

time: 132 us -> 132 us (level)
  starting transfers between devices: 49.1 us -> 45.2 us
  waiting for transfers between devices: 32.1 us -> 35.6 us
    ppermute x12, starting transfers between devices: 15.4 us -> 11.9 us  [swap(): return lax.ppermute(a, 'core', [(0, 1), (1, 0)])]
    ppermute x8, waiting for transfers between devices: 31.3 us -> 34.8 us  [along_z(): return lax.ppermute(a, 'z', [(i, (i + step) % Z) for i in range(Z)])]
    ppermute x8, starting transfers between devices: 15.4 us -> 14 us  [along_z(): return lax.ppermute(a, 'z', [(i, (i + step) % Z) for i in range(Z)])]
  transfers between devices with their start and end apart: 23 -> 23, of which waited for: 6 -> 6; matrix products, arithmetic and copies ran while one was open for 1% -> 2% of each run, Pallas kernels for 23% -> 22%
where the time goes in v5:
time: 132 us; the launch traced here: 131 us
  starting transfers between devices  45.2 us (34%)
  waiting for transfers between devices  35.6 us (27%)
  Pallas kernels  31.4 us (24%)
  blocking collectives  14.1 us (11%)
  local copies, waits for them, and re-layouts  2.31 us (2%)
  other arithmetic  1.65 us (1%)
    ppermute x8, waiting for transfers between devices, along_z(): return lax.ppermute(a, 'z', [(i, (i + step) % Z) for i in range(Z)])  34.8 us
    pallas_call x1, Pallas kernels, rows_pass(): pl.pallas_call(rows_kernel, in_specs=[ANY] * (5 + 2 * len(RING)), out_spe...  14.8 us
    all_to_all x1, blocking collectives, shards(): gains = lax.all_to_all(gains, PLANE, 0, 0, tiled=True)  14.1 us
    ppermute x8, starting transfers between devices, along_z(): return lax.ppermute(a, 'z', [(i, (i + step) % Z) for i in range(Z)])  14 us
    ppermute x12, starting transfers between devices, swap(): return lax.ppermute(a, 'core', [(0, 1), (1, 0)])  11.9 us
    pallas_call x1, Pallas kernels, gradient_terms(): pl.pallas_call(grads_kernel, in_specs=[ANY] * 6, out_specs=[ANY] * 2, out...  10.4 us
    all_to_all x1, starting transfers between devices, shards(): received = lax.all_to_all(sent, ('z', 'core'), 0, 0, tiled=True)  7.44 us
    all_to_all x1, starting transfers between devices, shards(): sent = pack(lax.all_to_all(terms, PLANE, 0, 0, tiled=True), mine)  6.39 us
  transfers between devices with their start and end apart: 23, of which 6 were waited for; matrix products, arithmetic and copies ran while one was open for 2% of the time, Pallas kernels for 22%

profile of v5, /device:TPU:1, one launch (start us, length us, event | category | flops | bytes accessed | tf_op | source)
XLA Modules:
  0.0 131.1 jit_solution(5482642309825803899)
XLA Ops:
  0.6 3.3 %collective-permute-start = (bf16[512,4096]{1,0:T(8,128)(2,1)}, bf16[512,4096]{1,0:T(8,128)(2,1)}, u32[]{:S(2)}, u32[]{:S(2)}) collective-permute-start(bf16[512,4096]{1,0:T(8,128)(2,1)} %x_ref.1), channel_id=1, source_target_pairs={{0,2},{2,0},{1,3},{3,1},{4,6},{6,4},{5,7},{7,5},{8,10},{10,8},{9,1... | collective-permute-start | bytes 12582920 | tf_op jit(solution)/shard_map/ppermute | solution.py:440
  4.0 0.1 collective-permute-start.1
  4.1 0.4 collective-permute-start.2
  4.5 0.1 iota.11
  4.6 0.1 iota.12
  4.7 1.6 %broadcast_select_fusion = bf16[32,32,256]{2,1,0:T(8,128)(2,1)} fusion(pred[32]{0:T(512)(128)(4,1)S(1)} %iota.12, bf16[32,256]{1,0:T(8,128)(2,1)} %param.9, bf16[32,256]{1,0:T(8,128)(2,1)} %param.8), kind=kLoop, calls=%fused_computation | loop fusion | flops 262144 | bytes 557088 | tf_op jit(solution)/shard_map/jit(_where)/select_n | solution.py:464
  6.3 5.5 %all-to-all-start = ((bf16[32,32,256]{2,1,0:T(8,128)(2,1)}), bf16[32,32,256]{2,1,0:T(8,128)(2,1)S(1)}, u32[]{:S(2)}, u32[]{:S(2)}) async-start(bf16[32,32,256]{2,1,0:T(8,128)(2,1)} %broadcast_select_fusion), calls=%async_computation | async-start | bytes 1048576 | tf_op jit(solution)/shard_map/all_to_all | solution.py:465
  11.8 0.0 collective-permute-done.1.keys_other_ref
  11.8 0.0 copy-start.7
  11.8 0.5 collective-permute-done.2.values_other_ref
  12.3 0.3 collective-permute-done.other_ref
  12.6 0.0 copy-done.7
  12.6 0.5 copy-done.8
  13.1 10.4 %gradient_terms.1 = (bf16[16,8,2,32,256]{4,3,2,1,0:T(8,128)(2,1)}, f32[512,128]{1,0:T(8,128)}) custom-call(bf16[512,4096]{1,0:T(8,128)(2,1)} %x_ref.1, bf16[512,4096]{1,0:T(8,128)(2,1)} %collective-permute-done.other_ref, bf16[512,512]{1,0:T(8,128)(2,1)} %keys_ref.1, bf16[512,512]{1,0:T(8,128)(2,1)} %values_ref.1, bf16[512,512]{1,0:T(8,128)(2,1)} %copy-done.7, ...), custom_call_target="tpu_custom_call" | custom-call | flops 1048576 | bytes 1048576 | tf_op jit(solution)/shard_map/gradient_terms/pallas_call | solution.py:149
  23.6 0.0 all-to-all-done
  23.6 0.0 copy-start
  23.6 6.4 %all-to-all-start.1 = ((bf16[16,8,2,32,256]{4,3,2,1,0:T(8,128)(2,1)}), bf16[16,8,2,32,256]{4,3,2,1,0:T(8,128)(2,1)}, u32[]{:S(2)}, u32[]{:S(2)}) async-start(bf16[16,8,2,32,256]{4,3,2,1,0:T(8,128)(2,1)} %get-tuple-element.18), calls=%async_computation.1 | async-start | bytes 8388608 | tf_op jit(solution)/shard_map/all_to_all | solution.py:475
  30.0 1.7 %collective-permute-start.3 = (bf16[8,2,2,32,256]{4,3,2,1,0:T(8,128)(2,1)S(1)}, bf16[8,2,2,32,256]{4,3,2,1,0:T(8,128)(2,1)S(1)}, u32[]{:S(2)}, u32[]{:S(2)}) collective-permute-start(bf16[8,2,2,32,256]{4,3,2,1,0:T(8,128)(2,1)S(1)} %bitcast.21), channel_id=1, source_target_pairs={{0,32},{32,64},{64,96},{96,128},{128,160},{160,192},{192,224},{224... | collective-permute-start | bytes 1572872 | tf_op jit(solution)/shard_map/ppermute | solution.py:444
  31.7 4.0 %collective-permute-start.7 = (bf16[8,2,2,32,256]{4,3,2,1,0:T(8,128)(2,1)S(1)}, bf16[8,2,2,32,256]{4,3,2,1,0:T(8,128)(2,1)S(1)}, u32[]{:S(2)}, u32[]{:S(2)}) collective-permute-start(bf16[8,2,2,32,256]{4,3,2,1,0:T(8,128)(2,1)S(1)} %bitcast.22), channel_id=1, source_target_pairs={{0,224},{32,0},{64,32},{96,64},{128,96},{160,128},{192,160},{224,1... | collective-permute-start | bytes 1572872 | tf_op jit(solution)/shard_map/ppermute | solution.py:444
  35.7 11.7 %collective-permute-done.3.refs_1_ = bf16[8,2,2,32,256]{4,3,2,1,0:T(8,128)(2,1)S(1)} collective-permute-done((bf16[8,2,2,32,256]{4,3,2,1,0:T(8,128)(2,1)S(1)}, bf16[8,2,2,32,256]{4,3,2,1,0:T(8,128)(2,1)S(1)}, u32[]{:S(2)}, u32[]{:S(2)}) %collective-permute-start.3) | collective-permute-done | bytes 524320 | tf_op jit(solution)/shard_map/ppermute | solution.py:444
  47.4 0.0 collective-permute-start.4
  47.4 0.0 collective-permute-done.7.refs_8_
  47.4 2.7 %collective-permute-start.8 = (bf16[8,2,2,32,256]{4,3,2,1,0:T(8,128)(2,1)S(1)}, bf16[8,2,2,32,256]{4,3,2,1,0:T(8,128)(2,1)}, u32[]{:S(2)}, u32[]{:S(2)}) collective-permute-start(bf16[8,2,2,32,256]{4,3,2,1,0:T(8,128)(2,1)S(1)} %collective-permute-done.7.refs_8_), channel_id=1, source_target_pairs={{0,224},{32,0},{64,32},{96,64},{128,96},{160,128},{192,160},{224,1... | collective-permute-start | bytes 1572872 | tf_op jit(solution)/shard_map/ppermute | solution.py:444
  50.1 11.0 %collective-permute-done.4.refs_2_ = bf16[8,2,2,32,256]{4,3,2,1,0:T(8,128)(2,1)S(1)} collective-permute-done((bf16[8,2,2,32,256]{4,3,2,1,0:T(8,128)(2,1)S(1)}, bf16[8,2,2,32,256]{4,3,2,1,0:T(8,128)(2,1)S(1)}, u32[]{:S(2)}, u32[]{:S(2)}) %collective-permute-start.4) | collective-permute-done | bytes 524320 | tf_op jit(solution)/shard_map/ppermute | solution.py:444
  61.1 0.0 collective-permute-start.5
  61.1 0.0 collective-permute-done.8.refs_7_
  61.1 2.7 %collective-permute-start.9 = (bf16[8,2,2,32,256]{4,3,2,1,0:T(8,128)(2,1)}, bf16[8,2,2,32,256]{4,3,2,1,0:T(8,128)(2,1)S(1)}, u32[]{:S(2)}, u32[]{:S(2)}) collective-permute-start(bf16[8,2,2,32,256]{4,3,2,1,0:T(8,128)(2,1)} %collective-permute-done.8.refs_7_), channel_id=1, source_target_pairs={{0,224},{32,0},{64,32},{96,64},{128,96},{160,128},{192,160},{224,1... | collective-permute-start | bytes 1572872 | tf_op jit(solution)/shard_map/ppermute | solution.py:444
  63.7 0.0 copy-done
  63.8 2.5 %collective-permute-start.11 = (bf16[8,2,2,32,256]{4,3,2,1,0:T(8,128)(2,1)S(1)}, bf16[8,2,2,32,256]{4,3,2,1,0:T(8,128)(2,1)S(1)}, u32[]{:S(2)}, u32[]{:S(2)}) collective-permute-start(bf16[8,2,2,32,256]{4,3,2,1,0:T(8,128)(2,1)S(1)} %bitcast.23), channel_id=1, source_target_pairs={{0,2},{2,0},{1,3},{3,1},{4,6},{6,4},{5,7},{7,5},{8,10},{10,8},{9,1... | collective-permute-start | bytes 1572872 | tf_op jit(solution)/shard_map/ppermute | solution.py:440
  66.2 0.0 collective-permute-start.12
  66.2 0.5 collective-permute-start.19
  66.7 7.2 %collective-permute-done.5.refs_3_ = bf16[8,2,2,32,256]{4,3,2,1,0:T(8,128)(2,1)S(1)} collective-permute-done((bf16[8,2,2,32,256]{4,3,2,1,0:T(8,128)(2,1)S(1)}, bf16[8,2,2,32,256]{4,3,2,1,0:T(8,128)(2,1)S(1)}, u32[]{:S(2)}, u32[]{:S(2)}) %collective-permute-start.5) | collective-permute-done | bytes 524320 | tf_op jit(solution)/shard_map/ppermute | solution.py:444
  73.9 2.7 %collective-permute-start.13 = (bf16[8,2,2,32,256]{4,3,2,1,0:T(8,128)(2,1)S(1)}, bf16[8,2,2,32,256]{4,3,2,1,0:T(8,128)(2,1)S(1)}, u32[]{:S(2)}, u32[]{:S(2)}) collective-permute-start(bf16[8,2,2,32,256]{4,3,2,1,0:T(8,128)(2,1)S(1)} %collective-permute-done.4.refs_2_), channel_id=1, source_target_pairs={{0,2},{2,0},{1,3},{3,1},{4,6},{6,4},{5,7},{7,5},{8,10},{10,8},{9,1... | collective-permute-start | bytes 1572872 | tf_op jit(solution)/shard_map/ppermute | solution.py:440
  76.6 0.0 collective-permute-done.9.refs_6_
  76.7 0.0 copy-start.3
  76.7 0.1 collective-permute-start.18
  76.8 0.0 collective-permute-done.11
  76.8 0.1 collective-permute-start.6
  76.9 0.0 collective-permute-done.12
  76.9 2.8 %collective-permute-start.10 = (bf16[4,2,2,32,256]{4,3,2,1,0:T(8,128)(2,1)S(1)}, bf16[4,2,2,32,256]{4,3,2,1,0:T(8,128)(2,1)}, u32[]{:S(2)}, u32[]{:S(2)}) collective-permute-start(bf16[4,2,2,32,256]{4,3,2,1,0:T(8,128)(2,1)S(1)} %slice.9), channel_id=1, source_target_pairs={{0,224},{32,0},{64,32},{96,64},{128,96},{160,128},{192,160},{224,1... | collective-permute-start | bytes 786440 | tf_op jit(solution)/shard_map/ppermute | solution.py:444
  79.7 0.0 collective-permute-done.19
  79.7 0.9 collective-permute-start.14
  80.6 0.0 collective-permute-done.13
  80.6 0.1 collective-permute-start.17
  80.7 5.0 %collective-permute-done.6.refs_4_ = bf16[4,2,2,32,256]{4,3,2,1,0:T(8,128)(2,1)S(1)} collective-permute-done((bf16[4,2,2,32,256]{4,3,2,1,0:T(8,128)(2,1)S(1)}, bf16[4,2,2,32,256]{4,3,2,1,0:T(8,128)(2,1)S(1)}, u32[]{:S(2)}, u32[]{:S(2)}) %collective-permute-start.6) | collective-permute-done | bytes 262176 | tf_op jit(solution)/shard_map/ppermute | solution.py:444
  85.7 1.2 collective-permute-start.15
  86.9 0.0 collective-permute-done.10.refs_5_
  86.9 0.1 collective-permute-start.16
  87.0 0.0 copy-done.12
  87.0 0.8 dynamic_slice.3
  87.8 0.0 all-to-all-done.1.in_ref
  87.8 3.8 %pack.1 = bf16[16,48,256]{2,1,0:T(8,128)(2,1)} custom-call(bf16[16,8,2,32,256]{4,3,2,1,0:T(8,128)(2,1)} %all-to-all-done.1.in_ref, bf16[8,2,2,32,256]{4,3,2,1,0:T(8,128)(2,1)} %bitcast.24, bf16[8,2,2,32,256]{4,3,2,1,0:T(8,128)(2,1)} %copy-done.4, bf16[8,2,2,32,256]{4,3,2,1,0:T(8,128)(2,1)} %copy-done.6, bf16[8,2,2,32,256]{4,3,2,1,0:T(8,128)(2,1)} %copy-done.2, ...), custom_call_target="tpu_custom_call" | custom-call | flops 1048576 | bytes 1048576 | tf_op jit(solution)/shard_map/pack/pallas_call | solution.py:234
  91.6 7.4 %all-to-all-start.2 = ((bf16[16,48,256]{2,1,0:T(8,128)(2,1)}), bf16[16,48,256]{2,1,0:T(8,128)(2,1)S(1)}, u32[]{:S(2)}, u32[]{:S(2)}) async-start(bf16[16,48,256]{2,1,0:T(8,128)(2,1)} %pack.1), calls=%async_computation.2 | async-start | bytes 786432 | tf_op jit(solution)/shard_map/all_to_all | solution.py:476
  99.1 0.0 collective-permute-done.18
  99.1 0.0 collective-permute-done.15
  99.1 0.0 collective-permute-done.16
  99.1 0.0 collective-permute-done.14
  99.1 0.0 collective-permute-done.17
  99.1 14.8 %rows_pass.1 = (bf16[512,512]{1,0:T(8,128)(2,1)}, bf16[512,512]{1,0:T(8,128)(2,1)}, bf16[512,4096]{1,0:T(8,128)(2,1)}) custom-call(bf16[512,4096]{1,0:T(8,128)(2,1)} %x_ref.1, f32[1,4096]{1,0:T(1,128)} %bitcast.37, f32[512,128]{1,0:T(8,128)} %get-tuple-element.14.inv_ref, bf16[512,512]{1,0:T(8,128)(2,1)} %keys_ref.1, bf16[512,512]{1,0:T(8,128)(2,1)} %values_ref.1, ...), custom_call_target="tpu_custom_call" | custom-call | flops 8589934592 | bytes 18874368 | tf_op jit(solution)/shard_map/rows_pass/pallas_call | solution.py:383
  113.9 0.0 all-to-all-done.2.refs_0_
  113.9 0.7 broadcast_in_dim.26.refs_1_
  114.7 1.7 %unpack.1 = (f32[32,256]{1,0:T(8,128)}, f32[32,256]{1,0:T(8,128)}, f32[16,4,128]{2,1,0:T(4,128)}) custom-call(bf16[16,48,256]{2,1,0:T(8,128)(2,1)} %copy-done.1, f32[32,256]{1,0:T(8,128)} %broadcast_in_dim.26.refs_1_, bf16[512,512]{1,0:T(8,128)(2,1)} %get-tuple-element.8.refs_2_), custom_call_target="tpu_custom_call" | custom-call | flops 1048576 | bytes 1048576 | tf_op jit(solution)/shard_map/unpack/pallas_call | solution.py:273
  116.3 14.1 %all_to_all.20.refs_0_ = f32[16,4,128]{2,1,0:T(4,128)S(1)} all-to-all(f32[16,4,128]{2,1,0:T(4,128)} %get-tuple-element.21), channel_id=1, replica_groups=mesh['z'=8,'y'=4,'xl'=2,'core'=2,'xh'=2] {'y','xl','xh'}, dimensions={0} | all-to-all | bytes 65536 | tf_op jit(solution)/shard_map/all_to_all | solution.py:481
  130.4 0.7 finish.1
  (24 shorter events, 0.1 us)
Async XLA Ops:
  0.6 12.0 %collective-permute-start = (bf16[512,4096]{1,0:T(8,128)(2,1)}, bf16[512,4096]{1,0:T(8,128)(2,1)}, u32[]{:S(2)}, u32[]{:S(2)}) collective-permute-start(bf16[512,4096]{1,0:T(8,128)(2,1)} %x_ref.1), channel_id=1, source_target_pairs={{0,2},{2,0},{1,3},{3,1},{4,6},{6,4},{5,7},{7,5},{8,10},{10,8},{9,1... | collective-permute-start | bytes 12582920 | tf_op jit(solution)/shard_map/ppermute | solution.py:440
  4.0 7.8 %collective-permute-start.1 = (bf16[512,512]{1,0:T(8,128)(2,1)}, bf16[512,512]{1,0:T(8,128)(2,1)S(1)}, u32[]{:S(2)}, u32[]{:S(2)}) collective-permute-start(bf16[512,512]{1,0:T(8,128)(2,1)} %keys_ref.1), channel_id=1, source_target_pairs={{0,2},{2,0},{1,3},{3,1},{4,6},{6,4},{5,7},{7,5},{8,10},{10,8},{9,1... | collective-permute-start | bytes 1572872 | tf_op jit(solution)/shard_map/ppermute | solution.py:440
  4.1 8.3 %collective-permute-start.2 = (bf16[512,512]{1,0:T(8,128)(2,1)}, bf16[512,512]{1,0:T(8,128)(2,1)S(1)}, u32[]{:S(2)}, u32[]{:S(2)}) collective-permute-start(bf16[512,512]{1,0:T(8,128)(2,1)} %values_ref.1), channel_id=1, source_target_pairs={{0,2},{2,0},{1,3},{3,1},{4,6},{6,4},{5,7},{7,5},{8,10},{10,8},{9,1... | collective-permute-start | bytes 1572872 | tf_op jit(solution)/shard_map/ppermute | solution.py:440
  6.3 17.3 %all-to-all-start = ((bf16[32,32,256]{2,1,0:T(8,128)(2,1)}), bf16[32,32,256]{2,1,0:T(8,128)(2,1)S(1)}, u32[]{:S(2)}, u32[]{:S(2)}) async-start(bf16[32,32,256]{2,1,0:T(8,128)(2,1)} %broadcast_select_fusion), calls=%async_computation | async-start | bytes 1048576 | tf_op jit(solution)/shard_map/all_to_all | solution.py:465
  11.8 0.8 copy-start.7
  12.3 0.8 copy-start.8
  23.6 40.2 %copy-start = (bf16[32,32,256]{2,1,0:T(8,128)(2,1)}, bf16[32,32,256]{2,1,0:T(8,128)(2,1)S(1)}, u32[]{:S(2)}) copy-start(bf16[32,32,256]{2,1,0:T(8,128)(2,1)S(1)} %all-to-all-done) | copy-start | bytes 1572868
  23.6 64.2 %all-to-all-start.1 = ((bf16[16,8,2,32,256]{4,3,2,1,0:T(8,128)(2,1)}), bf16[16,8,2,32,256]{4,3,2,1,0:T(8,128)(2,1)}, u32[]{:S(2)}, u32[]{:S(2)}) async-start(bf16[16,8,2,32,256]{4,3,2,1,0:T(8,128)(2,1)} %get-tuple-element.18), calls=%async_computation.1 | async-start | bytes 8388608 | tf_op jit(solution)/shard_map/all_to_all | solution.py:475
  30.0 17.4 %collective-permute-start.3 = (bf16[8,2,2,32,256]{4,3,2,1,0:T(8,128)(2,1)S(1)}, bf16[8,2,2,32,256]{4,3,2,1,0:T(8,128)(2,1)S(1)}, u32[]{:S(2)}, u32[]{:S(2)}) collective-permute-start(bf16[8,2,2,32,256]{4,3,2,1,0:T(8,128)(2,1)S(1)} %bitcast.21), channel_id=1, source_target_pairs={{0,32},{32,64},{64,96},{96,128},{128,160},{160,192},{192,224},{224... | collective-permute-start | bytes 1572872 | tf_op jit(solution)/shard_map/ppermute | solution.py:444
  31.7 15.7 %collective-permute-start.7 = (bf16[8,2,2,32,256]{4,3,2,1,0:T(8,128)(2,1)S(1)}, bf16[8,2,2,32,256]{4,3,2,1,0:T(8,128)(2,1)S(1)}, u32[]{:S(2)}, u32[]{:S(2)}) collective-permute-start(bf16[8,2,2,32,256]{4,3,2,1,0:T(8,128)(2,1)S(1)} %bitcast.22), channel_id=1, source_target_pairs={{0,224},{32,0},{64,32},{96,64},{128,96},{160,128},{192,160},{224,1... | collective-permute-start | bytes 1572872 | tf_op jit(solution)/shard_map/ppermute | solution.py:444
  47.4 40.4 %copy-start.4 = (bf16[8,2,2,32,256]{4,3,2,1,0:T(8,128)(2,1)}, bf16[8,2,2,32,256]{4,3,2,1,0:T(8,128)(2,1)S(1)}, u32[]{:S(2)}) copy-start(bf16[8,2,2,32,256]{4,3,2,1,0:T(8,128)(2,1)S(1)} %collective-permute-done.3.refs_1_) | copy-start | bytes 1572868
  47.4 13.6 %collective-permute-start.4 = (bf16[8,2,2,32,256]{4,3,2,1,0:T(8,128)(2,1)S(1)}, bf16[8,2,2,32,256]{4,3,2,1,0:T(8,128)(2,1)S(1)}, u32[]{:S(2)}, u32[]{:S(2)}) collective-permute-start(bf16[8,2,2,32,256]{4,3,2,1,0:T(8,128)(2,1)S(1)} %collective-permute-done.3.refs_1_), channel_id=1, source_target_pairs={{0,32},{32,64},{64,96},{96,128},{128,160},{160,192},{192,224},{224... | collective-permute-start | bytes 1572872 | tf_op jit(solution)/shard_map/ppermute | solution.py:444
  47.4 40.4 %copy-start.5 = (bf16[8,2,2,32,256]{4,3,2,1,0:T(8,128)(2,1)}, bf16[8,2,2,32,256]{4,3,2,1,0:T(8,128)(2,1)S(1)}, u32[]{:S(2)}) copy-start(bf16[8,2,2,32,256]{4,3,2,1,0:T(8,128)(2,1)S(1)} %collective-permute-done.7.refs_8_) | copy-start | bytes 1572868
  47.4 13.6 %collective-permute-start.8 = (bf16[8,2,2,32,256]{4,3,2,1,0:T(8,128)(2,1)S(1)}, bf16[8,2,2,32,256]{4,3,2,1,0:T(8,128)(2,1)}, u32[]{:S(2)}, u32[]{:S(2)}) collective-permute-start(bf16[8,2,2,32,256]{4,3,2,1,0:T(8,128)(2,1)S(1)} %collective-permute-done.7.refs_8_), channel_id=1, source_target_pairs={{0,224},{32,0},{64,32},{96,64},{128,96},{160,128},{192,160},{224,1... | collective-permute-start | bytes 1572872 | tf_op jit(solution)/shard_map/ppermute | solution.py:444
  61.1 26.7 %copy-start.6 = (bf16[8,2,2,32,256]{4,3,2,1,0:T(8,128)(2,1)}, bf16[8,2,2,32,256]{4,3,2,1,0:T(8,128)(2,1)S(1)}, u32[]{:S(2)}) copy-start(bf16[8,2,2,32,256]{4,3,2,1,0:T(8,128)(2,1)S(1)} %collective-permute-done.4.refs_2_) | copy-start | bytes 1572868
  61.1 12.8 %collective-permute-start.5 = (bf16[8,2,2,32,256]{4,3,2,1,0:T(8,128)(2,1)S(1)}, bf16[8,2,2,32,256]{4,3,2,1,0:T(8,128)(2,1)S(1)}, u32[]{:S(2)}, u32[]{:S(2)}) collective-permute-start(bf16[8,2,2,32,256]{4,3,2,1,0:T(8,128)(2,1)S(1)} %collective-permute-done.4.refs_2_), channel_id=1, source_target_pairs={{0,32},{32,64},{64,96},{96,128},{128,160},{160,192},{192,224},{224... | collective-permute-start | bytes 1572872 | tf_op jit(solution)/shard_map/ppermute | solution.py:444
  61.1 15.6 %collective-permute-start.9 = (bf16[8,2,2,32,256]{4,3,2,1,0:T(8,128)(2,1)}, bf16[8,2,2,32,256]{4,3,2,1,0:T(8,128)(2,1)S(1)}, u32[]{:S(2)}, u32[]{:S(2)}) collective-permute-start(bf16[8,2,2,32,256]{4,3,2,1,0:T(8,128)(2,1)} %collective-permute-done.8.refs_7_), channel_id=1, source_target_pairs={{0,224},{32,0},{64,32},{96,64},{128,96},{160,128},{192,160},{224,1... | collective-permute-start | bytes 1572872 | tf_op jit(solution)/shard_map/ppermute | solution.py:444
  63.8 13.0 %collective-permute-start.11 = (bf16[8,2,2,32,256]{4,3,2,1,0:T(8,128)(2,1)S(1)}, bf16[8,2,2,32,256]{4,3,2,1,0:T(8,128)(2,1)S(1)}, u32[]{:S(2)}, u32[]{:S(2)}) collective-permute-start(bf16[8,2,2,32,256]{4,3,2,1,0:T(8,128)(2,1)S(1)} %bitcast.23), channel_id=1, source_target_pairs={{0,2},{2,0},{1,3},{3,1},{4,6},{6,4},{5,7},{7,5},{8,10},{10,8},{9,1... | collective-permute-start | bytes 1572872 | tf_op jit(solution)/shard_map/ppermute | solution.py:440
  66.2 10.7 %collective-permute-start.12 = (bf16[8,2,2,32,256]{4,3,2,1,0:T(8,128)(2,1)S(1)}, bf16[8,2,2,32,256]{4,3,2,1,0:T(8,128)(2,1)S(1)}, u32[]{:S(2)}, u32[]{:S(2)}) collective-permute-start(bf16[8,2,2,32,256]{4,3,2,1,0:T(8,128)(2,1)S(1)} %collective-permute-done.3.refs_1_), channel_id=1, source_target_pairs={{0,2},{2,0},{1,3},{3,1},{4,6},{6,4},{5,7},{7,5},{8,10},{10,8},{9,1... | collective-permute-start | bytes 1572872 | tf_op jit(solution)/shard_map/ppermute | solution.py:440
  66.2 13.5 %collective-permute-start.19 = (bf16[8,2,2,32,256]{4,3,2,1,0:T(8,128)(2,1)S(1)}, bf16[8,2,2,32,256]{4,3,2,1,0:T(8,128)(2,1)S(1)}, u32[]{:S(2)}, u32[]{:S(2)}) collective-permute-start(bf16[8,2,2,32,256]{4,3,2,1,0:T(8,128)(2,1)S(1)} %collective-permute-done.7.refs_8_), channel_id=1, source_target_pairs={{0,2},{2,0},{1,3},{3,1},{4,6},{6,4},{5,7},{7,5},{8,10},{10,8},{9,1... | collective-permute-start | bytes 1572872 | tf_op jit(solution)/shard_map/ppermute | solution.py:440
  73.9 13.9 %copy-start.2 = (bf16[8,2,2,32,256]{4,3,2,1,0:T(8,128)(2,1)}, bf16[8,2,2,32,256]{4,3,2,1,0:T(8,128)(2,1)S(1)}, u32[]{:S(2)}) copy-start(bf16[8,2,2,32,256]{4,3,2,1,0:T(8,128)(2,1)S(1)} %collective-permute-done.5.refs_3_) | copy-start | bytes 1572868
  73.9 6.7 %collective-permute-start.13 = (bf16[8,2,2,32,256]{4,3,2,1,0:T(8,128)(2,1)S(1)}, bf16[8,2,2,32,256]{4,3,2,1,0:T(8,128)(2,1)S(1)}, u32[]{:S(2)}, u32[]{:S(2)}) collective-permute-start(bf16[8,2,2,32,256]{4,3,2,1,0:T(8,128)(2,1)S(1)} %collective-permute-done.4.refs_2_), channel_id=1, source_target_pairs={{0,2},{2,0},{1,3},{3,1},{4,6},{6,4},{5,7},{7,5},{8,10},{10,8},{9,1... | collective-permute-start | bytes 1572872 | tf_op jit(solution)/shard_map/ppermute | solution.py:440
  76.7 11.1 %copy-start.3 = (bf16[8,2,2,32,256]{4,3,2,1,0:T(8,128)(2,1)}, bf16[8,2,2,32,256]{4,3,2,1,0:T(8,128)(2,1)S(1)}, u32[]{:S(2)}) copy-start(bf16[8,2,2,32,256]{4,3,2,1,0:T(8,128)(2,1)S(1)} %collective-permute-done.9.refs_6_) | copy-start | bytes 1572868
  76.7 22.4 %collective-permute-start.18 = (bf16[8,2,2,32,256]{4,3,2,1,0:T(8,128)(2,1)}, bf16[8,2,2,32,256]{4,3,2,1,0:T(8,128)(2,1)}, u32[]{:S(2)}, u32[]{:S(2)}) collective-permute-start(bf16[8,2,2,32,256]{4,3,2,1,0:T(8,128)(2,1)} %collective-permute-done.8.refs_7_), channel_id=1, source_target_pairs={{0,2},{2,0},{1,3},{3,1},{4,6},{6,4},{5,7},{7,5},{8,10},{10,8},{9,1... | collective-permute-start | bytes 1572872 | tf_op jit(solution)/shard_map/ppermute | solution.py:440
  76.8 10.1 %copy-start.10 = (bf16[8,2,2,32,256]{4,3,2,1,0:T(8,128)(2,1)}, bf16[8,2,2,32,256]{4,3,2,1,0:T(8,128)(2,1)S(1)}, u32[]{:S(2)}) copy-start(bf16[8,2,2,32,256]{4,3,2,1,0:T(8,128)(2,1)S(1)} %collective-permute-done.11) | copy-start | bytes 1572868
  76.8 8.9 %collective-permute-start.6 = (bf16[4,2,2,32,256]{4,3,2,1,0:T(8,128)(2,1)S(1)}, bf16[4,2,2,32,256]{4,3,2,1,0:T(8,128)(2,1)S(1)}, u32[]{:S(2)}, u32[]{:S(2)}) collective-permute-start(bf16[4,2,2,32,256]{4,3,2,1,0:T(8,128)(2,1)S(1)} %slice.8), channel_id=1, source_target_pairs={{0,32},{32,64},{64,96},{96,128},{128,160},{160,192},{192,224},{224... | collective-permute-start | bytes 786440 | tf_op jit(solution)/shard_map/ppermute | solution.py:444
  76.9 10.1 %copy-start.11 = (bf16[8,2,2,32,256]{4,3,2,1,0:T(8,128)(2,1)}, bf16[8,2,2,32,256]{4,3,2,1,0:T(8,128)(2,1)S(1)}, u32[]{:S(2)}) copy-start(bf16[8,2,2,32,256]{4,3,2,1,0:T(8,128)(2,1)S(1)} %collective-permute-done.12) | copy-start | bytes 1572868
  76.9 10.0 %collective-permute-start.10 = (bf16[4,2,2,32,256]{4,3,2,1,0:T(8,128)(2,1)S(1)}, bf16[4,2,2,32,256]{4,3,2,1,0:T(8,128)(2,1)}, u32[]{:S(2)}, u32[]{:S(2)}) collective-permute-start(bf16[4,2,2,32,256]{4,3,2,1,0:T(8,128)(2,1)S(1)} %slice.9), channel_id=1, source_target_pairs={{0,224},{32,0},{64,32},{96,64},{128,96},{160,128},{192,160},{224,1... | collective-permute-start | bytes 786440 | tf_op jit(solution)/shard_map/ppermute | solution.py:444
  79.7 7.3 %copy-start.12 = (bf16[8,2,2,32,256]{4,3,2,1,0:T(8,128)(2,1)}, bf16[8,2,2,32,256]{4,3,2,1,0:T(8,128)(2,1)S(1)}, u32[]{:S(2)}) copy-start(bf16[8,2,2,32,256]{4,3,2,1,0:T(8,128)(2,1)S(1)} %collective-permute-done.19) | copy-start | bytes 1572868
  79.7 19.4 %collective-permute-start.14 = (bf16[8,2,2,32,256]{4,3,2,1,0:T(8,128)(2,1)S(1)}, bf16[8,2,2,32,256]{4,3,2,1,0:T(8,128)(2,1)}, u32[]{:S(2)}, u32[]{:S(2)}) collective-permute-start(bf16[8,2,2,32,256]{4,3,2,1,0:T(8,128)(2,1)S(1)} %collective-permute-done.5.refs_3_), channel_id=1, source_target_pairs={{0,2},{2,0},{1,3},{3,1},{4,6},{6,4},{5,7},{7,5},{8,10},{10,8},{9,1... | collective-permute-start | bytes 1572872 | tf_op jit(solution)/shard_map/ppermute | solution.py:440
  80.6 6.4 %copy-start.13 = (bf16[8,2,2,32,256]{4,3,2,1,0:T(8,128)(2,1)}, bf16[8,2,2,32,256]{4,3,2,1,0:T(8,128)(2,1)S(1)}, u32[]{:S(2)}) copy-start(bf16[8,2,2,32,256]{4,3,2,1,0:T(8,128)(2,1)S(1)} %collective-permute-done.13) | copy-start | bytes 1572868
  80.6 18.5 %collective-permute-start.17 = (bf16[8,2,2,32,256]{4,3,2,1,0:T(8,128)(2,1)S(1)}, bf16[8,2,2,32,256]{4,3,2,1,0:T(8,128)(2,1)}, u32[]{:S(2)}, u32[]{:S(2)}) collective-permute-start(bf16[8,2,2,32,256]{4,3,2,1,0:T(8,128)(2,1)S(1)} %collective-permute-done.9.refs_6_), channel_id=1, source_target_pairs={{0,2},{2,0},{1,3},{3,1},{4,6},{6,4},{5,7},{7,5},{8,10},{10,8},{9,1... | collective-permute-start | bytes 1572872 | tf_op jit(solution)/shard_map/ppermute | solution.py:440
  85.7 2.1 %copy-start.9 = (bf16[4,2,2,32,256]{4,3,2,1,0:T(8,128)(2,1)}, bf16[4,2,2,32,256]{4,3,2,1,0:T(8,128)(2,1)S(1)}, u32[]{:S(2)}) copy-start(bf16[4,2,2,32,256]{4,3,2,1,0:T(8,128)(2,1)S(1)} %collective-permute-done.6.refs_4_) | copy-start | bytes 786436
  85.7 13.3 %collective-permute-start.15 = (bf16[4,2,2,32,256]{4,3,2,1,0:T(8,128)(2,1)S(1)}, bf16[4,2,2,32,256]{4,3,2,1,0:T(8,128)(2,1)}, u32[]{:S(2)}, u32[]{:S(2)}) collective-permute-start(bf16[4,2,2,32,256]{4,3,2,1,0:T(8,128)(2,1)S(1)} %collective-permute-done.6.refs_4_), channel_id=1, source_target_pairs={{0,2},{2,0},{1,3},{3,1},{4,6},{6,4},{5,7},{7,5},{8,10},{10,8},{9,1... | collective-permute-start | bytes 786440 | tf_op jit(solution)/shard_map/ppermute | solution.py:440
  86.9 12.2 %collective-permute-start.16 = (bf16[4,2,2,32,256]{4,3,2,1,0:T(8,128)(2,1)}, bf16[4,2,2,32,256]{4,3,2,1,0:T(8,128)(2,1)}, u32[]{:S(2)}, u32[]{:S(2)}) collective-permute-start(bf16[4,2,2,32,256]{4,3,2,1,0:T(8,128)(2,1)} %collective-permute-done.10.refs_5_), channel_id=1, source_target_pairs={{0,2},{2,0},{1,3},{3,1},{4,6},{6,4},{5,7},{7,5},{8,10},{10,8},{9,1... | collective-permute-start | bytes 786440 | tf_op jit(solution)/shard_map/ppermute | solution.py:440
  91.6 22.3 %all-to-all-start.2 = ((bf16[16,48,256]{2,1,0:T(8,128)(2,1)}), bf16[16,48,256]{2,1,0:T(8,128)(2,1)S(1)}, u32[]{:S(2)}, u32[]{:S(2)}) async-start(bf16[16,48,256]{2,1,0:T(8,128)(2,1)} %pack.1), calls=%async_computation.2 | async-start | bytes 786432 | tf_op jit(solution)/shard_map/all_to_all | solution.py:476
  113.9 0.8 copy-start.1
